TPU v7x, 256 devices: a whole 4x4x8 slice. The times are simulated.
256 devices in a mesh: rows: 64 (over z, x, core), bal: 4 (over y).
Axes of the slice: x: 4, y: 4, z: 8, core: 2. Of those that a mesh axis runs over, the one named last changes fastest.
Arguments:
- embeddings: bfloat16 [131072, 1024], P(('rows', 'bal')), may hold values from -60 to 60
- cluster_blocks: int32 [128], replicated, may hold values from 1 to 4, as said below
Outputs:
- row_max: float32 [131072], P(('rows', 'bal'))
Inputs may be any that keep to these rules, and one draw needn't show every extreme that they name: `cluster_blocks`: the sizes sum to 256; at least one cluster has exactly 4 blocks.
All inputs are finite; a program needn't handle non-finite values.
Results may differ from a plain program's by a relative error of at most 0.00051.
Values may be sent and summed in bfloat16 or wider, within the bound.
No kernel may reach another device: no remote copies, remote signals or barrier semaphores. Data moves between devices by JAX's collectives and lax.ppermute only.
A program may use at most 64 MiB of HBM per device.

v0:
```python
import jax
import jax.numpy as jnp
from jax import lax
from jax.sharding import PartitionSpec as P

MAXB = 4


EPSILON = 1e-06


def passed_along(block, axis, distance):
    devices = range(lax.axis_size(axis))
    route = [(i - distance, i) for i in devices if i - distance in devices]
    return lax.ppermute(block, axis, route)


def unit_rows(block_rows):
    values = block_rows.astype(jnp.float32)
    scaled = values * lax.rsqrt(jnp.sum(values * values, axis=1, keepdims=True) + EPSILON)
    return scaled.astype(jnp.bfloat16)


def joined(bounds, lower, upper):
    crossing = jnp.sum(((bounds > lower) & (bounds <= upper)).astype(jnp.int32))
    return (lower >= 0) & (crossing == 0)


def products_of(normed, partner):
    return lax.dot_general(
        normed, partner, (((1,), (1,)), ((), ())), preferred_element_type=jnp.float32
    )


def tile_maxima(normed, partner, allowed):

    def compute(theirs):
        products = products_of(normed, theirs)
        return (jnp.max(products, axis=1), jnp.max(products, axis=0))

    def nothing(theirs):
        filled = jnp.full((normed.shape[0],), -2.0, jnp.float32)
        return (filled, filled)

    return lax.cond(allowed, compute, nothing, partner)


def shards(embeddings, cluster_blocks):
    normed = unit_rows(embeddings)
    bounds = jnp.cumsum(cluster_blocks)
    my_block = lax.axis_index(("rows", "bal"))
    own_products = products_of(normed, normed)
    diagonal_mask = jnp.arange(normed.shape[0])[:, None] == jnp.arange(normed.shape[0])[None, :]
    highest = jnp.max(jnp.where(diagonal_mask, -2.0, own_products), axis=1)
    for offset in range(1, MAXB):
        earlier_rows = passed_along(normed, ("rows", "bal"), offset)
        row_part, col_part = tile_maxima(
            normed, earlier_rows, joined(bounds, my_block - offset, my_block)
        )
        highest = jnp.maximum(highest, row_part)
        returned = passed_along(col_part, ("rows", "bal"), -offset)
        returned = jnp.where(joined(bounds, my_block, my_block + offset), returned, -2.0)
        highest = jnp.maximum(highest, returned)
    return highest


def solution(mesh):
    in_specs = (P(("rows", "bal"), None), P())
    out_specs = P(("rows", "bal"))
    return jax.shard_map(shards, mesh=mesh, in_specs=in_specs, out_specs=out_specs, check_vma=False)
```

profile of v0, /device:TPU:15, one launch (start us, length us, event | category | flops | bytes accessed | tf_op | source)
XLA Modules:
  0.0 69.8 jit_solution(1589533773072004586)
XLA Ops:
  0.0 1.6 %fusion = f32[512]{0:T(512)S(1)} fusion(bf16[512,1024]{1,0:T(8,128)(2,1)} %param.8), kind=kLoop, calls=%fused_computation.2 | loop fusion | flops 1572352 | bytes 1050624 | tf_op jit(solution)/shard_map/reduce_sum | solution.py:20
  1.6 0.0 copy-done
  1.6 0.0 copy-start.1
  1.6 0.2 fusion.1
  1.9 3.2 %collective-permute-start = (bf16[512,1024]{1,0:T(8,128)(2,1)S(1)}, bf16[512,1024]{1,0:T(8,128)(2,1)}, u32[]{:S(2)}, u32[]{:S(2)}) collective-permute-start(bf16[512,1024]{1,0:T(8,128)(2,1)S(1)} %fusion.1), channel_id=1, source_target_pairs={{0,1},{1,2},{2,3},{3,4},{4,5},{5,6},{6,7},{7,8},{8,9},{9,10},{10,1... | collective-permute-start | bytes 3145736 | tf_op jit(solution)/shard_map/ppermute | solution.py:15
  5.1 4.4 %collective-permute-start.2 = (bf16[512,1024]{1,0:T(8,128)(2,1)S(1)}, bf16[512,1024]{1,0:T(8,128)(2,1)S(1)}, u32[]{:S(2)}, u32[]{:S(2)}) collective-permute-start(bf16[512,1024]{1,0:T(8,128)(2,1)S(1)} %fusion.1), channel_id=1, source_target_pairs={{0,2},{1,3},{2,4},{3,5},{4,6},{5,7},{6,8},{7,9},{8,10},{9,11},{10,... | collective-permute-start | bytes 3145736 | tf_op jit(solution)/shard_map/ppermute | solution.py:15
  9.5 4.6 %collective-permute-start.4 = (bf16[512,1024]{1,0:T(8,128)(2,1)S(1)}, bf16[512,1024]{1,0:T(8,128)(2,1)S(1)}, u32[]{:S(2)}, u32[]{:S(2)}) collective-permute-start(bf16[512,1024]{1,0:T(8,128)(2,1)S(1)} %fusion.1), channel_id=1, source_target_pairs={{0,3},{1,4},{2,5},{3,6},{4,7},{5,8},{6,9},{7,10},{8,11},{9,12},{10... | collective-permute-start | bytes 3145736 | tf_op jit(solution)/shard_map/ppermute | solution.py:15
  14.1 0.0 copy-done.1
  14.1 0.1 copy.3
  14.2 0.2 reduce-window.9
  14.4 0.8 %convert_reduce_fusion.4 = (s32[]{:T(128)}, s32[]{:T(128)}, s32[]{:T(128)}, s32[]{:T(128)}, s32[]{:T(128)}, /*index=5*/s32[]{:T(128)}) fusion(s32[128,1]{1,0:T(8,128)S(1)} %reduce-window.9, s32[]{:T(128)S(6)} %add.29, s32[]{:T(128)S(6)} %add.28, s32[]{:T(128)S(6)} %add.30, s32[]{:T(128)S(6)} %sub.10, s32[]{:T(128)S(6)} %sub.11, s32[]{:T(128)S(6)} %add.31, ...), kind=kLoop, calls=%fused_computation.11 | loop fusion | flops 3322 | bytes 564 | tf_op jit(solution)/shard_map/reduce_sum | solution.py:25
  17.0 10.9 %collective-permute-done = bf16[512,1024]{1,0:T(8,128)(2,1)} collective-permute-done((bf16[512,1024]{1,0:T(8,128)(2,1)S(1)}, bf16[512,1024]{1,0:T(8,128)(2,1)}, u32[]{:S(2)}, u32[]{:S(2)}) %collective-permute-start) | collective-permute-done | bytes 1048608 | tf_op jit(solution)/shard_map/ppermute | solution.py:15
  27.9 2.0 %conditional.3 = (f32[512]{0:T(512)S(1)}, f32[512]{0:T(512)S(1)}) conditional(s32[]{:T(128)} %convert_element_type.42, () %tuple.29, (bf16[512,1024]{1,0:T(8,128)(2,1)S(1)}, bf16[512,1024]{1,0:T(8,128)(2,1)}) %tuple.30), branch_computations={%region_4.5_spmd, %region_5.8_spmd} | conditional | flops 537394176 | bytes 2101264 | solution.py:45
  27.9 2.0 %fusion.3 = (f32[512]{0:T(512)S(1)}, f32[512]{0:T(512)S(1)}) fusion(bf16[512,1024]{1,0:T(8,128)(2,1)S(1)} %get-tuple-element.17, bf16[512,1024]{1,0:T(8,128)(2,1)} %get-tuple-element.18), kind=kOutput, calls=%fused_computation.17 | convolution fusion | flops 537394176 | bytes 2101248 | tf_op jit(solution)/shard_map/cond/branch_1_fun/dot_general | solution.py:30
  29.9 14.3 %collective-permute-start.1 = (f32[512]{0:T(512)S(1)}, f32[512]{0:T(512)S(1)}, u32[]{:S(2)}, u32[]{:S(2)}) collective-permute-start(f32[512]{0:T(512)S(1)} %get-tuple-element.30), channel_id=1, source_target_pairs={{1,0},{2,1},{3,2},{4,3},{5,4},{6,5},{7,6},{8,7},{9,8},{10,9},{11,1... | collective-permute-start | bytes 6152 | tf_op jit(solution)/shard_map/ppermute | solution.py:15
  44.2 0.0 collective-permute-done.2
  44.3 17.0 %collective-permute-start.3 = (f32[512]{0:T(512)S(1)}, f32[512]{0:T(512)S(1)}, u32[]{:S(2)}, u32[]{:S(2)}) collective-permute-start(f32[512]{0:T(512)S(1)} %get-tuple-element.32), channel_id=1, source_target_pairs={{2,0},{3,1},{4,2},{5,3},{6,4},{7,5},{8,6},{9,7},{10,8},{11,9},{12,... | collective-permute-start | bytes 6152 | tf_op jit(solution)/shard_map/ppermute | solution.py:15
  61.3 0.0 collective-permute-done.4
  61.3 1.9 %collective-permute-start.5 = (f32[512]{0:T(512)S(1)}, f32[512]{0:T(512)S(1)}, u32[]{:S(2)}, u32[]{:S(2)}) collective-permute-start(f32[512]{0:T(512)S(1)} %get-tuple-element.34), channel_id=1, source_target_pairs={{3,0},{4,1},{5,2},{6,3},{7,4},{8,5},{9,6},{10,7},{11,8},{12,9},{13... | collective-permute-start | bytes 6152 | tf_op jit(solution)/shard_map/ppermute | solution.py:15
  63.3 0.8 %fusion.2 = f32[512]{0:T(512)S(1)} fusion(bf16[512,1024]{1,0:T(8,128)(2,1)S(1)} %fusion.1), kind=kOutput, calls=%fused_computation.5 | convolution fusion | flops 537656832 | bytes 1050624 | tf_op jit(solution)/shard_map/dot_general | solution.py:30
  65.9 0.0 collective-permute-done.1
  65.9 0.0 collective-permute-done.3
  66.0 3.3 %collective-permute-done.5 = f32[512]{0:T(512)S(1)} collective-permute-done((f32[512]{0:T(512)S(1)}, f32[512]{0:T(512)S(1)}, u32[]{:S(2)}, u32[]{:S(2)}) %collective-permute-start.5) | collective-permute-done | bytes 2080 | tf_op jit(solution)/shard_map/ppermute | solution.py:15
  69.3 0.6 select_maximum_fusion
  (8 shorter events, 0.1 us)
Async XLA Ops:
  0.0 1.6 %copy-start = (bf16[512,1024]{1,0:T(8,128)(2,1)S(1)}, bf16[512,1024]{1,0:T(8,128)(2,1)}, u32[]{:S(2)}) copy-start(bf16[512,1024]{1,0:T(8,128)(2,1)} %param.8) | copy-start | bytes 3145732
  1.6 12.5 %copy-start.1 = (s32[128]{0:T(128)S(1)}, s32[128]{0:T(128)}, u32[]{:S(2)}) copy-start(s32[128]{0:T(128)} %param.9) | copy-start | bytes 1540
  1.9 26.0 %collective-permute-start = (bf16[512,1024]{1,0:T(8,128)(2,1)S(1)}, bf16[512,1024]{1,0:T(8,128)(2,1)}, u32[]{:S(2)}, u32[]{:S(2)}) collective-permute-start(bf16[512,1024]{1,0:T(8,128)(2,1)S(1)} %fusion.1), channel_id=1, source_target_pairs={{0,1},{1,2},{2,3},{3,4},{4,5},{5,6},{6,7},{7,8},{8,9},{9,10},{10,1... | collective-permute-start | bytes 3145736 | tf_op jit(solution)/shard_map/ppermute | solution.py:15
  5.1 39.1 %collective-permute-start.2 = (bf16[512,1024]{1,0:T(8,128)(2,1)S(1)}, bf16[512,1024]{1,0:T(8,128)(2,1)S(1)}, u32[]{:S(2)}, u32[]{:S(2)}) collective-permute-start(bf16[512,1024]{1,0:T(8,128)(2,1)S(1)} %fusion.1), channel_id=1, source_target_pairs={{0,2},{1,3},{2,4},{3,5},{4,6},{5,7},{6,8},{7,9},{8,10},{9,11},{10,... | collective-permute-start | bytes 3145736 | tf_op jit(solution)/shard_map/ppermute | solution.py:15
  9.5 51.8 %collective-permute-start.4 = (bf16[512,1024]{1,0:T(8,128)(2,1)S(1)}, bf16[512,1024]{1,0:T(8,128)(2,1)S(1)}, u32[]{:S(2)}, u32[]{:S(2)}) collective-permute-start(bf16[512,1024]{1,0:T(8,128)(2,1)S(1)} %fusion.1), channel_id=1, source_target_pairs={{0,3},{1,4},{2,5},{3,6},{4,7},{5,8},{6,9},{7,10},{8,11},{9,12},{10... | collective-permute-start | bytes 3145736 | tf_op jit(solution)/shard_map/ppermute | solution.py:15
  29.9 36.0 %collective-permute-start.1 = (f32[512]{0:T(512)S(1)}, f32[512]{0:T(512)S(1)}, u32[]{:S(2)}, u32[]{:S(2)}) collective-permute-start(f32[512]{0:T(512)S(1)} %get-tuple-element.30), channel_id=1, source_target_pairs={{1,0},{2,1},{3,2},{4,3},{5,4},{6,5},{7,6},{8,7},{9,8},{10,9},{11,1... | collective-permute-start | bytes 6152 | tf_op jit(solution)/shard_map/ppermute | solution.py:15
  44.3 21.7 %collective-permute-start.3 = (f32[512]{0:T(512)S(1)}, f32[512]{0:T(512)S(1)}, u32[]{:S(2)}, u32[]{:S(2)}) collective-permute-start(f32[512]{0:T(512)S(1)} %get-tuple-element.32), channel_id=1, source_target_pairs={{2,0},{3,1},{4,2},{5,3},{6,4},{7,5},{8,6},{9,7},{10,8},{11,9},{12,... | collective-permute-start | bytes 6152 | tf_op jit(solution)/shard_map/ppermute | solution.py:15
  61.3 7.9 %collective-permute-start.5 = (f32[512]{0:T(512)S(1)}, f32[512]{0:T(512)S(1)}, u32[]{:S(2)}, u32[]{:S(2)}) collective-permute-start(f32[512]{0:T(512)S(1)} %get-tuple-element.34), channel_id=1, source_target_pairs={{3,0},{4,1},{5,2},{6,3},{7,4},{8,5},{9,6},{10,7},{11,8},{12,9},{13... | collective-permute-start | bytes 6152 | tf_op jit(solution)/shard_map/ppermute | solution.py:15
where the time goes:
time: 70.4 us; the launch traced here: 69.8 us
  starting transfers between devices  45.4 us (64%)
  waiting for transfers between devices  14.2 us (20%)
  between operations  3.91 us (6%)
  other arithmetic  3.36 us (5%)
  matrix products  2.8 us (4%)
    ppermute x6, starting transfers between devices, passed_along(): return lax.ppermute(block, axis, route)  45.4 us
    ppermute x6, waiting for transfers between devices, passed_along(): return lax.ppermute(block, axis, route)  14.2 us
    dot_general x2, matrix products, products_of(): lax.dot_general(normed, partner, (((1,), (1,)), ((), ())), preferred_elem...  2.8 us
    reduce_sum x1, other arithmetic, unit_rows(): jnp.sum(values * values, axis=1, keepdims=True) + EPSILON  1.59 us
  transfers between devices with their start and end apart: 6, of which 2 were waited for; matrix products, arithmetic and copies ran while one was open for 6% of the time, Pallas kernels for 0%

commit v1 on v0

v1 whole, which is shorter than its diff:
```python
import jax
import jax.numpy as jnp
from jax import lax
from jax.experimental import pallas as pl
from jax.experimental.pallas import tpu as pltpu
from jax.sharding import PartitionSpec as P

EPSILON = 1e-06
AXES = ("rows", "bal")
LOWEST = -2.0
STRIP = 64


def shifted(block, distance):
    n = lax.axis_size(AXES)
    return lax.ppermute(block, AXES, [(i, (i + distance) % n) for i in range(n)])


def joined(bounds, lower, distance):
    n = lax.axis_size(AXES)
    lower = lax.rem(lower + n, n)
    upper = lower + distance
    crossing = jnp.sum(((bounds > lower) & (bounds <= upper)).astype(jnp.int32))
    return ((upper < n) & (crossing == 0)).astype(jnp.int32)


def write_units(raw_ref, unit_ref):
    for start in range(0, raw_ref.shape[0], STRIP):
        rows = pl.ds(start, STRIP)
        values = raw_ref[rows, :].astype(jnp.float32)
        scale = lax.rsqrt(jnp.sum(values * values, axis=1, keepdims=True) + EPSILON)
        unit_ref[rows, :] = (values * scale).astype(jnp.bfloat16)


def products_of(left, right):
    return lax.dot_general(
        left, right, (((1,), (1,)), ((), ())), preferred_element_type=jnp.float32
    )


def column_max(products):
    return jnp.max(products, axis=0, keepdims=True)


def row_max(products):
    width = products.shape[1]
    folded = products[:, :128]
    for start in range(128, width, 128):
        folded = jnp.maximum(folded, products[:, start : start + 128])
    return jnp.max(folded.T, axis=0, keepdims=True)


def own_kernel(raw_ref, unit_ref, high_ref):
    write_units(raw_ref, unit_ref)
    products = products_of(unit_ref[...], unit_ref[...])
    row = lax.broadcasted_iota(jnp.int32, products.shape, 0)
    col = lax.broadcasted_iota(jnp.int32, products.shape, 1)
    high_ref[...] = column_max(jnp.where(row == col, LOWEST, products))


def far_kernel(down_ref, up_ref, down_unit_ref, up_unit_ref):
    write_units(down_ref, down_unit_ref)
    write_units(up_ref, up_unit_ref)


def prev_kernel(flags_ref, raw_ref, own_ref, far_ref, high_in_ref, unit_ref, high_ref, back_ref):
    write_units(raw_ref, unit_ref)
    high_ref[...] = high_in_ref[...]
    back_ref[...] = jnp.full_like(back_ref, LOWEST)

    @pl.when(flags_ref[0] == 1)
    def _():
        products = products_of(own_ref[...], unit_ref[...])
        high_ref[...] = jnp.maximum(high_ref[...], row_max(products))
        back_ref[...] = column_max(products)

    @pl.when(flags_ref[2] == 1)
    def _():
        back_ref[...] = jnp.maximum(
            back_ref[...], column_max(products_of(far_ref[...], unit_ref[...]))
        )


def next_kernel(flags_ref, raw_ref, prev_ref, far_ref, back_in_ref, back_ref, ahead_ref, unit_ref):
    back_ref[...] = back_in_ref[...]
    ahead_ref[...] = jnp.full_like(ahead_ref, LOWEST)

    @pl.when(flags_ref[1] + flags_ref[3] > 0)
    def _():
        write_units(raw_ref, unit_ref)

    @pl.when(flags_ref[1] == 1)
    def _():
        products = products_of(prev_ref[...], unit_ref[...])
        back_ref[...] = jnp.maximum(back_ref[...], row_max(products))
        ahead_ref[...] = column_max(products)

    @pl.when(flags_ref[3] == 1)
    def _():
        ahead_ref[...] = jnp.maximum(
            ahead_ref[...], column_max(products_of(far_ref[...], unit_ref[...]))
        )


VMEM = pl.BlockSpec(memory_space=pltpu.VMEM)
SMEM = pl.BlockSpec(memory_space=pltpu.SMEM)
PARAMS = pltpu.CompilerParams(vmem_limit_bytes=40 * 1024 * 1024)


def call(kernel, args, outs, scratch=(), flops=0):
    specs = [SMEM if a.ndim == 1 else VMEM for a in args]
    moved = sum(a.size * a.dtype.itemsize for a in args)
    return pl.pallas_call(
        kernel,
        in_specs=specs,
        out_specs=[VMEM] * len(outs),
        out_shape=[jax.ShapeDtypeStruct(*o) for o in outs],
        scratch_shapes=list(scratch),
        compiler_params=PARAMS,
        cost_estimate=pl.CostEstimate(flops=flops, bytes_accessed=moved, transcendentals=0),
    )(*args)


def shards(embeddings, cluster_blocks):
    block, width = embeddings.shape
    from_prev = shifted(embeddings, 1)
    from_next = shifted(embeddings, -1)
    from_down = shifted(embeddings, 4)
    from_up = shifted(embeddings, -4)

    bounds = jnp.cumsum(cluster_blocks)
    me = lax.axis_index(AXES)
    flags = jnp.stack(
        [
            joined(bounds, me - 1, 1),
            joined(bounds, me - 1, 2),
            joined(bounds, me - 4, 3),
            joined(bounds, me + 1, 3),
        ]
    )
    units = ((block, width), jnp.bfloat16)
    line = ((1, block), jnp.float32)
    tile = 2 * block * block * width

    own, high = call(own_kernel, (embeddings,), [units, line], flops=tile)
    down, up = call(far_kernel, (from_down, from_up), [units, units])
    prev, high, back = call(
        prev_kernel, (flags, from_prev, own, down, high), [units, line, line], flops=2 * tile
    )
    back, ahead = call(
        next_kernel,
        (flags, from_next, prev, up, back),
        [line, line],
        scratch=[pltpu.VMEM(*units)],
        flops=2 * tile,
    )
    returned = jnp.maximum(shifted(back, -1), shifted(ahead, 1))
    return jnp.maximum(high, returned).reshape(block)


def solution(mesh):
    in_specs = (P(AXES, None), P())
    out_specs = P(AXES)
    return jax.shard_map(shards, mesh=mesh, in_specs=in_specs, out_specs=out_specs, check_vma=False)
```

time: 70.4 us -> 47.8 us (0.68)
  the two profiles are of different devices: /device:TPU:15 before, /device:TPU:0 now
where the time goes in v1:
time: 47.8 us; the launch traced here: 47.6 us
  waiting for transfers between devices  20.6 us (43%)
  starting transfers between devices  17 us (36%)
  Pallas kernels  3.78 us (8%)
  between operations  2.63 us (6%)
  local copies, waits for them, and re-layouts  1.99 us (4%)
  other arithmetic  1.58 us (3%)
    ppermute x6, waiting for transfers between devices, shifted(): lax.ppermute(block, AXES, [(i, (i + distance) % n) for i in range(n)])  20.6 us
    ppermute x6, starting transfers between devices, shifted(): lax.ppermute(block, AXES, [(i, (i + distance) % n) for i in range(n)])  17 us
    pallas_call x4, Pallas kernels, call(): pl.pallas_call(kernel, in_specs=specs, out_specs=[VMEM] * len(outs), out_...  3.78 us
    unnamed x4, local copies, waits for them, and re-layouts  1.87 us
  transfers between devices with their start and end apart: 6, of which 3 were waited for; matrix products, arithmetic and copies ran while one was open for 2% of the time, Pallas kernels for 7%

profile of v1, /device:TPU:0, one launch (start us, length us, event | category | flops | bytes accessed | tf_op | source)
XLA Modules:
  0.0 47.6 jit_solution(6981241324505998645)
XLA Ops:
  0.0 0.0 collective-permute-start.1
  0.0 5.8 %collective-permute-start.2 = (bf16[512,1024]{1,0:T(8,128)(2,1)}, bf16[512,1024]{1,0:T(8,128)(2,1)S(1)}, u32[]{:S(2)}, u32[]{:S(2)}) collective-permute-start(bf16[512,1024]{1,0:T(8,128)(2,1)} %raw_ref.1), channel_id=1, source_target_pairs={{0,252},{1,253},{2,254},{3,255},{4,0},{5,1},{6,2},{7,3},{8,4},{9,5... | collective-permute-start | bytes 3145736 | tf_op jit(solution)/shard_map/ppermute | solution.py:16
  5.8 1.6 %collective-permute-start = (bf16[512,1024]{1,0:T(8,128)(2,1)}, bf16[512,1024]{1,0:T(8,128)(2,1)}, u32[]{:S(2)}, u32[]{:S(2)}) collective-permute-start(bf16[512,1024]{1,0:T(8,128)(2,1)} %raw_ref.1), channel_id=1, source_target_pairs={{0,1},{1,2},{2,3},{3,4},{4,5},{5,6},{6,7},{7,8},{8,9},{9,10},{10,1... | collective-permute-start | bytes 3145736 | tf_op jit(solution)/shard_map/ppermute | solution.py:16
  7.3 5.6 %collective-permute-start.3 = (bf16[512,1024]{1,0:T(8,128)(2,1)}, bf16[512,1024]{1,0:T(8,128)(2,1)S(1)}, u32[]{:S(2)}, u32[]{:S(2)}) collective-permute-start(bf16[512,1024]{1,0:T(8,128)(2,1)} %raw_ref.1), channel_id=1, source_target_pairs={{0,255},{1,0},{2,1},{3,2},{4,3},{5,4},{6,5},{7,6},{8,7},{9,8},{10,... | collective-permute-start | bytes 3145736 | tf_op jit(solution)/shard_map/ppermute | solution.py:16
  12.9 0.7 %copy-done.1 = s32[128]{0:T(128)S(1)} copy-done((s32[128]{0:T(128)S(1)}, s32[128]{0:T(128)}, u32[]{:S(2)}) %copy-start.1) | copy-done | bytes 536
  13.6 0.1 copy.3
  13.7 0.2 reduce-window.9
  13.9 0.7 %convert_reduce_fusion.3 = (s32[]{:T(128)}, s32[]{:T(128)}, s32[]{:T(128)}, s32[]{:T(128)}) fusion(s32[128,1]{1,0:T(8,128)S(1)} %reduce-window.9, s32[]{:T(128)S(6)} %add.36, s32[]{:T(128)S(6)} %rem.45, s32[]{:T(128)S(6)} %add.41, s32[]{:T(128)S(6)} %rem.57, s32[]{:T(128)S(6)} %add.37, s32[]{:T(128)S(6)} %add.39, s32[]{:T(128)S(6)} %rem.51), kind=kLoop, calls=%fused_computation.3 | loop fusion | flops 2428 | bytes 556 | tf_op jit(solution)/shard_map/reduce_sum | solution.py:23
  17.2 0.0 copy-start
  17.2 1.2 %copy-done = bf16[512,1024]{1,0:T(8,128)(2,1)S(1)} copy-done((bf16[512,1024]{1,0:T(8,128)(2,1)S(1)}, bf16[512,1024]{1,0:T(8,128)(2,1)}, u32[]{:S(2)}) %copy-start) | copy-done | bytes 1048600
  18.4 1.0 %shard_map.28 = (bf16[512,1024]{1,0:T(8,128)(2,1)S(1)}, f32[1,512]{1,0:T(1,128)S(1)}) custom-call(bf16[512,1024]{1,0:T(8,128)(2,1)S(1)} %copy-done), custom_call_target="tpu_custom_call" | custom-call | flops 536870912 | bytes 1048576 | tf_op jit(solution)/shard_map/pallas_call | solution.py:113
  19.4 0.1 add_convert_fusion.flags_ref
  19.5 0.0 collective-permute-done.1.down_ref
  19.5 0.0 collective-permute-done.2.up_ref
  19.5 0.6 %shard_map.29 = (bf16[512,1024]{1,0:T(8,128)(2,1)S(1)}, bf16[512,1024]{1,0:T(8,128)(2,1)S(1)}) custom-call(bf16[512,1024]{1,0:T(8,128)(2,1)S(1)} %collective-permute-done.1.down_ref, bf16[512,1024]{1,0:T(8,128)(2,1)S(1)} %collective-permute-done.2.up_ref), custom_call_target="tpu_custom_call" | custom-call | bytes 2097152 | tf_op jit(solution)/shard_map/pallas_call | solution.py:113
  20.2 12.2 %collective-permute-done.raw_ref = bf16[512,1024]{1,0:T(8,128)(2,1)} collective-permute-done((bf16[512,1024]{1,0:T(8,128)(2,1)}, bf16[512,1024]{1,0:T(8,128)(2,1)}, u32[]{:S(2)}, u32[]{:S(2)}) %collective-permute-start) | collective-permute-done | bytes 1048608 | tf_op jit(solution)/shard_map/ppermute | solution.py:16
  32.3 1.6 %shard_map.30 = (bf16[512,1024]{1,0:T(8,128)(2,1)S(1)}, f32[1,512]{1,0:T(1,128)S(1)}, f32[1,512]{1,0:T(1,128)S(1)}) custom-call(s32[4]{0:T(128)S(1)} %add_convert_fusion.flags_ref, bf16[512,1024]{1,0:T(8,128)(2,1)} %collective-permute-done.raw_ref, bf16[512,1024]{1,0:T(8,128)(2,1)S(1)} %get-tuple-element.14.own_ref, ...), custom_call_target="tpu_custom_call" | custom-call | flops 1073741824 | bytes 3147792 | tf_op jit(solution)/shard_map/pallas_call | solution.py:113
  33.9 0.0 collective-permute-done.3.raw_ref
  33.9 0.6 %shard_map.31 = (f32[1,512]{1,0:T(1,128)S(1)}, f32[1,512]{1,0:T(1,128)S(1)}) custom-call(s32[4]{0:T(128)S(1)} %add_convert_fusion.flags_ref, bf16[512,1024]{1,0:T(8,128)(2,1)S(1)} %collective-permute-done.3.raw_ref, bf16[512,1024]{1,0:T(8,128)(2,1)S(1)} %get-tuple-element.18.prev_ref, bf16[512,1024]{1,0:T(8,128)(2,1)S(1)} %get-tuple-element.19.far_ref, ...), custom_call_target="tpu_custom_call" | custom-call | flops 1073741824 | bytes 3147792 | tf_op jit(solution)/shard_map/pallas_call | solution.py:113
  34.5 4.1 %collective-permute-start.4 = (f32[1,512]{1,0:T(1,128)S(1)}, f32[1,512]{1,0:T(1,128)S(1)}, u32[]{:S(2)}, u32[]{:S(2)}) collective-permute-start(f32[1,512]{1,0:T(1,128)S(1)} %get-tuple-element.21), channel_id=1, source_target_pairs={{0,255},{1,0},{2,1},{3,2},{4,3},{5,4},{6,5},{7,6},{8,7},{9,8},{10,... | collective-permute-start | bytes 6152 | tf_op jit(solution)/shard_map/ppermute | solution.py:16
  38.6 0.0 collective-permute-start.5
  38.6 1.3 %collective-permute-done.4 = f32[1,512]{1,0:T(1,128)S(1)} collective-permute-done((f32[1,512]{1,0:T(1,128)S(1)}, f32[1,512]{1,0:T(1,128)S(1)}, u32[]{:S(2)}, u32[]{:S(2)}) %collective-permute-start.4) | collective-permute-done | bytes 2080 | tf_op jit(solution)/shard_map/ppermute | solution.py:16
  39.9 7.1 %collective-permute-done.5 = f32[1,512]{1,0:T(1,128)S(1)} collective-permute-done((f32[1,512]{1,0:T(1,128)S(1)}, f32[1,512]{1,0:T(1,128)S(1)}, u32[]{:S(2)}, u32[]{:S(2)}) %collective-permute-start.5) | collective-permute-done | bytes 2080 | tf_op jit(solution)/shard_map/ppermute | solution.py:16
  47.0 0.6 %maximum_maximum_fusion = f32[1,512]{1,0:T(1,128)} fusion(f32[1,512]{1,0:T(1,128)S(1)} %get-tuple-element.17, f32[1,512]{1,0:T(1,128)S(1)} %collective-permute-done.4, f32[1,512]{1,0:T(1,128)S(1)} %collective-permute-done.5), kind=kLoop, calls=%fused_computation.5 | loop fusion | flops 1024 | bytes 8192 | tf_op jit(solution)/shard_map/max | solution.py:158
  (1 shorter events, 0.0 us)
Async XLA Ops:
  0.0 19.5 %collective-permute-start.1 = (bf16[512,1024]{1,0:T(8,128)(2,1)}, bf16[512,1024]{1,0:T(8,128)(2,1)S(1)}, u32[]{:S(2)}, u32[]{:S(2)}) collective-permute-start(bf16[512,1024]{1,0:T(8,128)(2,1)} %raw_ref.1), channel_id=1, source_target_pairs={{0,4},{1,5},{2,6},{3,7},{4,8},{5,9},{6,10},{7,11},{8,12},{9,13},{1... | collective-permute-start | bytes 3145736 | tf_op jit(solution)/shard_map/ppermute | solution.py:16
  0.0 19.5 %collective-permute-start.2 = (bf16[512,1024]{1,0:T(8,128)(2,1)}, bf16[512,1024]{1,0:T(8,128)(2,1)S(1)}, u32[]{:S(2)}, u32[]{:S(2)}) collective-permute-start(bf16[512,1024]{1,0:T(8,128)(2,1)} %raw_ref.1), channel_id=1, source_target_pairs={{0,252},{1,253},{2,254},{3,255},{4,0},{5,1},{6,2},{7,3},{8,4},{9,5... | collective-permute-start | bytes 3145736 | tf_op jit(solution)/shard_map/ppermute | solution.py:16
  5.8 26.6 %collective-permute-start = (bf16[512,1024]{1,0:T(8,128)(2,1)}, bf16[512,1024]{1,0:T(8,128)(2,1)}, u32[]{:S(2)}, u32[]{:S(2)}) collective-permute-start(bf16[512,1024]{1,0:T(8,128)(2,1)} %raw_ref.1), channel_id=1, source_target_pairs={{0,1},{1,2},{2,3},{3,4},{4,5},{5,6},{6,7},{7,8},{8,9},{9,10},{10,1... | collective-permute-start | bytes 3145736 | tf_op jit(solution)/shard_map/ppermute | solution.py:16
  7.3 26.6 %collective-permute-start.3 = (bf16[512,1024]{1,0:T(8,128)(2,1)}, bf16[512,1024]{1,0:T(8,128)(2,1)S(1)}, u32[]{:S(2)}, u32[]{:S(2)}) collective-permute-start(bf16[512,1024]{1,0:T(8,128)(2,1)} %raw_ref.1), channel_id=1, source_target_pairs={{0,255},{1,0},{2,1},{3,2},{4,3},{5,4},{6,5},{7,6},{8,7},{9,8},{10,... | collective-permute-start | bytes 3145736 | tf_op jit(solution)/shard_map/ppermute | solution.py:16
  12.9 0.7 %copy-start.1 = (s32[128]{0:T(128)S(1)}, s32[128]{0:T(128)}, u32[]{:S(2)}) copy-start(s32[128]{0:T(128)} %param.3) | copy-start | bytes 1540
  17.2 1.2 %copy-start = (bf16[512,1024]{1,0:T(8,128)(2,1)S(1)}, bf16[512,1024]{1,0:T(8,128)(2,1)}, u32[]{:S(2)}) copy-start(bf16[512,1024]{1,0:T(8,128)(2,1)} %raw_ref.1) | copy-start | bytes 3145732
  34.5 5.4 %collective-permute-start.4 = (f32[1,512]{1,0:T(1,128)S(1)}, f32[1,512]{1,0:T(1,128)S(1)}, u32[]{:S(2)}, u32[]{:S(2)}) collective-permute-start(f32[1,512]{1,0:T(1,128)S(1)} %get-tuple-element.21), channel_id=1, source_target_pairs={{0,255},{1,0},{2,1},{3,2},{4,3},{5,4},{6,5},{7,6},{8,7},{9,8},{10,... | collective-permute-start | bytes 6152 | tf_op jit(solution)/shard_map/ppermute | solution.py:16
  38.6 8.4 %collective-permute-start.5 = (f32[1,512]{1,0:T(1,128)S(1)}, f32[1,512]{1,0:T(1,128)S(1)}, u32[]{:S(2)}, u32[]{:S(2)}) collective-permute-start(f32[1,512]{1,0:T(1,128)S(1)} %get-tuple-element.22), channel_id=1, source_target_pairs={{0,1},{1,2},{2,3},{3,4},{4,5},{5,6},{6,7},{7,8},{8,9},{9,10},{10,1... | collective-permute-start | bytes 6152 | tf_op jit(solution)/shard_map/ppermute | solution.py:16

commit v2 on v1

--- a/solution.py
+++ b/solution.py
@@ -11,9 +11,25 @@
 STRIP = 64
 
 
-def shifted(block, distance):
+def pair_mate(i, n):
+    return i ^ 1
+
+
+def other_neighbour(i, n):
+    return (i + 1) % n if i % 2 else (i - 1) % n
+
+
+def core_mate(i, n):
+    return i ^ 4
+
+
+def column_neighbour(i, n):
+    return (i + 4) % n if i // 4 % 2 else (i - 4) % n
+
+
+def swapped(block, partner):
     n = lax.axis_size(AXES)
-    return lax.ppermute(block, AXES, [(i, (i + distance) % n) for i in range(n)])
+    return lax.ppermute(block, AXES, [(i, partner(i, n)) for i in range(n)])
 
 
 def joined(bounds, lower, distance):
@@ -58,48 +74,46 @@
     high_ref[...] = column_max(jnp.where(row == col, LOWEST, products))
 
 
-def far_kernel(down_ref, up_ref, down_unit_ref, up_unit_ref):
-    write_units(down_ref, down_unit_ref)
-    write_units(up_ref, up_unit_ref)
+def other_kernel(flags_ref, raw_ref, own_ref, high_in_ref, unit_ref, high_ref):
+    write_units(raw_ref, unit_ref)
+    high_ref[...] = high_in_ref[...]
+
+    @pl.when(flags_ref[0] == 1)
+    def _():
+        products = products_of(unit_ref[...], own_ref[...])
+        high_ref[...] = jnp.maximum(high_ref[...], column_max(products))
 
 
-def prev_kernel(flags_ref, raw_ref, own_ref, far_ref, high_in_ref, unit_ref, high_ref, back_ref):
+def mate_kernel(
+    flags_ref, raw_ref, own_ref, other_ref, core_ref, column_ref, high_in_ref,
+    high_ref, back_ref, unit_ref,
+):
     write_units(raw_ref, unit_ref)
     high_ref[...] = high_in_ref[...]
     back_ref[...] = jnp.full_like(back_ref, LOWEST)
 
-    @pl.when(flags_ref[0] == 1)
+    @pl.when(flags_ref[1] == 1)
     def _():
-        products = products_of(own_ref[...], unit_ref[...])
-        high_ref[...] = jnp.maximum(high_ref[...], row_max(products))
-        back_ref[...] = column_max(products)
+        products = products_of(unit_ref[...], own_ref[...])
+        high_ref[...] = jnp.maximum(high_ref[...], column_max(products))
 
     @pl.when(flags_ref[2] == 1)
     def _():
-        back_ref[...] = jnp.maximum(
-            back_ref[...], column_max(products_of(far_ref[...], unit_ref[...]))
-        )
+        products = products_of(other_ref[...], unit_ref[...])
+        back_ref[0] = row_max(products)
+        back_ref[1] = column_max(products)
 
+    for slot, far_ref in ((3, core_ref), (5, column_ref)):
 
-def next_kernel(flags_ref, raw_ref, prev_ref, far_ref, back_in_ref, back_ref, ahead_ref, unit_ref):
-    back_ref[...] = back_in_ref[...]
-    ahead_ref[...] = jnp.full_like(ahead_ref, LOWEST)
+        @pl.when((flags_ref[slot] == 1) & (flags_ref[slot + 1] == 0))
+        def _():
+            products = products_of(far_ref[...], other_ref[...])
+            back_ref[0] = jnp.maximum(back_ref[0], column_max(products))
 
-    @pl.when(flags_ref[1] + flags_ref[3] > 0)
-    def _():
-        write_units(raw_ref, unit_ref)
-
-    @pl.when(flags_ref[1] == 1)
-    def _():
-        products = products_of(prev_ref[...], unit_ref[...])
-        back_ref[...] = jnp.maximum(back_ref[...], row_max(products))
-        ahead_ref[...] = column_max(products)
-
-    @pl.when(flags_ref[3] == 1)
-    def _():
-        ahead_ref[...] = jnp.maximum(
-            ahead_ref[...], column_max(products_of(far_ref[...], unit_ref[...]))
-        )
+        @pl.when((flags_ref[slot] == 1) & (flags_ref[slot + 1] == 1))
+        def _():
+            products = products_of(far_ref[...], unit_ref[...])
+            back_ref[1] = jnp.maximum(back_ref[1], column_max(products))
 
 
 VMEM = pl.BlockSpec(memory_space=pltpu.VMEM)
@@ -123,19 +137,27 @@
 
 def shards(embeddings, cluster_blocks):
     block, width = embeddings.shape
-    from_prev = shifted(embeddings, 1)
-    from_next = shifted(embeddings, -1)
-    from_down = shifted(embeddings, 4)
-    from_up = shifted(embeddings, -4)
+    from_other = swapped(embeddings, other_neighbour)
+    from_mate = swapped(embeddings, pair_mate)
 
     bounds = jnp.cumsum(cluster_blocks)
     me = lax.axis_index(AXES)
+    odd = me % 2
+    second = me // 4 % 2
+    with_prev = joined(bounds, me - 1, 1)
+    with_next = joined(bounds, me, 1)
+    around = joined(bounds, me - 1, 2)
+    before = joined(bounds, me - 4, 3)
+    after = joined(bounds, me + 1, 3)
     flags = jnp.stack(
         [
-            joined(bounds, me - 1, 1),
-            joined(bounds, me - 1, 2),
-            joined(bounds, me - 4, 3),
-            joined(bounds, me + 1, 3),
+            jnp.where(odd == 1, with_next, with_prev),
+            jnp.where(odd == 1, with_prev, with_next),
+            around,
+            jnp.where(second == 1, before, after),
+            jnp.where(second == 1, odd, 1 - odd),
+            jnp.where(second == 1, after, before),
+            jnp.where(second == 1, 1 - odd, odd),
         ]
     )
     units = ((block, width), jnp.bfloat16)
@@ -143,18 +165,17 @@
     tile = 2 * block * block * width
 
     own, high = call(own_kernel, (embeddings,), [units, line], flops=tile)
-    down, up = call(far_kernel, (from_down, from_up), [units, units])
-    prev, high, back = call(
-        prev_kernel, (flags, from_prev, own, down, high), [units, line, line], flops=2 * tile
-    )
-    back, ahead = call(
-        next_kernel,
-        (flags, from_next, prev, up, back),
-        [line, line],
+    column = swapped(own, column_neighbour)
+    core = swapped(own, core_mate)
+    other, high = call(other_kernel, (flags, from_other, own, high), [units, line], flops=tile)
+    high, back = call(
+        mate_kernel,
+        (flags, from_mate, own, other, core, column, high),
+        [line, ((2, 1, block), jnp.float32)],
         scratch=[pltpu.VMEM(*units)],
         flops=2 * tile,
     )
-    returned = jnp.maximum(shifted(back, -1), shifted(ahead, 1))
+    returned = jnp.maximum(swapped(back[0], other_neighbour), swapped(back[1], pair_mate))
     return jnp.maximum(high, returned).reshape(block)
 
 

time: 47.8 us -> 48.2 us (level)
  starting transfers between devices: 17 us -> 10.9 us
  waiting for transfers between devices: 20.6 us -> 25.3 us
  Pallas kernels: 3.78 us -> 6.18 us
  local copies, waits for them, and re-layouts: 1.99 us -> 0.86 us
  between operations: 2.63 us -> 3.19 us
    ppermute x6, starting transfers between devices: 17 us -> 10.9 us  [swapped(): return lax.ppermute(block, AXES, [(i, partner(i, n)) for i in range(n)])]
    ppermute x6, waiting for transfers between devices: 20.6 us -> 25.3 us  [swapped(): return lax.ppermute(block, AXES, [(i, partner(i, n)) for i in range(n)])]
    pallas_call x4 -> x3, Pallas kernels: 3.78 us -> 6.18 us  [call(): pl.pallas_call(kernel, in_specs=specs, out_specs=[VMEM] * len(outs), out_...]
    unnamed x4 -> x2, local copies, waits for them, and re-layouts: 1.87 us -> 0.65 us
  transfers between devices with their start and end apart: 6 -> 6, of which waited for: 3 -> 4; matrix products, arithmetic and copies ran while one was open for 2% -> 2% of each run, Pallas kernels for 7% -> 8%
where the time goes in v2:
time: 48.2 us; the launch traced here: 48 us
  waiting for transfers between devices  25.3 us (52%)
  starting transfers between devices  10.9 us (23%)
  Pallas kernels  6.18 us (13%)
  between operations  3.19 us (7%)
  other arithmetic  1.49 us (3%)
  local copies, waits for them, and re-layouts  0.86 us (2%)
    ppermute x6, waiting for transfers between devices, swapped(): return lax.ppermute(block, AXES, [(i, partner(i, n)) for i in range(n)])  25.3 us
    ppermute x6, starting transfers between devices, swapped(): return lax.ppermute(block, AXES, [(i, partner(i, n)) for i in range(n)])  10.9 us
    pallas_call x3, Pallas kernels, call(): pl.pallas_call(kernel, in_specs=specs, out_specs=[VMEM] * len(outs), out_...  6.18 us
  transfers between devices with their start and end apart: 6, of which 4 were waited for; matrix products, arithmetic and copies ran while one was open for 2% of the time, Pallas kernels for 8%

profile of v2, /device:TPU:0, one launch (start us, length us, event | category | flops | bytes accessed | tf_op | source)
XLA Modules:
  0.0 48.0 jit_solution(1206598331580790134)
XLA Ops:
  0.0 8.2 %collective-permute-start.1 = (bf16[512,1024]{1,0:T(8,128)(2,1)}, bf16[512,1024]{1,0:T(8,128)(2,1)}, u32[]{:S(2)}, u32[]{:S(2)}) collective-permute-start(bf16[512,1024]{1,0:T(8,128)(2,1)} %raw_ref.1), channel_id=1, source_target_pairs={{0,255},{1,2},{2,1},{3,4},{4,3},{5,6},{6,5},{7,8},{8,7},{9,10},{10... | collective-permute-start | bytes 3145736 | tf_op jit(solution)/shard_map/ppermute | solution.py:32
  8.2 2.3 %shard_map.28 = (bf16[512,1024]{1,0:T(8,128)(2,1)S(1)}, f32[1,512]{1,0:T(1,128)S(1)}) custom-call(bf16[512,1024]{1,0:T(8,128)(2,1)} %raw_ref.1), custom_call_target="tpu_custom_call" | custom-call | flops 536870912 | bytes 1048576 | tf_op jit(solution)/shard_map/pallas_call | solution.py:127
  10.5 0.1 collective-permute-start.2
  10.6 0.9 %collective-permute-start.3 = (bf16[512,1024]{1,0:T(8,128)(2,1)S(1)}, bf16[512,1024]{1,0:T(8,128)(2,1)S(1)}, u32[]{:S(2)}, u32[]{:S(2)}) collective-permute-start(bf16[512,1024]{1,0:T(8,128)(2,1)S(1)} %get-tuple-element.11.own_ref), channel_id=1, source_target_pairs={{0,252},{1,253},{2,254},{3,255},{4,8},{5,9},{6,10},{7,11},{8,4},{9... | collective-permute-start | bytes 3145736 | tf_op jit(solution)/shard_map/ppermute | solution.py:32
  11.5 0.4 collective-permute-start
  12.0 0.0 copy-start
  12.0 0.7 %copy-done = s32[128]{0:T(128)S(1)} copy-done((s32[128]{0:T(128)S(1)}, s32[128]{0:T(128)}, u32[]{:S(2)}) %copy-start) | copy-done | bytes 536
  12.6 0.1 copy.3
  12.7 0.2 reduce-window.9
  12.9 0.7 %convert_reduce_fusion = (s32[]{:T(128)}, s32[]{:T(128)}, s32[]{:T(128)}, s32[]{:T(128)}, s32[]{:T(128)}) fusion(s32[128,1]{1,0:T(8,128)S(1)} %reduce-window.9, s32[]{:T(128)S(6)} %add.59, s32[]{:T(128)S(6)} %rem.126, s32[]{:T(128)S(6)} %add.54, s32[]{:T(128)S(6)} %rem.105, s32[]{:T(128)S(6)} %add.53, s32[]{:T(128)S(6)} %add.51, s32[]{:T(128)S(6)} %rem.99, ...), kind=kLoop, calls=%fused_computation | loop fusion | flops 3067 | bytes 568 | tf_op jit(solution)/shard_map/reduce_sum | solution.py:39
  16.8 0.1 stack.35.flags_ref
  16.9 4.3 %collective-permute-done.1.raw_ref = bf16[512,1024]{1,0:T(8,128)(2,1)} collective-permute-done((bf16[512,1024]{1,0:T(8,128)(2,1)}, bf16[512,1024]{1,0:T(8,128)(2,1)}, u32[]{:S(2)}, u32[]{:S(2)}) %collective-permute-start.1) | collective-permute-done | bytes 1048608 | tf_op jit(solution)/shard_map/ppermute | solution.py:32
  21.1 1.6 %shard_map.29 = (bf16[512,1024]{1,0:T(8,128)(2,1)S(1)}, f32[1,512]{1,0:T(1,128)S(1)}) custom-call(s32[7]{0:T(128)S(1)} %stack.35.flags_ref, bf16[512,1024]{1,0:T(8,128)(2,1)} %collective-permute-done.1.raw_ref, bf16[512,1024]{1,0:T(8,128)(2,1)S(1)} %get-tuple-element.11.own_ref, f32[1,512]{1,0:T(1,128)S(1)} %get-tuple-element.12.high_in_ref), custom_call_target="tpu_custom_call" | custom-call | flops 536870912 | bytes 2099228 | tf_op jit(solution)/shard_map/pallas_call | solution.py:127
  22.7 0.0 collective-permute-done.2.core_ref
  22.7 9.3 %collective-permute-done.3.column_ref = bf16[512,1024]{1,0:T(8,128)(2,1)S(1)} collective-permute-done((bf16[512,1024]{1,0:T(8,128)(2,1)S(1)}, bf16[512,1024]{1,0:T(8,128)(2,1)S(1)}, u32[]{:S(2)}, u32[]{:S(2)}) %collective-permute-start.3) | collective-permute-done | bytes 1048608 | tf_op jit(solution)/shard_map/ppermute | solution.py:32
  32.0 4.5 %collective-permute-done.raw_ref = bf16[512,1024]{1,0:T(8,128)(2,1)} collective-permute-done((bf16[512,1024]{1,0:T(8,128)(2,1)}, bf16[512,1024]{1,0:T(8,128)(2,1)}, u32[]{:S(2)}, u32[]{:S(2)}) %collective-permute-start) | collective-permute-done | bytes 1048608 | tf_op jit(solution)/shard_map/ppermute | solution.py:32
  36.5 2.3 %shard_map.30 = (f32[1,512]{1,0:T(1,128)S(1)}, f32[2,1,512]{2,1,0:T(1,128)S(1)}) custom-call(s32[7]{0:T(128)S(1)} %stack.35.flags_ref, bf16[512,1024]{1,0:T(8,128)(2,1)} %collective-permute-done.raw_ref, bf16[512,1024]{1,0:T(8,128)(2,1)S(1)} %get-tuple-element.11.own_ref, bf16[512,1024]{1,0:T(8,128)(2,1)S(1)} %get-tuple-element.13.other_ref, ...), custom_call_target="tpu_custom_call" | custom-call | flops 1073741824 | bytes 5244956 | tf_op jit(solution)/shard_map/pallas_call | solution.py:127
  38.8 0.1 collective-permute-start.4
  38.9 1.2 %collective-permute-start.5 = (f32[1,512]{1,0:T(1,128)S(1)}, f32[1,512]{1,0:T(1,128)S(1)}, u32[]{:S(2)}, u32[]{:S(2)}) collective-permute-start(f32[1,512]{1,0:T(1,128)S(1)} %get-tuple-element.22), channel_id=1, source_target_pairs={{0,1},{1,0},{2,3},{3,2},{4,5},{5,4},{6,7},{7,6},{8,9},{9,8},{10,11... | collective-permute-start | bytes 6152 | tf_op jit(solution)/shard_map/ppermute | solution.py:32
  40.1 7.2 %collective-permute-done.4 = f32[1,512]{1,0:T(1,128)S(1)} collective-permute-done((f32[1,512]{1,0:T(1,128)S(1)}, f32[1,512]{1,0:T(1,128)S(1)}, u32[]{:S(2)}, u32[]{:S(2)}) %collective-permute-start.4) | collective-permute-done | bytes 2080 | tf_op jit(solution)/shard_map/ppermute | solution.py:32
  47.4 0.0 collective-permute-done.5
  47.4 0.6 %maximum_maximum_fusion = f32[1,512]{1,0:T(1,128)} fusion(f32[1,512]{1,0:T(1,128)S(1)} %get-tuple-element.15, f32[1,512]{1,0:T(1,128)S(1)} %collective-permute-done.4, f32[1,512]{1,0:T(1,128)S(1)} %collective-permute-done.5), kind=kLoop, calls=%fused_computation.6 | loop fusion | flops 1024 | bytes 8192 | tf_op jit(solution)/shard_map/max | solution.py:179
  (1 shorter events, 0.0 us)
Async XLA Ops:
  0.0 21.1 %collective-permute-start.1 = (bf16[512,1024]{1,0:T(8,128)(2,1)}, bf16[512,1024]{1,0:T(8,128)(2,1)}, u32[]{:S(2)}, u32[]{:S(2)}) collective-permute-start(bf16[512,1024]{1,0:T(8,128)(2,1)} %raw_ref.1), channel_id=1, source_target_pairs={{0,255},{1,2},{2,1},{3,4},{4,3},{5,6},{6,5},{7,8},{8,7},{9,10},{10... | collective-permute-start | bytes 3145736 | tf_op jit(solution)/shard_map/ppermute | solution.py:32
  10.5 12.2 %collective-permute-start.2 = (bf16[512,1024]{1,0:T(8,128)(2,1)S(1)}, bf16[512,1024]{1,0:T(8,128)(2,1)S(1)}, u32[]{:S(2)}, u32[]{:S(2)}) collective-permute-start(bf16[512,1024]{1,0:T(8,128)(2,1)S(1)} %get-tuple-element.11.own_ref), channel_id=1, source_target_pairs={{0,4},{1,5},{2,6},{3,7},{4,0},{5,1},{6,2},{7,3},{8,12},{9,13},{10,... | collective-permute-start | bytes 3145736 | tf_op jit(solution)/shard_map/ppermute | solution.py:32
  10.6 21.4 %collective-permute-start.3 = (bf16[512,1024]{1,0:T(8,128)(2,1)S(1)}, bf16[512,1024]{1,0:T(8,128)(2,1)S(1)}, u32[]{:S(2)}, u32[]{:S(2)}) collective-permute-start(bf16[512,1024]{1,0:T(8,128)(2,1)S(1)} %get-tuple-element.11.own_ref), channel_id=1, source_target_pairs={{0,252},{1,253},{2,254},{3,255},{4,8},{5,9},{6,10},{7,11},{8,4},{9... | collective-permute-start | bytes 3145736 | tf_op jit(solution)/shard_map/ppermute | solution.py:32
  11.5 24.9 %collective-permute-start = (bf16[512,1024]{1,0:T(8,128)(2,1)}, bf16[512,1024]{1,0:T(8,128)(2,1)}, u32[]{:S(2)}, u32[]{:S(2)}) collective-permute-start(bf16[512,1024]{1,0:T(8,128)(2,1)} %raw_ref.1), channel_id=1, source_target_pairs={{0,1},{1,0},{2,3},{3,2},{4,5},{5,4},{6,7},{7,6},{8,9},{9,8},{10,11... | collective-permute-start | bytes 3145736 | tf_op jit(solution)/shard_map/ppermute | solution.py:32
  12.0 0.7 %copy-start = (s32[128]{0:T(128)S(1)}, s32[128]{0:T(128)}, u32[]{:S(2)}) copy-start(s32[128]{0:T(128)} %param.3) | copy-start | bytes 1540
  38.8 8.5 %collective-permute-start.4 = (f32[1,512]{1,0:T(1,128)S(1)}, f32[1,512]{1,0:T(1,128)S(1)}, u32[]{:S(2)}, u32[]{:S(2)}) collective-permute-start(f32[1,512]{1,0:T(1,128)S(1)} %get-tuple-element.23), channel_id=1, source_target_pairs={{0,255},{1,2},{2,1},{3,4},{4,3},{5,6},{6,5},{7,8},{8,7},{9,10},{10... | collective-permute-start | bytes 6152 | tf_op jit(solution)/shard_map/ppermute | solution.py:32
  38.9 8.4 %collective-permute-start.5 = (f32[1,512]{1,0:T(1,128)S(1)}, f32[1,512]{1,0:T(1,128)S(1)}, u32[]{:S(2)}, u32[]{:S(2)}) collective-permute-start(f32[1,512]{1,0:T(1,128)S(1)} %get-tuple-element.22), channel_id=1, source_target_pairs={{0,1},{1,0},{2,3},{3,2},{4,5},{5,4},{6,7},{7,6},{8,9},{9,8},{10,11... | collective-permute-start | bytes 6152 | tf_op jit(solution)/shard_map/ppermute | solution.py:32

commit v3 on v2

--- a/solution.py
+++ b/solution.py
@@ -16,7 +16,8 @@
 
 
 def other_neighbour(i, n):
-    return (i + 1) % n if i % 2 else (i - 1) % n
+    j = i + 1 if i % 2 else i - 1
+    return j if 0 <= j < n else None
 
 
 def core_mate(i, n):
@@ -24,20 +25,21 @@
 
 
 def column_neighbour(i, n):
-    return (i + 4) % n if i // 4 % 2 else (i - 4) % n
+    j = i + 4 if i // 4 % 2 else i - 4
+    return j if 0 <= j < n else i ^ 3
 
 
 def swapped(block, partner):
     n = lax.axis_size(AXES)
-    return lax.ppermute(block, AXES, [(i, partner(i, n)) for i in range(n)])
+    pairs = [(i, partner(i, n)) for i in range(n)]
+    return lax.ppermute(block, AXES, [p for p in pairs if p[1] is not None])
 
 
 def joined(bounds, lower, distance):
-    n = lax.axis_size(AXES)
-    lower = lax.rem(lower + n, n)
     upper = lower + distance
     crossing = jnp.sum(((bounds > lower) & (bounds <= upper)).astype(jnp.int32))
-    return ((upper < n) & (crossing == 0)).astype(jnp.int32)
+    inside = (lower >= 0) & (upper < lax.axis_size(AXES))
+    return (inside & (crossing == 0)).astype(jnp.int32)
 
 
 def write_units(raw_ref, unit_ref):
@@ -84,36 +86,46 @@
         high_ref[...] = jnp.maximum(high_ref[...], column_max(products))
 
 
-def mate_kernel(
-    flags_ref, raw_ref, own_ref, other_ref, core_ref, column_ref, high_in_ref,
-    high_ref, back_ref, unit_ref,
-):
+def mate_kernel(flags_ref, raw_ref, other_ref, unit_ref, to_other_ref, to_mate_ref):
     write_units(raw_ref, unit_ref)
-    high_ref[...] = high_in_ref[...]
-    back_ref[...] = jnp.full_like(back_ref, LOWEST)
-
-    @pl.when(flags_ref[1] == 1)
-    def _():
-        products = products_of(unit_ref[...], own_ref[...])
-        high_ref[...] = jnp.maximum(high_ref[...], column_max(products))
+    to_other_ref[...] = jnp.full_like(to_other_ref, LOWEST)
+    to_mate_ref[...] = jnp.full_like(to_mate_ref, LOWEST)
 
     @pl.when(flags_ref[2] == 1)
     def _():
         products = products_of(other_ref[...], unit_ref[...])
-        back_ref[0] = row_max(products)
-        back_ref[1] = column_max(products)
-
-    for slot, far_ref in ((3, core_ref), (5, column_ref)):
-
-        @pl.when((flags_ref[slot] == 1) & (flags_ref[slot + 1] == 0))
+        to_other_ref[...] = row_max(products)
+        to_mate_ref[...] = column_max(products)
+
+
+def far_kernel(
+    flags_ref, core_ref, column_ref, other_ref, mate_ref, own_ref, other_in_ref, mate_in_ref, high_in_ref,
+    to_other_ref, to_mate_ref, high_ref,
+):
+    to_other_ref[...] = other_in_ref[...]
+    to_mate_ref[...] = mate_in_ref[...]
+    high_ref[...] = high_in_ref[...]
+    for far_ref, slot, near_ref, line_ref in (
+        (core_ref, 3, other_ref, to_other_ref),
+        (core_ref, 4, mate_ref, to_mate_ref),
+        (column_ref, 5, other_ref, to_other_ref),
+        (column_ref, 6, mate_ref, to_mate_ref),
+        (column_ref, 7, own_ref, high_ref),
+    ):
+
+        @pl.when(flags_ref[slot] == 1)
         def _():
-            products = products_of(far_ref[...], other_ref[...])
-            back_ref[0] = jnp.maximum(back_ref[0], column_max(products))
-
-        @pl.when((flags_ref[slot] == 1) & (flags_ref[slot + 1] == 1))
-        def _():
-            products = products_of(far_ref[...], unit_ref[...])
-            back_ref[1] = jnp.maximum(back_ref[1], column_max(products))
+            products = products_of(far_ref[...], near_ref[...])
+            line_ref[...] = jnp.maximum(line_ref[...], column_max(products))
+
+
+def last_kernel(flags_ref, mate_ref, own_ref, high_in_ref, high_ref):
+    high_ref[...] = high_in_ref[...]
+
+    @pl.when(flags_ref[1] == 1)
+    def _():
+        products = products_of(mate_ref[...], own_ref[...])
+        high_ref[...] = jnp.maximum(high_ref[...], column_max(products))
 
 
 VMEM = pl.BlockSpec(memory_space=pltpu.VMEM)
@@ -149,15 +161,22 @@
     around = joined(bounds, me - 1, 2)
     before = joined(bounds, me - 4, 3)
     after = joined(bounds, me + 1, 3)
+    edge = jnp.where(me == 0, joined(bounds, 0, 3), 0)
+    last = lax.axis_size(AXES) - 1
+    edge = jnp.where(me == last, joined(bounds, last - 3, 3), edge)
+    with_core = jnp.where(second == 1, before, after)
+    with_column = jnp.where(second == 1, after, before)
+    core_to_mate = jnp.where(second == 1, odd, 1 - odd)
     flags = jnp.stack(
         [
             jnp.where(odd == 1, with_next, with_prev),
             jnp.where(odd == 1, with_prev, with_next),
             around,
-            jnp.where(second == 1, before, after),
-            jnp.where(second == 1, odd, 1 - odd),
-            jnp.where(second == 1, after, before),
-            jnp.where(second == 1, 1 - odd, odd),
+            with_core * (1 - core_to_mate),
+            with_core * core_to_mate,
+            with_column * core_to_mate,
+            with_column * (1 - core_to_mate),
+            edge,
         ]
     )
     units = ((block, width), jnp.bfloat16)
@@ -168,14 +187,19 @@
     column = swapped(own, column_neighbour)
     core = swapped(own, core_mate)
     other, high = call(other_kernel, (flags, from_other, own, high), [units, line], flops=tile)
-    high, back = call(
-        mate_kernel,
-        (flags, from_mate, own, other, core, column, high),
-        [line, ((2, 1, block), jnp.float32)],
-        scratch=[pltpu.VMEM(*units)],
-        flops=2 * tile,
-    )
-    returned = jnp.maximum(swapped(back[0], other_neighbour), swapped(back[1], pair_mate))
+    mate, to_other, to_mate = call(
+        mate_kernel, (flags, from_mate, other), [units, line, line], flops=tile
+    )
+    to_other, to_mate, high = call(
+        far_kernel,
+        (flags, core, column, other, mate, own, to_other, to_mate, high),
+        [line, line, line],
+        flops=tile,
+    )
+    returned = swapped(to_other, other_neighbour), swapped(to_mate, pair_mate)
+    high = call(last_kernel, (flags, mate, own, high), [line], flops=tile)[0]
+    has_other = (me > 0) & (me < last)
+    returned = jnp.maximum(jnp.where(has_other, returned[0], LOWEST), returned[1])
     return jnp.maximum(high, returned).reshape(block)
 
 

time: 48.2 us -> 52.5 us (1.089)
  the two profiles are of different devices: /device:TPU:0 before, /device:TPU:1 now
where the time goes in v3:
time: 52.5 us; the launch traced here: 52.2 us
  waiting for transfers between devices  24.1 us (46%)
  starting transfers between devices  13.5 us (26%)
  Pallas kernels  6.39 us (12%)
  between operations  4.48 us (9%)
  local copies, waits for them, and re-layouts  2.1 us (4%)
  other arithmetic  1.59 us (3%)
    ppermute x6, waiting for transfers between devices, swapped(): return lax.ppermute(block, AXES, [p for p in pairs if p[1] is not None])  24.1 us
    ppermute x6, starting transfers between devices, swapped(): return lax.ppermute(block, AXES, [p for p in pairs if p[1] is not None])  13.5 us
    pallas_call x5, Pallas kernels, call(): pl.pallas_call(kernel, in_specs=specs, out_specs=[VMEM] * len(outs), out_...  6.39 us
    unnamed x4, local copies, waits for them, and re-layouts  1.9 us
  transfers between devices with their start and end apart: 6, of which 2 were waited for; matrix products, arithmetic and copies ran while one was open for 2% of the time, Pallas kernels for 8%

profile of v3, /device:TPU:1, one launch (start us, length us, event | category | flops | bytes accessed | tf_op | source)
XLA Modules:
  0.0 52.2 jit_solution(13030842375741793312)
XLA Ops:
  0.0 6.0 %collective-permute-start.1 = (bf16[512,1024]{1,0:T(8,128)(2,1)}, bf16[512,1024]{1,0:T(8,128)(2,1)S(1)}, u32[]{:S(2)}, u32[]{:S(2)}) collective-permute-start(bf16[512,1024]{1,0:T(8,128)(2,1)} %raw_ref.1), channel_id=1, source_target_pairs={{1,2},{2,1},{3,4},{4,3},{5,6},{6,5},{7,8},{8,7},{9,10},{10,9},{11,... | collective-permute-start | bytes 3145736 | tf_op jit(solution)/shard_map/ppermute | solution.py:35
  6.0 0.1 collective-permute-start
  6.1 1.2 %copy-done = bf16[512,1024]{1,0:T(8,128)(2,1)S(1)} copy-done((bf16[512,1024]{1,0:T(8,128)(2,1)S(1)}, bf16[512,1024]{1,0:T(8,128)(2,1)}, u32[]{:S(2)}) %copy-start) | copy-done | bytes 1048600
  7.4 1.0 %shard_map.28 = (bf16[512,1024]{1,0:T(8,128)(2,1)S(1)}, f32[1,512]{1,0:T(1,128)S(1)}) custom-call(bf16[512,1024]{1,0:T(8,128)(2,1)S(1)} %copy-done), custom_call_target="tpu_custom_call" | custom-call | flops 536870912 | bytes 1048576 | tf_op jit(solution)/shard_map/pallas_call | solution.py:139
  8.4 0.6 %collective-permute-start.2 = (bf16[512,1024]{1,0:T(8,128)(2,1)S(1)}, bf16[512,1024]{1,0:T(8,128)(2,1)}, u32[]{:S(2)}, u32[]{:S(2)}) collective-permute-start(bf16[512,1024]{1,0:T(8,128)(2,1)S(1)} %get-tuple-element.15.own_ref), channel_id=1, source_target_pairs={{0,4},{1,5},{2,6},{3,7},{4,0},{5,1},{6,2},{7,3},{8,12},{9,13},{10,... | collective-permute-start | bytes 3145736 | tf_op jit(solution)/shard_map/ppermute | solution.py:35
  9.0 1.2 %collective-permute-start.3 = (bf16[512,1024]{1,0:T(8,128)(2,1)S(1)}, bf16[512,1024]{1,0:T(8,128)(2,1)}, u32[]{:S(2)}, u32[]{:S(2)}) collective-permute-start(bf16[512,1024]{1,0:T(8,128)(2,1)S(1)} %get-tuple-element.15.own_ref), channel_id=1, source_target_pairs={{0,3},{1,2},{2,1},{3,0},{4,8},{5,9},{6,10},{7,11},{8,4},{9,5},{10,... | collective-permute-start | bytes 3145736 | tf_op jit(solution)/shard_map/ppermute | solution.py:35
  10.2 0.7 %copy-done.1 = s32[128]{0:T(128)S(1)} copy-done((s32[128]{0:T(128)S(1)}, s32[128]{0:T(128)}, u32[]{:S(2)}) %copy-start.1) | copy-done | bytes 536
  10.9 0.1 copy.3
  11.0 0.2 reduce-window.9
  11.2 0.8 %convert_reduce_fusion = (s32[]{:T(128)}, s32[]{:T(128)}, s32[]{:T(128)}, s32[]{:T(128)}, s32[]{:T(128)}, /*index=5*/s32[]{:T(128)}, s32[]{:T(128)}) fusion(s32[128,1]{1,0:T(8,128)S(1)} %reduce-window.9, s32[]{:T(128)S(6)} %sub.18, s32[]{:T(128)S(6)} %sub.20, s32[]{:T(128)S(6)} %add.31, s32[]{:T(128)S(6)} %add.33, s32[]{:T(128)S(6)} %add.35), kind=kLoop, calls=%fused_computation | loop fusion | flops 4217 | bytes 560 | tf_op jit(solution)/shard_map/reduce_sum | solution.py:40
  16.4 0.1 stack.39.flags_ref
  16.4 23.0 %collective-permute-done.1.raw_ref = bf16[512,1024]{1,0:T(8,128)(2,1)S(1)} collective-permute-done((bf16[512,1024]{1,0:T(8,128)(2,1)}, bf16[512,1024]{1,0:T(8,128)(2,1)S(1)}, u32[]{:S(2)}, u32[]{:S(2)}) %collective-permute-start.1) | collective-permute-done | bytes 1048608 | tf_op jit(solution)/shard_map/ppermute | solution.py:35
  39.5 0.9 %shard_map.29 = (bf16[512,1024]{1,0:T(8,128)(2,1)S(1)}, f32[1,512]{1,0:T(1,128)S(1)}) custom-call(s32[8]{0:T(128)S(1)} %stack.39.flags_ref, bf16[512,1024]{1,0:T(8,128)(2,1)S(1)} %collective-permute-done.1.raw_ref, bf16[512,1024]{1,0:T(8,128)(2,1)S(1)} %get-tuple-element.15.own_ref, f32[1,512]{1,0:T(1,128)S(1)} %get-tuple-element.16.high_in_ref), custom_call_target="tpu_custom_call" | custom-call | flops 536870912 | bytes 2099232 | tf_op jit(solution)/shard_map/pallas_call | solution.py:139
  40.3 0.0 collective-permute-done.raw_ref
  40.3 0.9 %shard_map.30 = (bf16[512,1024]{1,0:T(8,128)(2,1)S(1)}, f32[1,512]{1,0:T(1,128)S(1)}, f32[1,512]{1,0:T(1,128)S(1)}) custom-call(s32[8]{0:T(128)S(1)} %stack.39.flags_ref, bf16[512,1024]{1,0:T(8,128)(2,1)S(1)} %collective-permute-done.raw_ref, bf16[512,1024]{1,0:T(8,128)(2,1)S(1)} %get-tuple-element.17.other_ref), custom_call_target="tpu_custom_call" | custom-call | flops 536870912 | bytes 2097184 | tf_op jit(solution)/shard_map/pallas_call | solution.py:139
  41.2 0.0 collective-permute-done.2.core_ref
  41.2 0.0 collective-permute-done.3.column_ref
  41.2 2.3 %shard_map.31 = (f32[1,512]{1,0:T(1,128)S(1)}, f32[1,512]{1,0:T(1,128)S(1)}, f32[1,512]{1,0:T(1,128)S(1)}) custom-call(s32[8]{0:T(128)S(1)} %stack.39.flags_ref, bf16[512,1024]{1,0:T(8,128)(2,1)} %collective-permute-done.2.core_ref, bf16[512,1024]{1,0:T(8,128)(2,1)} %collective-permute-done.3.column_ref, bf16[512,1024]{1,0:T(8,128)(2,1)S(1)} %get-tuple-element.17.other_ref, ...), custom_call_target="tpu_custom_call" | custom-call | flops 536870912 | bytes 5249056 | tf_op jit(solution)/shard_map/pallas_call | solution.py:139
  43.6 5.5 %collective-permute-start.4 = (f32[1,512]{1,0:T(1,128)S(1)}, f32[1,512]{1,0:T(1,128)S(1)}, u32[]{:S(2)}, u32[]{:S(2)}) collective-permute-start(f32[1,512]{1,0:T(1,128)S(1)} %get-tuple-element.23), channel_id=1, source_target_pairs={{1,2},{2,1},{3,4},{4,3},{5,6},{6,5},{7,8},{8,7},{9,10},{10,9},{11,... | collective-permute-start | bytes 6152 | tf_op jit(solution)/shard_map/ppermute | solution.py:35
  49.1 0.1 collective-permute-start.5
  49.2 1.3 %shard_map.32 = f32[1,512]{1,0:T(1,128)S(1)} custom-call(s32[8]{0:T(128)S(1)} %stack.39.flags_ref, bf16[512,1024]{1,0:T(8,128)(2,1)S(1)} %get-tuple-element.18.mate_ref, bf16[512,1024]{1,0:T(8,128)(2,1)S(1)} %get-tuple-element.15.own_ref, f32[1,512]{1,0:T(1,128)S(1)} %get-tuple-element.22.high_in_ref), custom_call_target="tpu_custom_call" | custom-call | flops 536870912 | bytes 2099232 | tf_op jit(solution)/shard_map/pallas_call | solution.py:139
  50.5 0.0 collective-permute-done.4
  50.5 1.1 %collective-permute-done.5 = f32[1,512]{1,0:T(1,128)S(1)} collective-permute-done((f32[1,512]{1,0:T(1,128)S(1)}, f32[1,512]{1,0:T(1,128)S(1)}, u32[]{:S(2)}, u32[]{:S(2)}) %collective-permute-start.5) | collective-permute-done | bytes 2080 | tf_op jit(solution)/shard_map/ppermute | solution.py:35
  51.6 0.6 %fusion.1 = f32[1,512]{1,0:T(1,128)} fusion(f32[1,512]{1,0:T(1,128)S(1)} %shard_map.32, f32[1,512]{1,0:T(1,128)S(1)} %collective-permute-done.5, f32[1,512]{1,0:T(1,128)S(1)} %collective-permute-done.4, pred[]{:T(512)S(6)} %and.97), kind=kLoop, calls=%fused_computation.11 | loop fusion | flops 1536 | bytes 8193 | tf_op jit(solution)/shard_map/max | solution.py:203
  (2 shorter events, 0.0 us)
Async XLA Ops:
  0.0 39.5 %collective-permute-start.1 = (bf16[512,1024]{1,0:T(8,128)(2,1)}, bf16[512,1024]{1,0:T(8,128)(2,1)S(1)}, u32[]{:S(2)}, u32[]{:S(2)}) collective-permute-start(bf16[512,1024]{1,0:T(8,128)(2,1)} %raw_ref.1), channel_id=1, source_target_pairs={{1,2},{2,1},{3,4},{4,3},{5,6},{6,5},{7,8},{8,7},{9,10},{10,9},{11,... | collective-permute-start | bytes 3145736 | tf_op jit(solution)/shard_map/ppermute | solution.py:35
  6.0 34.3 %collective-permute-start = (bf16[512,1024]{1,0:T(8,128)(2,1)}, bf16[512,1024]{1,0:T(8,128)(2,1)S(1)}, u32[]{:S(2)}, u32[]{:S(2)}) collective-permute-start(bf16[512,1024]{1,0:T(8,128)(2,1)} %raw_ref.1), channel_id=1, source_target_pairs={{0,1},{1,0},{2,3},{3,2},{4,5},{5,4},{6,7},{7,6},{8,9},{9,8},{10,11... | collective-permute-start | bytes 3145736 | tf_op jit(solution)/shard_map/ppermute | solution.py:35
  6.1 1.3 %copy-start = (bf16[512,1024]{1,0:T(8,128)(2,1)S(1)}, bf16[512,1024]{1,0:T(8,128)(2,1)}, u32[]{:S(2)}) copy-start(bf16[512,1024]{1,0:T(8,128)(2,1)} %raw_ref.1) | copy-start | bytes 3145732
  8.4 32.8 %collective-permute-start.2 = (bf16[512,1024]{1,0:T(8,128)(2,1)S(1)}, bf16[512,1024]{1,0:T(8,128)(2,1)}, u32[]{:S(2)}, u32[]{:S(2)}) collective-permute-start(bf16[512,1024]{1,0:T(8,128)(2,1)S(1)} %get-tuple-element.15.own_ref), channel_id=1, source_target_pairs={{0,4},{1,5},{2,6},{3,7},{4,0},{5,1},{6,2},{7,3},{8,12},{9,13},{10,... | collective-permute-start | bytes 3145736 | tf_op jit(solution)/shard_map/ppermute | solution.py:35
  9.0 32.2 %collective-permute-start.3 = (bf16[512,1024]{1,0:T(8,128)(2,1)S(1)}, bf16[512,1024]{1,0:T(8,128)(2,1)}, u32[]{:S(2)}, u32[]{:S(2)}) collective-permute-start(bf16[512,1024]{1,0:T(8,128)(2,1)S(1)} %get-tuple-element.15.own_ref), channel_id=1, source_target_pairs={{0,3},{1,2},{2,1},{3,0},{4,8},{5,9},{6,10},{7,11},{8,4},{9,5},{10,... | collective-permute-start | bytes 3145736 | tf_op jit(solution)/shard_map/ppermute | solution.py:35
  10.2 0.7 %copy-start.1 = (s32[128]{0:T(128)S(1)}, s32[128]{0:T(128)}, u32[]{:S(2)}) copy-start(s32[128]{0:T(128)} %param.3) | copy-start | bytes 1540
  43.6 6.9 %collective-permute-start.4 = (f32[1,512]{1,0:T(1,128)S(1)}, f32[1,512]{1,0:T(1,128)S(1)}, u32[]{:S(2)}, u32[]{:S(2)}) collective-permute-start(f32[1,512]{1,0:T(1,128)S(1)} %get-tuple-element.23), channel_id=1, source_target_pairs={{1,2},{2,1},{3,4},{4,3},{5,6},{6,5},{7,8},{8,7},{9,10},{10,9},{11,... | collective-permute-start | bytes 6152 | tf_op jit(solution)/shard_map/ppermute | solution.py:35
  49.1 2.5 %collective-permute-start.5 = (f32[1,512]{1,0:T(1,128)S(1)}, f32[1,512]{1,0:T(1,128)S(1)}, u32[]{:S(2)}, u32[]{:S(2)}) collective-permute-start(f32[1,512]{1,0:T(1,128)S(1)} %get-tuple-element.24), channel_id=1, source_target_pairs={{0,1},{1,0},{2,3},{3,2},{4,5},{5,4},{6,7},{7,6},{8,9},{9,8},{10,11... | collective-permute-start | bytes 6152 | tf_op jit(solution)/shard_map/ppermute | solution.py:35

commit v4 on v3

--- a/solution.py
+++ b/solution.py
@@ -26,7 +26,11 @@
 
 def column_neighbour(i, n):
     j = i + 4 if i // 4 % 2 else i - 4
-    return j if 0 <= j < n else i ^ 3
+    return j if 0 <= j < n else None
+
+
+def to_the_ends(i, n):
+    return {4: 0, n - 5: n - 1}.get(i)
 
 
 def swapped(block, partner):
@@ -86,10 +90,13 @@
         high_ref[...] = jnp.maximum(high_ref[...], column_max(products))
 
 
-def mate_kernel(flags_ref, raw_ref, other_ref, unit_ref, to_other_ref, to_mate_ref):
+def mate_kernel(
+    flags_ref, raw_ref, other_ref, column_ref, core_ref,
+    unit_ref, to_other_ref, to_mate_ref, to_core_ref,
+):
     write_units(raw_ref, unit_ref)
-    to_other_ref[...] = jnp.full_like(to_other_ref, LOWEST)
-    to_mate_ref[...] = jnp.full_like(to_mate_ref, LOWEST)
+    for line_ref in (to_other_ref, to_mate_ref, to_core_ref):
+        line_ref[...] = jnp.full_like(line_ref, LOWEST)
 
     @pl.when(flags_ref[2] == 1)
     def _():
@@ -97,26 +104,19 @@
         to_other_ref[...] = row_max(products)
         to_mate_ref[...] = column_max(products)
 
-
-def far_kernel(
-    flags_ref, core_ref, column_ref, other_ref, mate_ref, own_ref, other_in_ref, mate_in_ref, high_in_ref,
-    to_other_ref, to_mate_ref, high_ref,
-):
-    to_other_ref[...] = other_in_ref[...]
-    to_mate_ref[...] = mate_in_ref[...]
-    high_ref[...] = high_in_ref[...]
     for far_ref, slot, near_ref, line_ref in (
         (core_ref, 3, other_ref, to_other_ref),
-        (core_ref, 4, mate_ref, to_mate_ref),
+        (core_ref, 4, unit_ref, to_mate_ref),
         (column_ref, 5, other_ref, to_other_ref),
-        (column_ref, 6, mate_ref, to_mate_ref),
-        (column_ref, 7, own_ref, high_ref),
+        (column_ref, 6, unit_ref, to_mate_ref),
     ):
 
         @pl.when(flags_ref[slot] == 1)
         def _():
             products = products_of(far_ref[...], near_ref[...])
             line_ref[...] = jnp.maximum(line_ref[...], column_max(products))
+            if slot == 3:
+                to_core_ref[...] = row_max(products)
 
 
 def last_kernel(flags_ref, mate_ref, own_ref, high_in_ref, high_ref):
@@ -130,7 +130,7 @@
 
 VMEM = pl.BlockSpec(memory_space=pltpu.VMEM)
 SMEM = pl.BlockSpec(memory_space=pltpu.SMEM)
-PARAMS = pltpu.CompilerParams(vmem_limit_bytes=40 * 1024 * 1024)
+PARAMS = pltpu.CompilerParams(vmem_limit_bytes=16 * 1024 * 1024)
 
 
 def call(kernel, args, outs, scratch=(), flops=0):
@@ -161,9 +161,6 @@
     around = joined(bounds, me - 1, 2)
     before = joined(bounds, me - 4, 3)
     after = joined(bounds, me + 1, 3)
-    edge = jnp.where(me == 0, joined(bounds, 0, 3), 0)
-    last = lax.axis_size(AXES) - 1
-    edge = jnp.where(me == last, joined(bounds, last - 3, 3), edge)
     with_core = jnp.where(second == 1, before, after)
     with_column = jnp.where(second == 1, after, before)
     core_to_mate = jnp.where(second == 1, odd, 1 - odd)
@@ -176,7 +173,6 @@
             with_core * core_to_mate,
             with_column * core_to_mate,
             with_column * (1 - core_to_mate),
-            edge,
         ]
     )
     units = ((block, width), jnp.bfloat16)
@@ -187,19 +183,18 @@
     column = swapped(own, column_neighbour)
     core = swapped(own, core_mate)
     other, high = call(other_kernel, (flags, from_other, own, high), [units, line], flops=tile)
-    mate, to_other, to_mate = call(
-        mate_kernel, (flags, from_mate, other), [units, line, line], flops=tile
-    )
-    to_other, to_mate, high = call(
-        far_kernel,
-        (flags, core, column, other, mate, own, to_other, to_mate, high),
-        [line, line, line],
+    mate, to_other, to_mate, to_core = call(
+        mate_kernel,
+        (flags, from_mate, other, column, core),
+        [units, line, line, line],
         flops=tile,
     )
-    returned = swapped(to_other, other_neighbour), swapped(to_mate, pair_mate)
+    from_other = swapped(to_other, other_neighbour)
+    from_mate = swapped(to_mate, pair_mate)
+    from_core = swapped(to_core, to_the_ends)
     high = call(last_kernel, (flags, mate, own, high), [line], flops=tile)[0]
-    has_other = (me > 0) & (me < last)
-    returned = jnp.maximum(jnp.where(has_other, returned[0], LOWEST), returned[1])
+    at_end = (me == 0) | (me == lax.axis_size(AXES) - 1)
+    returned = jnp.maximum(jnp.where(at_end, from_core, from_other), from_mate)
     return jnp.maximum(high, returned).reshape(block)
 
 

time: 52.5 us -> 50.7 us (0.966)
  the two profiles are of different devices: /device:TPU:1 before, /device:TPU:128 now
where the time goes in v4:
time: 50.7 us; the launch traced here: 50.4 us
  waiting for transfers between devices  21.1 us (42%)
  starting transfers between devices  15.4 us (30%)
  Pallas kernels  8.27 us (16%)
  between operations  3.21 us (6%)
  other arithmetic  1.49 us (3%)
  local copies, waits for them, and re-layouts  0.85 us (2%)
    ppermute x7, waiting for transfers between devices, swapped(): return lax.ppermute(block, AXES, [p for p in pairs if p[1] is not None])  21.1 us
    ppermute x7, starting transfers between devices, swapped(): return lax.ppermute(block, AXES, [p for p in pairs if p[1] is not None])  15.4 us
    pallas_call x4, Pallas kernels, call(): pl.pallas_call(kernel, in_specs=specs, out_specs=[VMEM] * len(outs), out_...  8.27 us
  transfers between devices with their start and end apart: 7, of which 4 were waited for; matrix products, arithmetic and copies ran while one was open for 2% of the time, Pallas kernels for 12%

profile of v4, /device:TPU:128, one launch (start us, length us, event | category | flops | bytes accessed | tf_op | source)
XLA Modules:
  0.0 50.4 jit_solution(5667431003458964303)
XLA Ops:
  0.0 6.1 %collective-permute-start.1 = (bf16[512,1024]{1,0:T(8,128)(2,1)}, bf16[512,1024]{1,0:T(8,128)(2,1)}, u32[]{:S(2)}, u32[]{:S(2)}) collective-permute-start(bf16[512,1024]{1,0:T(8,128)(2,1)} %raw_ref.1), channel_id=1, source_target_pairs={{1,2},{2,1},{3,4},{4,3},{5,6},{6,5},{7,8},{8,7},{9,10},{10,9},{11,... | collective-permute-start | bytes 3145736 | tf_op jit(solution)/shard_map/ppermute | solution.py:39
  6.1 2.3 %shard_map.28 = (bf16[512,1024]{1,0:T(8,128)(2,1)S(1)}, f32[1,512]{1,0:T(1,128)S(1)}) custom-call(bf16[512,1024]{1,0:T(8,128)(2,1)} %raw_ref.1), custom_call_target="tpu_custom_call" | custom-call | flops 536870912 | bytes 1048576 | tf_op jit(solution)/shard_map/pallas_call | solution.py:139
  8.4 0.1 collective-permute-start.3
  8.5 2.8 %collective-permute-start.2 = (bf16[512,1024]{1,0:T(8,128)(2,1)S(1)}, bf16[512,1024]{1,0:T(8,128)(2,1)S(1)}, u32[]{:S(2)}, u32[]{:S(2)}) collective-permute-start(bf16[512,1024]{1,0:T(8,128)(2,1)S(1)} %get-tuple-element.13.own_ref), channel_id=1, source_target_pairs={{4,8},{5,9},{6,10},{7,11},{8,4},{9,5},{10,6},{11,7},{12,16},{13,17... | collective-permute-start | bytes 3145736 | tf_op jit(solution)/shard_map/ppermute | solution.py:39
  11.3 0.5 %collective-permute-start = (bf16[512,1024]{1,0:T(8,128)(2,1)}, bf16[512,1024]{1,0:T(8,128)(2,1)}, u32[]{:S(2)}, u32[]{:S(2)}) collective-permute-start(bf16[512,1024]{1,0:T(8,128)(2,1)} %raw_ref.1), channel_id=1, source_target_pairs={{0,1},{1,0},{2,3},{3,2},{4,5},{5,4},{6,7},{7,6},{8,9},{9,8},{10,11... | collective-permute-start | bytes 3145736 | tf_op jit(solution)/shard_map/ppermute | solution.py:39
  11.8 0.7 %copy-done = s32[128]{0:T(128)S(1)} copy-done((s32[128]{0:T(128)S(1)}, s32[128]{0:T(128)}, u32[]{:S(2)}) %copy-start) | copy-done | bytes 536
  12.5 0.1 copy.3
  12.6 0.2 reduce-window.9
  12.8 0.7 %convert_reduce_fusion = (s32[]{:T(128)}, s32[]{:T(128)}, s32[]{:T(128)}, s32[]{:T(128)}, s32[]{:T(128)}) fusion(s32[128,1]{1,0:T(8,128)S(1)} %reduce-window.9, s32[]{:T(128)S(6)} %add.35, s32[]{:T(128)S(6)} %add.33, s32[]{:T(128)S(6)} %add.31, s32[]{:T(128)S(6)} %sub.18, s32[]{:T(128)S(6)} %sub.20), kind=kLoop, calls=%fused_computation | loop fusion | flops 2939 | bytes 552 | tf_op jit(solution)/shard_map/reduce_sum | solution.py:44
  16.6 0.1 stack.35.flags_ref
  16.7 5.3 %collective-permute-done.1.raw_ref = bf16[512,1024]{1,0:T(8,128)(2,1)} collective-permute-done((bf16[512,1024]{1,0:T(8,128)(2,1)}, bf16[512,1024]{1,0:T(8,128)(2,1)}, u32[]{:S(2)}, u32[]{:S(2)}) %collective-permute-start.1) | collective-permute-done | bytes 1048608 | tf_op jit(solution)/shard_map/ppermute | solution.py:39
  22.0 2.3 %shard_map.29 = (bf16[512,1024]{1,0:T(8,128)(2,1)S(1)}, f32[1,512]{1,0:T(1,128)S(1)}) custom-call(s32[7]{0:T(128)S(1)} %stack.35.flags_ref, bf16[512,1024]{1,0:T(8,128)(2,1)} %collective-permute-done.1.raw_ref, bf16[512,1024]{1,0:T(8,128)(2,1)S(1)} %get-tuple-element.13.own_ref, f32[1,512]{1,0:T(1,128)S(1)} %get-tuple-element.14.high_in_ref), custom_call_target="tpu_custom_call" | custom-call | flops 536870912 | bytes 2099228 | tf_op jit(solution)/shard_map/pallas_call | solution.py:139
  24.3 0.0 collective-permute-done.3.core_ref
  24.3 5.6 %collective-permute-done.2.column_ref = bf16[512,1024]{1,0:T(8,128)(2,1)S(1)} collective-permute-done((bf16[512,1024]{1,0:T(8,128)(2,1)S(1)}, bf16[512,1024]{1,0:T(8,128)(2,1)S(1)}, u32[]{:S(2)}, u32[]{:S(2)}) %collective-permute-start.2) | collective-permute-done | bytes 1048608 | tf_op jit(solution)/shard_map/ppermute | solution.py:39
  29.8 6.5 %collective-permute-done.raw_ref = bf16[512,1024]{1,0:T(8,128)(2,1)} collective-permute-done((bf16[512,1024]{1,0:T(8,128)(2,1)}, bf16[512,1024]{1,0:T(8,128)(2,1)}, u32[]{:S(2)}, u32[]{:S(2)}) %collective-permute-start) | collective-permute-done | bytes 1048608 | tf_op jit(solution)/shard_map/ppermute | solution.py:39
  36.4 2.4 %shard_map.30 = (bf16[512,1024]{1,0:T(8,128)(2,1)S(1)}, f32[1,512]{1,0:T(1,128)S(1)}, f32[1,512]{1,0:T(1,128)S(1)}, f32[1,512]{1,0:T(1,128)S(1)}) custom-call(s32[7]{0:T(128)S(1)} %stack.35.flags_ref, bf16[512,1024]{1,0:T(8,128)(2,1)} %collective-permute-done.raw_ref, bf16[512,1024]{1,0:T(8,128)(2,1)S(1)} %get-tuple-element.15.other_ref, ...), custom_call_target="tpu_custom_call" | custom-call | flops 536870912 | bytes 4194332 | tf_op jit(solution)/shard_map/pallas_call | solution.py:139
  38.8 0.7 %collective-permute-start.4 = (f32[1,512]{1,0:T(1,128)S(1)}, f32[1,512]{1,0:T(1,128)S(1)}, u32[]{:S(2)}, u32[]{:S(2)}) collective-permute-start(f32[1,512]{1,0:T(1,128)S(1)} %get-tuple-element.18), channel_id=1, source_target_pairs={{4,0},{251,255}} | collective-permute-start | bytes 6152 | tf_op jit(solution)/shard_map/ppermute | solution.py:39
  39.4 5.1 %collective-permute-start.5 = (f32[1,512]{1,0:T(1,128)S(1)}, f32[1,512]{1,0:T(1,128)S(1)}, u32[]{:S(2)}, u32[]{:S(2)}) collective-permute-start(f32[1,512]{1,0:T(1,128)S(1)} %get-tuple-element.19), channel_id=1, source_target_pairs={{1,2},{2,1},{3,4},{4,3},{5,6},{6,5},{7,8},{8,7},{9,10},{10,9},{11,... | collective-permute-start | bytes 6152 | tf_op jit(solution)/shard_map/ppermute | solution.py:39
  44.6 0.1 collective-permute-start.6
  44.7 1.3 %shard_map.31 = f32[1,512]{1,0:T(1,128)S(1)} custom-call(s32[7]{0:T(128)S(1)} %stack.35.flags_ref, bf16[512,1024]{1,0:T(8,128)(2,1)S(1)} %get-tuple-element.16.mate_ref, bf16[512,1024]{1,0:T(8,128)(2,1)S(1)} %get-tuple-element.13.own_ref, f32[1,512]{1,0:T(1,128)S(1)} %get-tuple-element.17.high_in_ref), custom_call_target="tpu_custom_call" | custom-call | flops 536870912 | bytes 2099228 | tf_op jit(solution)/shard_map/pallas_call | solution.py:139
  46.0 0.0 collective-permute-done.4
  46.0 3.8 %collective-permute-done.5 = f32[1,512]{1,0:T(1,128)S(1)} collective-permute-done((f32[1,512]{1,0:T(1,128)S(1)}, f32[1,512]{1,0:T(1,128)S(1)}, u32[]{:S(2)}, u32[]{:S(2)}) %collective-permute-start.5) | collective-permute-done | bytes 2080 | tf_op jit(solution)/shard_map/ppermute | solution.py:39
  49.8 0.0 collective-permute-done.6
  49.8 0.6 %fusion.1 = f32[1,512]{1,0:T(1,128)} fusion(f32[1,512]{1,0:T(1,128)S(1)} %shard_map.31, f32[1,512]{1,0:T(1,128)S(1)} %collective-permute-done.6, f32[1,512]{1,0:T(1,128)S(1)} %collective-permute-done.4, f32[1,512]{1,0:T(1,128)S(1)} %collective-permute-done.5, pred[]{:T(512)S(6)} %or.3), kind=kLoop, calls=%fused_computation.9 | loop fusion | flops 1536 | bytes 10241 | tf_op jit(solution)/shard_map/max | solution.py:198
  (1 shorter events, 0.0 us)
Async XLA Ops:
  0.0 22.0 %collective-permute-start.1 = (bf16[512,1024]{1,0:T(8,128)(2,1)}, bf16[512,1024]{1,0:T(8,128)(2,1)}, u32[]{:S(2)}, u32[]{:S(2)}) collective-permute-start(bf16[512,1024]{1,0:T(8,128)(2,1)} %raw_ref.1), channel_id=1, source_target_pairs={{1,2},{2,1},{3,4},{4,3},{5,6},{6,5},{7,8},{8,7},{9,10},{10,9},{11,... | collective-permute-start | bytes 3145736 | tf_op jit(solution)/shard_map/ppermute | solution.py:39
  8.4 15.9 %collective-permute-start.3 = (bf16[512,1024]{1,0:T(8,128)(2,1)S(1)}, bf16[512,1024]{1,0:T(8,128)(2,1)S(1)}, u32[]{:S(2)}, u32[]{:S(2)}) collective-permute-start(bf16[512,1024]{1,0:T(8,128)(2,1)S(1)} %get-tuple-element.13.own_ref), channel_id=1, source_target_pairs={{0,4},{1,5},{2,6},{3,7},{4,0},{5,1},{6,2},{7,3},{8,12},{9,13},{10,... | collective-permute-start | bytes 3145736 | tf_op jit(solution)/shard_map/ppermute | solution.py:39
  8.5 21.4 %collective-permute-start.2 = (bf16[512,1024]{1,0:T(8,128)(2,1)S(1)}, bf16[512,1024]{1,0:T(8,128)(2,1)S(1)}, u32[]{:S(2)}, u32[]{:S(2)}) collective-permute-start(bf16[512,1024]{1,0:T(8,128)(2,1)S(1)} %get-tuple-element.13.own_ref), channel_id=1, source_target_pairs={{4,8},{5,9},{6,10},{7,11},{8,4},{9,5},{10,6},{11,7},{12,16},{13,17... | collective-permute-start | bytes 3145736 | tf_op jit(solution)/shard_map/ppermute | solution.py:39
  11.3 25.1 %collective-permute-start = (bf16[512,1024]{1,0:T(8,128)(2,1)}, bf16[512,1024]{1,0:T(8,128)(2,1)}, u32[]{:S(2)}, u32[]{:S(2)}) collective-permute-start(bf16[512,1024]{1,0:T(8,128)(2,1)} %raw_ref.1), channel_id=1, source_target_pairs={{0,1},{1,0},{2,3},{3,2},{4,5},{5,4},{6,7},{7,6},{8,9},{9,8},{10,11... | collective-permute-start | bytes 3145736 | tf_op jit(solution)/shard_map/ppermute | solution.py:39
  11.8 0.7 %copy-start = (s32[128]{0:T(128)S(1)}, s32[128]{0:T(128)}, u32[]{:S(2)}) copy-start(s32[128]{0:T(128)} %param.3) | copy-start | bytes 1540
  38.8 7.2 %collective-permute-start.4 = (f32[1,512]{1,0:T(1,128)S(1)}, f32[1,512]{1,0:T(1,128)S(1)}, u32[]{:S(2)}, u32[]{:S(2)}) collective-permute-start(f32[1,512]{1,0:T(1,128)S(1)} %get-tuple-element.18), channel_id=1, source_target_pairs={{4,0},{251,255}} | collective-permute-start | bytes 6152 | tf_op jit(solution)/shard_map/ppermute | solution.py:39
  39.4 10.3 %collective-permute-start.5 = (f32[1,512]{1,0:T(1,128)S(1)}, f32[1,512]{1,0:T(1,128)S(1)}, u32[]{:S(2)}, u32[]{:S(2)}) collective-permute-start(f32[1,512]{1,0:T(1,128)S(1)} %get-tuple-element.19), channel_id=1, source_target_pairs={{1,2},{2,1},{3,4},{4,3},{5,6},{6,5},{7,8},{8,7},{9,10},{10,9},{11,... | collective-permute-start | bytes 6152 | tf_op jit(solution)/shard_map/ppermute | solution.py:39
  44.6 5.2 %collective-permute-start.6 = (f32[1,512]{1,0:T(1,128)S(1)}, f32[1,512]{1,0:T(1,128)S(1)}, u32[]{:S(2)}, u32[]{:S(2)}) collective-permute-start(f32[1,512]{1,0:T(1,128)S(1)} %get-tuple-element.20), channel_id=1, source_target_pairs={{0,1},{1,0},{2,3},{3,2},{4,5},{5,4},{6,7},{7,6},{8,9},{9,8},{10,11... | collective-permute-start | bytes 6152 | tf_op jit(solution)/shard_map/ppermute | solution.py:39

commit v5 on v3

--- a/solution.py
+++ b/solution.py
@@ -16,8 +16,7 @@
 
 
 def other_neighbour(i, n):
-    j = i + 1 if i % 2 else i - 1
-    return j if 0 <= j < n else None
+    return (i + 1) % n if i % 2 else (i - 1) % n
 
 
 def core_mate(i, n):
@@ -25,8 +24,7 @@
 
 
 def column_neighbour(i, n):
-    j = i + 4 if i // 4 % 2 else i - 4
-    return j if 0 <= j < n else i ^ 3
+    return (i + 4) % n if i // 4 % 2 else (i - 4) % n
 
 
 def swapped(block, partner):
@@ -36,10 +34,11 @@
 
 
 def joined(bounds, lower, distance):
+    n = lax.axis_size(AXES)
+    lower = lax.rem(lower + n, n)
     upper = lower + distance
     crossing = jnp.sum(((bounds > lower) & (bounds <= upper)).astype(jnp.int32))
-    inside = (lower >= 0) & (upper < lax.axis_size(AXES))
-    return (inside & (crossing == 0)).astype(jnp.int32)
+    return ((upper < n) & (crossing == 0)).astype(jnp.int32)
 
 
 def write_units(raw_ref, unit_ref):
@@ -99,18 +98,16 @@
 
 
 def far_kernel(
-    flags_ref, core_ref, column_ref, other_ref, mate_ref, own_ref, other_in_ref, mate_in_ref, high_in_ref,
-    to_other_ref, to_mate_ref, high_ref,
+    flags_ref, core_ref, column_ref, other_ref, mate_ref, other_in_ref, mate_in_ref,
+    to_other_ref, to_mate_ref,
 ):
     to_other_ref[...] = other_in_ref[...]
     to_mate_ref[...] = mate_in_ref[...]
-    high_ref[...] = high_in_ref[...]
     for far_ref, slot, near_ref, line_ref in (
         (core_ref, 3, other_ref, to_other_ref),
         (core_ref, 4, mate_ref, to_mate_ref),
         (column_ref, 5, other_ref, to_other_ref),
         (column_ref, 6, mate_ref, to_mate_ref),
-        (column_ref, 7, own_ref, high_ref),
     ):
 
         @pl.when(flags_ref[slot] == 1)
@@ -130,7 +127,7 @@
 
 VMEM = pl.BlockSpec(memory_space=pltpu.VMEM)
 SMEM = pl.BlockSpec(memory_space=pltpu.SMEM)
-PARAMS = pltpu.CompilerParams(vmem_limit_bytes=40 * 1024 * 1024)
+PARAMS = pltpu.CompilerParams(vmem_limit_bytes=16 * 1024 * 1024)
 
 
 def call(kernel, args, outs, scratch=(), flops=0):
@@ -161,9 +158,6 @@
     around = joined(bounds, me - 1, 2)
     before = joined(bounds, me - 4, 3)
     after = joined(bounds, me + 1, 3)
-    edge = jnp.where(me == 0, joined(bounds, 0, 3), 0)
-    last = lax.axis_size(AXES) - 1
-    edge = jnp.where(me == last, joined(bounds, last - 3, 3), edge)
     with_core = jnp.where(second == 1, before, after)
     with_column = jnp.where(second == 1, after, before)
     core_to_mate = jnp.where(second == 1, odd, 1 - odd)
@@ -176,7 +170,6 @@
             with_core * core_to_mate,
             with_column * core_to_mate,
             with_column * (1 - core_to_mate),
-            edge,
         ]
     )
     units = ((block, width), jnp.bfloat16)
@@ -190,16 +183,15 @@
     mate, to_other, to_mate = call(
         mate_kernel, (flags, from_mate, other), [units, line, line], flops=tile
     )
-    to_other, to_mate, high = call(
+    to_other, to_mate = call(
         far_kernel,
-        (flags, core, column, other, mate, own, to_other, to_mate, high),
-        [line, line, line],
+        (flags, core, column, other, mate, to_other, to_mate),
+        [line, line],
         flops=tile,
     )
     returned = swapped(to_other, other_neighbour), swapped(to_mate, pair_mate)
     high = call(last_kernel, (flags, mate, own, high), [line], flops=tile)[0]
-    has_other = (me > 0) & (me < last)
-    returned = jnp.maximum(jnp.where(has_other, returned[0], LOWEST), returned[1])
+    returned = jnp.maximum(*returned)
     return jnp.maximum(high, returned).reshape(block)
 
 

time: 52.5 us -> 41.9 us (0.80)
  the two profiles are of different devices: /device:TPU:1 before, /device:TPU:0 now
where the time goes in v5:
time: 41.9 us; the launch traced here: 41.7 us
  waiting for transfers between devices  16.2 us (39%)
  starting transfers between devices  12.6 us (30%)
  Pallas kernels  6.01 us (14%)
  between operations  3.19 us (8%)
  local copies, waits for them, and re-layouts  2.14 us (5%)
  other arithmetic  1.52 us (4%)
    ppermute x6, waiting for transfers between devices, swapped(): return lax.ppermute(block, AXES, [p for p in pairs if p[1] is not None])  16.2 us
    ppermute x6, starting transfers between devices, swapped(): return lax.ppermute(block, AXES, [p for p in pairs if p[1] is not None])  12.6 us
    pallas_call x5, Pallas kernels, call(): pl.pallas_call(kernel, in_specs=specs, out_specs=[VMEM] * len(outs), out_...  6.01 us
    unnamed x4, local copies, waits for them, and re-layouts  1.94 us
  transfers between devices with their start and end apart: 6, of which 4 were waited for; matrix products, arithmetic and copies ran while one was open for 3% of the time, Pallas kernels for 13%

profile of v5, /device:TPU:0, one launch (start us, length us, event | category | flops | bytes accessed | tf_op | source)
XLA Modules:
  0.0 41.7 jit_solution(10486114929033350996)
XLA Ops:
  0.0 8.2 %collective-permute-start.1 = (bf16[512,1024]{1,0:T(8,128)(2,1)}, bf16[512,1024]{1,0:T(8,128)(2,1)}, u32[]{:S(2)}, u32[]{:S(2)}) collective-permute-start(bf16[512,1024]{1,0:T(8,128)(2,1)} %raw_ref.1), channel_id=1, source_target_pairs={{0,255},{1,2},{2,1},{3,4},{4,3},{5,6},{6,5},{7,8},{8,7},{9,10},{10... | collective-permute-start | bytes 3145736 | tf_op jit(solution)/shard_map/ppermute | solution.py:33
  8.2 0.0 collective-permute-start
  8.2 1.3 %copy-done = bf16[512,1024]{1,0:T(8,128)(2,1)S(1)} copy-done((bf16[512,1024]{1,0:T(8,128)(2,1)S(1)}, bf16[512,1024]{1,0:T(8,128)(2,1)}, u32[]{:S(2)}) %copy-start) | copy-done | bytes 1048600
  9.5 1.0 %shard_map.28 = (bf16[512,1024]{1,0:T(8,128)(2,1)S(1)}, f32[1,512]{1,0:T(1,128)S(1)}) custom-call(bf16[512,1024]{1,0:T(8,128)(2,1)S(1)} %copy-done), custom_call_target="tpu_custom_call" | custom-call | flops 536870912 | bytes 1048576 | tf_op jit(solution)/shard_map/pallas_call | solution.py:136
  10.5 0.1 collective-permute-start.2
  10.6 1.3 %collective-permute-start.3 = (bf16[512,1024]{1,0:T(8,128)(2,1)S(1)}, bf16[512,1024]{1,0:T(8,128)(2,1)S(1)}, u32[]{:S(2)}, u32[]{:S(2)}) collective-permute-start(bf16[512,1024]{1,0:T(8,128)(2,1)S(1)} %get-tuple-element.14.own_ref), channel_id=1, source_target_pairs={{0,252},{1,253},{2,254},{3,255},{4,8},{5,9},{6,10},{7,11},{8,4},{9... | collective-permute-start | bytes 3145736 | tf_op jit(solution)/shard_map/ppermute | solution.py:33
  12.0 0.7 %copy-done.1 = s32[128]{0:T(128)S(1)} copy-done((s32[128]{0:T(128)S(1)}, s32[128]{0:T(128)}, u32[]{:S(2)}) %copy-start.1) | copy-done | bytes 536
  12.6 0.1 copy.3
  12.7 0.2 reduce-window.9
  12.9 0.8 %convert_reduce_fusion = (s32[]{:T(128)}, s32[]{:T(128)}, s32[]{:T(128)}, s32[]{:T(128)}, s32[]{:T(128)}) fusion(s32[128,1]{1,0:T(8,128)S(1)} %reduce-window.9, s32[]{:T(128)S(6)} %add.59, s32[]{:T(128)S(6)} %rem.126, s32[]{:T(128)S(6)} %add.54, s32[]{:T(128)S(6)} %rem.105, s32[]{:T(128)S(6)} %add.53, s32[]{:T(128)S(6)} %add.51, s32[]{:T(128)S(6)} %rem.99, ...), kind=kLoop, calls=%fused_computation | loop fusion | flops 3067 | bytes 568 | tf_op jit(solution)/shard_map/reduce_sum | solution.py:40
  16.8 0.1 stack.35.flags_ref
  16.9 4.2 %collective-permute-done.1.raw_ref = bf16[512,1024]{1,0:T(8,128)(2,1)} collective-permute-done((bf16[512,1024]{1,0:T(8,128)(2,1)}, bf16[512,1024]{1,0:T(8,128)(2,1)}, u32[]{:S(2)}, u32[]{:S(2)}) %collective-permute-start.1) | collective-permute-done | bytes 1048608 | tf_op jit(solution)/shard_map/ppermute | solution.py:33
  21.1 1.6 %shard_map.29 = (bf16[512,1024]{1,0:T(8,128)(2,1)S(1)}, f32[1,512]{1,0:T(1,128)S(1)}) custom-call(s32[7]{0:T(128)S(1)} %stack.35.flags_ref, bf16[512,1024]{1,0:T(8,128)(2,1)} %collective-permute-done.1.raw_ref, bf16[512,1024]{1,0:T(8,128)(2,1)S(1)} %get-tuple-element.14.own_ref, f32[1,512]{1,0:T(1,128)S(1)} %get-tuple-element.15.high_in_ref), custom_call_target="tpu_custom_call" | custom-call | flops 536870912 | bytes 2099228 | tf_op jit(solution)/shard_map/pallas_call | solution.py:136
  22.7 4.1 %collective-permute-done.raw_ref = bf16[512,1024]{1,0:T(8,128)(2,1)} collective-permute-done((bf16[512,1024]{1,0:T(8,128)(2,1)}, bf16[512,1024]{1,0:T(8,128)(2,1)}, u32[]{:S(2)}, u32[]{:S(2)}) %collective-permute-start) | collective-permute-done | bytes 1048608 | tf_op jit(solution)/shard_map/ppermute | solution.py:33
  26.8 1.6 %shard_map.30 = (bf16[512,1024]{1,0:T(8,128)(2,1)S(1)}, f32[1,512]{1,0:T(1,128)S(1)}, f32[1,512]{1,0:T(1,128)S(1)}) custom-call(s32[7]{0:T(128)S(1)} %stack.35.flags_ref, bf16[512,1024]{1,0:T(8,128)(2,1)} %collective-permute-done.raw_ref, bf16[512,1024]{1,0:T(8,128)(2,1)S(1)} %get-tuple-element.16.other_ref), custom_call_target="tpu_custom_call" | custom-call | flops 536870912 | bytes 2097180 | tf_op jit(solution)/shard_map/pallas_call | solution.py:136
  28.3 0.0 collective-permute-done.2.core_ref
  28.3 3.6 %collective-permute-done.3.column_ref = bf16[512,1024]{1,0:T(8,128)(2,1)S(1)} collective-permute-done((bf16[512,1024]{1,0:T(8,128)(2,1)S(1)}, bf16[512,1024]{1,0:T(8,128)(2,1)S(1)}, u32[]{:S(2)}, u32[]{:S(2)}) %collective-permute-start.3) | collective-permute-done | bytes 1048608 | tf_op jit(solution)/shard_map/ppermute | solution.py:33
  32.0 0.6 %shard_map.32 = (f32[1,512]{1,0:T(1,128)S(1)}, f32[1,512]{1,0:T(1,128)S(1)}) custom-call(s32[7]{0:T(128)S(1)} %stack.35.flags_ref, bf16[512,1024]{1,0:T(8,128)(2,1)S(1)} %collective-permute-done.2.core_ref, bf16[512,1024]{1,0:T(8,128)(2,1)S(1)} %collective-permute-done.3.column_ref, bf16[512,1024]{1,0:T(8,128)(2,1)S(1)} %get-tuple-element.16.other_ref, ...), custom_call_target="tpu_custom_call" | custom-call | flops 536870912 | bytes 4198428 | tf_op jit(solution)/shard_map/pallas_call | solution.py:136
  32.5 3.0 %collective-permute-start.4 = (f32[1,512]{1,0:T(1,128)S(1)}, f32[1,512]{1,0:T(1,128)S(1)}, u32[]{:S(2)}, u32[]{:S(2)}) collective-permute-start(f32[1,512]{1,0:T(1,128)S(1)} %get-tuple-element.21), channel_id=1, source_target_pairs={{0,255},{1,2},{2,1},{3,4},{4,3},{5,6},{6,5},{7,8},{8,7},{9,10},{10... | collective-permute-start | bytes 6152 | tf_op jit(solution)/shard_map/ppermute | solution.py:33
  35.6 0.0 collective-permute-start.5
  35.6 1.3 %shard_map.31 = f32[1,512]{1,0:T(1,128)S(1)} custom-call(s32[7]{0:T(128)S(1)} %stack.35.flags_ref, bf16[512,1024]{1,0:T(8,128)(2,1)S(1)} %get-tuple-element.17.mate_ref, bf16[512,1024]{1,0:T(8,128)(2,1)S(1)} %get-tuple-element.14.own_ref, f32[1,512]{1,0:T(1,128)S(1)} %get-tuple-element.18.high_in_ref), custom_call_target="tpu_custom_call" | custom-call | flops 536870912 | bytes 2099228 | tf_op jit(solution)/shard_map/pallas_call | solution.py:136
  36.9 4.2 %collective-permute-done.4 = f32[1,512]{1,0:T(1,128)S(1)} collective-permute-done((f32[1,512]{1,0:T(1,128)S(1)}, f32[1,512]{1,0:T(1,128)S(1)}, u32[]{:S(2)}, u32[]{:S(2)}) %collective-permute-start.4) | collective-permute-done | bytes 2080 | tf_op jit(solution)/shard_map/ppermute | solution.py:33
  41.1 0.0 collective-permute-done.5
  41.1 0.6 %maximum_maximum_fusion = f32[1,512]{1,0:T(1,128)} fusion(f32[1,512]{1,0:T(1,128)S(1)} %shard_map.31, f32[1,512]{1,0:T(1,128)S(1)} %collective-permute-done.4, f32[1,512]{1,0:T(1,128)S(1)} %collective-permute-done.5), kind=kLoop, calls=%fused_computation.6 | loop fusion | flops 1024 | bytes 8192 | tf_op jit(solution)/shard_map/max | solution.py:195
  (2 shorter events, 0.0 us)
Async XLA Ops:
  0.0 21.1 %collective-permute-start.1 = (bf16[512,1024]{1,0:T(8,128)(2,1)}, bf16[512,1024]{1,0:T(8,128)(2,1)}, u32[]{:S(2)}, u32[]{:S(2)}) collective-permute-start(bf16[512,1024]{1,0:T(8,128)(2,1)} %raw_ref.1), channel_id=1, source_target_pairs={{0,255},{1,2},{2,1},{3,4},{4,3},{5,6},{6,5},{7,8},{8,7},{9,10},{10... | collective-permute-start | bytes 3145736 | tf_op jit(solution)/shard_map/ppermute | solution.py:33
  8.2 18.6 %collective-permute-start = (bf16[512,1024]{1,0:T(8,128)(2,1)}, bf16[512,1024]{1,0:T(8,128)(2,1)}, u32[]{:S(2)}, u32[]{:S(2)}) collective-permute-start(bf16[512,1024]{1,0:T(8,128)(2,1)} %raw_ref.1), channel_id=1, source_target_pairs={{0,1},{1,0},{2,3},{3,2},{4,5},{5,4},{6,7},{7,6},{8,9},{9,8},{10,11... | collective-permute-start | bytes 3145736 | tf_op jit(solution)/shard_map/ppermute | solution.py:33
  8.2 1.3 %copy-start = (bf16[512,1024]{1,0:T(8,128)(2,1)S(1)}, bf16[512,1024]{1,0:T(8,128)(2,1)}, u32[]{:S(2)}) copy-start(bf16[512,1024]{1,0:T(8,128)(2,1)} %raw_ref.1) | copy-start | bytes 3145732
  10.5 17.8 %collective-permute-start.2 = (bf16[512,1024]{1,0:T(8,128)(2,1)S(1)}, bf16[512,1024]{1,0:T(8,128)(2,1)S(1)}, u32[]{:S(2)}, u32[]{:S(2)}) collective-permute-start(bf16[512,1024]{1,0:T(8,128)(2,1)S(1)} %get-tuple-element.14.own_ref), channel_id=1, source_target_pairs={{0,4},{1,5},{2,6},{3,7},{4,0},{5,1},{6,2},{7,3},{8,12},{9,13},{10,... | collective-permute-start | bytes 3145736 | tf_op jit(solution)/shard_map/ppermute | solution.py:33
  10.6 21.3 %collective-permute-start.3 = (bf16[512,1024]{1,0:T(8,128)(2,1)S(1)}, bf16[512,1024]{1,0:T(8,128)(2,1)S(1)}, u32[]{:S(2)}, u32[]{:S(2)}) collective-permute-start(bf16[512,1024]{1,0:T(8,128)(2,1)S(1)} %get-tuple-element.14.own_ref), channel_id=1, source_target_pairs={{0,252},{1,253},{2,254},{3,255},{4,8},{5,9},{6,10},{7,11},{8,4},{9... | collective-permute-start | bytes 3145736 | tf_op jit(solution)/shard_map/ppermute | solution.py:33
  12.0 0.7 %copy-start.1 = (s32[128]{0:T(128)S(1)}, s32[128]{0:T(128)}, u32[]{:S(2)}) copy-start(s32[128]{0:T(128)} %param.3) | copy-start | bytes 1540
  32.5 8.5 %collective-permute-start.4 = (f32[1,512]{1,0:T(1,128)S(1)}, f32[1,512]{1,0:T(1,128)S(1)}, u32[]{:S(2)}, u32[]{:S(2)}) collective-permute-start(f32[1,512]{1,0:T(1,128)S(1)} %get-tuple-element.21), channel_id=1, source_target_pairs={{0,255},{1,2},{2,1},{3,4},{4,3},{5,6},{6,5},{7,8},{8,7},{9,10},{10... | collective-permute-start | bytes 6152 | tf_op jit(solution)/shard_map/ppermute | solution.py:33
  35.6 5.5 %collective-permute-start.5 = (f32[1,512]{1,0:T(1,128)S(1)}, f32[1,512]{1,0:T(1,128)S(1)}, u32[]{:S(2)}, u32[]{:S(2)}) collective-permute-start(f32[1,512]{1,0:T(1,128)S(1)} %get-tuple-element.22), channel_id=1, source_target_pairs={{0,1},{1,0},{2,3},{3,2},{4,5},{5,4},{6,7},{7,6},{8,9},{9,8},{10,11... | collective-permute-start | bytes 6152 | tf_op jit(solution)/shard_map/ppermute | solution.py:33

commit v6 on v5

v6 whole, which is shorter than its diff:
```python
import jax
import jax.numpy as jnp
from jax import lax
from jax.experimental import pallas as pl
from jax.experimental.pallas import tpu as pltpu
from jax.sharding import PartitionSpec as P

EPSILON = 1e-06
AXES = ("rows", "bal")
LOWEST = -2.0
STRIP = 64
FETCHES = 4


def pair_mate(i, n):
    return i ^ 1


def other_neighbour(i, n):
    return (i + 1) % n if i % 2 else (i - 1) % n


def core_mate(i, n):
    return i ^ 4


def column_neighbour(i, n):
    j = i + 4 if i // 4 % 2 else i - 4
    return j if 0 <= j < n else None


def to_the_ends(i, n):
    return {4: 0, n - 5: n - 1}.get(i)


def swapped(block, partner):
    n = lax.axis_size(AXES)
    pairs = [(i, partner(i, n)) for i in range(n)]
    return lax.ppermute(block, AXES, [p for p in pairs if p[1] is not None])


def joined(bounds, lower, distance):
    upper = lower + distance
    crossing = jnp.sum(((bounds > lower) & (bounds <= upper)).astype(jnp.int32))
    inside = (lower >= 0) & (upper < lax.axis_size(AXES))
    return (inside & (crossing == 0)).astype(jnp.int32)


def write_units(raw_ref, unit_ref):
    for start in range(0, raw_ref.shape[0], STRIP):
        rows = pl.ds(start, STRIP)
        values = raw_ref[rows, :].astype(jnp.float32)
        scale = lax.rsqrt(jnp.sum(values * values, axis=1, keepdims=True) + EPSILON)
        unit_ref[rows, :] = (values * scale).astype(jnp.bfloat16)


def fetch_units(raw_ref, stage_ref, sems, unit_ref):
    rows = stage_ref.shape[0] // FETCHES
    copies = [
        pltpu.make_async_copy(
            raw_ref.at[pl.ds(i * rows, rows)], stage_ref.at[pl.ds(i * rows, rows)], sems.at[i]
        )
        for i in range(FETCHES)
    ]
    for copy in copies:
        copy.start()
    for i, copy in enumerate(copies):
        copy.wait()
        part = pl.ds(i * rows, rows)
        write_units(stage_ref.at[part], unit_ref.at[part])


def products_of(left, right):
    return lax.dot_general(
        left, right, (((1,), (1,)), ((), ())), preferred_element_type=jnp.float32
    )


def column_max(products):
    return jnp.max(products, axis=0, keepdims=True)


def row_max(products):
    width = products.shape[1]
    folded = products[:, :128]
    for start in range(128, width, 128):
        folded = jnp.maximum(folded, products[:, start : start + 128])
    return jnp.max(folded.T, axis=0, keepdims=True)


def own_kernel(raw_ref, unit_ref, high_ref, stage_ref, sems):
    fetch_units(raw_ref, stage_ref, sems, unit_ref)
    products = products_of(unit_ref[...], unit_ref[...])
    row = lax.broadcasted_iota(jnp.int32, products.shape, 0)
    col = lax.broadcasted_iota(jnp.int32, products.shape, 1)
    high_ref[...] = column_max(jnp.where(row == col, LOWEST, products))


def near_kernel(flags_ref, raw_ref, own_ref, high_in_ref, unit_ref, high_ref):
    write_units(raw_ref, unit_ref)
    high_ref[...] = high_in_ref[...]

    @pl.when(flags_ref[0, 0] == 1)
    def _():
        products = products_of(unit_ref[...], own_ref[...])
        high_ref[...] = jnp.maximum(high_ref[...], column_max(products))


def between_kernel(flags_ref, raw_ref, mate_ref, unit_ref, to_other_ref, to_mate_ref):
    write_units(raw_ref, unit_ref)
    to_other_ref[...] = jnp.full_like(to_other_ref, LOWEST)
    to_mate_ref[...] = jnp.full_like(to_mate_ref, LOWEST)

    @pl.when(flags_ref[0, 2] == 1)
    def _():
        products = products_of(mate_ref[...], unit_ref[...])
        to_mate_ref[...] = row_max(products)
        to_other_ref[...] = column_max(products)


def far_kernel(
    flags_ref, core_ref, column_ref, other_ref, mate_ref, other_in_ref, mate_in_ref,
    to_other_ref, to_mate_ref, to_core_ref, stage_ref, sems,
):
    to_other_ref[...] = other_in_ref[...]
    to_mate_ref[...] = mate_in_ref[...]
    to_core_ref[...] = jnp.full_like(to_core_ref, LOWEST)
    for i, (far_ref, slot) in enumerate(((core_ref, 3), (column_ref, 5))):

        @pl.when(flags_ref[0, slot] + flags_ref[0, slot + 1] > 0)
        def _():
            pltpu.make_async_copy(far_ref, stage_ref.at[i], sems.at[i]).start()

    for i, (far_ref, slot) in enumerate(((core_ref, 3), (column_ref, 5))):

        @pl.when(flags_ref[0, slot] + flags_ref[0, slot + 1] > 0)
        def _():
            pltpu.make_async_copy(far_ref, stage_ref.at[i], sems.at[i]).wait()

        for near_ref, line_ref, flag in (
            (other_ref, to_other_ref, flags_ref[0, slot]),
            (mate_ref, to_mate_ref, flags_ref[0, slot + 1]),
        ):

            @pl.when(flag == 1)
            def _():
                products = products_of(stage_ref[i], near_ref[...])
                line_ref[...] = jnp.maximum(line_ref[...], column_max(products))
                if far_ref is core_ref and near_ref is other_ref:
                    to_core_ref[...] = row_max(products)


def last_kernel(flags_ref, other_ref, own_ref, high_in_ref, high_ref):
    high_ref[...] = high_in_ref[...]

    @pl.when(flags_ref[0, 1] == 1)
    def _():
        products = products_of(other_ref[...], own_ref[...])
        high_ref[...] = jnp.maximum(high_ref[...], column_max(products))


VMEM = pl.BlockSpec(memory_space=pltpu.VMEM)
PARAMS = pltpu.CompilerParams(vmem_limit_bytes=16 * 1024 * 1024)


def call(kernel, args, outs, scratch=(), flops=0, aliases=None, in_hbm=()):
    specs = [VMEM] * len(args)
    for i in in_hbm:
        specs[i] = pl.BlockSpec(memory_space=pltpu.HBM)
    moved = sum(a.size * a.dtype.itemsize for a in args)
    return pl.pallas_call(
        kernel,
        in_specs=specs,
        out_specs=[VMEM] * len(outs),
        out_shape=[jax.ShapeDtypeStruct(*o) for o in outs],
        scratch_shapes=list(scratch),
        input_output_aliases=aliases or {},
        compiler_params=PARAMS,
        cost_estimate=pl.CostEstimate(flops=flops, bytes_accessed=moved, transcendentals=0),
    )(*args)


def shards(embeddings, cluster_blocks):
    block, width = embeddings.shape
    from_other = swapped(embeddings, other_neighbour)
    from_mate = swapped(embeddings, pair_mate)

    bounds = jnp.cumsum(cluster_blocks)
    me = lax.axis_index(AXES)
    odd = me % 2
    second = me // 4 % 2
    with_prev = joined(bounds, me - 1, 1)
    with_next = joined(bounds, me, 1)
    around = joined(bounds, me - 1, 2)
    before = joined(bounds, me - 4, 3)
    after = joined(bounds, me + 1, 3)
    with_core = jnp.where(second == 1, before, after)
    with_column = jnp.where(second == 1, after, before)
    core_to_mate = jnp.where(second == 1, odd, 1 - odd)
    flags = jnp.stack(
        [
            jnp.where(odd == 1, with_prev, with_next),
            jnp.where(odd == 1, with_next, with_prev),
            around,
            with_core * (1 - core_to_mate),
            with_core * core_to_mate,
            with_column * core_to_mate,
            with_column * (1 - core_to_mate),
            jnp.zeros_like(me),
        ]
    )[None, :]
    units = ((block, width), jnp.bfloat16)
    line = ((1, block), jnp.float32)
    tile = 2 * block * block * width

    stage = [pltpu.VMEM(*units), pltpu.SemaphoreType.DMA((FETCHES,))]
    own, high = call(own_kernel, (embeddings,), [units, line], stage, flops=tile, in_hbm=(0,))
    column = swapped(own, column_neighbour)
    core = swapped(own, core_mate)
    mate, high = call(
        near_kernel, (flags, from_mate, own, high), [units, line], flops=tile, aliases={1: 0}
    )
    other, to_other, to_mate = call(
        between_kernel, (flags, from_other, mate), [units, line, line], flops=tile, aliases={1: 0}
    )
    both = [pltpu.VMEM((2, block, width), jnp.bfloat16), pltpu.SemaphoreType.DMA((2,))]
    to_other, to_mate, to_core = call(
        far_kernel,
        (flags, core, column, other, mate, to_other, to_mate),
        [line, line, line],
        both,
        flops=tile,
        in_hbm=(1, 2),
    )
    from_other = swapped(to_other, other_neighbour)
    from_mate = swapped(to_mate, pair_mate)
    from_core = swapped(to_core, to_the_ends)
    high = call(last_kernel, (flags, other, own, high), [line], flops=tile)[0]
    at_end = (me == 0) | (me == lax.axis_size(AXES) - 1)
    returned = jnp.maximum(jnp.where(at_end, from_core, from_other), from_mate)
    return jnp.maximum(high, returned).reshape(block)


def solution(mesh):
    in_specs = (P(AXES, None), P())
    out_specs = P(AXES)
    return jax.shard_map(shards, mesh=mesh, in_specs=in_specs, out_specs=out_specs, check_vma=False)
```

time: 41.9 us -> 40.3 us (0.962)
  the two profiles are of different devices: /device:TPU:0 before, /device:TPU:1 now
where the time goes in v6:
time: 40.3 us; the launch traced here: 39.8 us
  starting transfers between devices  15.9 us (39%)
  waiting for transfers between devices  11.6 us (29%)
  Pallas kernels  5.36 us (13%)
  between operations  3.25 us (8%)
  local copies, waits for them, and re-layouts  2.11 us (5%)
  other arithmetic  1.51 us (4%)
    ppermute x7, starting transfers between devices, swapped(): return lax.ppermute(block, AXES, [p for p in pairs if p[1] is not None])  15.9 us
    ppermute x7, waiting for transfers between devices, swapped(): return lax.ppermute(block, AXES, [p for p in pairs if p[1] is not None])  11.6 us
    pallas_call x5, Pallas kernels, call(): pl.pallas_call(kernel, in_specs=specs, out_specs=[VMEM] * len(outs), out_...  5.36 us
    unnamed x4, local copies, waits for them, and re-layouts  1.91 us
  transfers between devices with their start and end apart: 7, of which 4 were waited for; matrix products, arithmetic and copies ran while one was open for 3% of the time, Pallas kernels for 7%

profile of v6, /device:TPU:1, one launch (start us, length us, event | category | flops | bytes accessed | tf_op | source)
XLA Modules:
  0.0 39.8 jit_solution(6779726292088340382)
XLA Ops:
  0.0 2.1 %collective-permute-start.1 = (bf16[512,1024]{1,0:T(8,128)(2,1)}, bf16[512,1024]{1,0:T(8,128)(2,1)S(1)}, u32[]{:S(2)}, u32[]{:S(2)}) collective-permute-start(bf16[512,1024]{1,0:T(8,128)(2,1)} %raw_ref.1), channel_id=1, source_target_pairs={{0,1},{1,0},{2,3},{3,2},{4,5},{5,4},{6,7},{7,6},{8,9},{9,8},{10,11... | collective-permute-start | bytes 3145736 | tf_op jit(solution)/shard_map/ppermute | solution.py:39
  2.1 2.7 %collective-permute-start = (bf16[512,1024]{1,0:T(8,128)(2,1)}, bf16[512,1024]{1,0:T(8,128)(2,1)S(1)}, u32[]{:S(2)}, u32[]{:S(2)}) collective-permute-start(bf16[512,1024]{1,0:T(8,128)(2,1)} %raw_ref.1), channel_id=1, source_target_pairs={{0,255},{1,2},{2,1},{3,4},{4,3},{5,6},{6,5},{7,8},{8,7},{9,10},{10... | collective-permute-start | bytes 3145736 | tf_op jit(solution)/shard_map/ppermute | solution.py:39
  4.9 1.3 %copy-done = bf16[512,1024]{1,0:T(8,128)(2,1)S(1)} copy-done((bf16[512,1024]{1,0:T(8,128)(2,1)S(1)}, bf16[512,1024]{1,0:T(8,128)(2,1)}, u32[]{:S(2)}) %copy-start) | copy-done | bytes 1048600
  6.1 1.3 %shard_map.28 = (bf16[512,1024]{1,0:T(8,128)(2,1)S(1)}, f32[1,512]{1,0:T(1,128)S(1)}) custom-call(bf16[512,1024]{1,0:T(8,128)(2,1)S(1)} %copy-done), custom_call_target="tpu_custom_call" | custom-call | flops 536870912 | bytes 1048576 | tf_op jit(solution)/shard_map/pallas_call | solution.py:171
  7.5 7.1 %collective-permute-start.2 = (bf16[512,1024]{1,0:T(8,128)(2,1)S(1)}, bf16[512,1024]{1,0:T(8,128)(2,1)}, u32[]{:S(2)}, u32[]{:S(2)}) collective-permute-start(bf16[512,1024]{1,0:T(8,128)(2,1)S(1)} %get-tuple-element.15.own_ref), channel_id=1, source_target_pairs={{0,4},{1,5},{2,6},{3,7},{4,0},{5,1},{6,2},{7,3},{8,12},{9,13},{10,... | collective-permute-start | bytes 3145736 | tf_op jit(solution)/shard_map/ppermute | solution.py:39
  14.6 1.9 %collective-permute-start.3 = (bf16[512,1024]{1,0:T(8,128)(2,1)S(1)}, bf16[512,1024]{1,0:T(8,128)(2,1)}, u32[]{:S(2)}, u32[]{:S(2)}) collective-permute-start(bf16[512,1024]{1,0:T(8,128)(2,1)S(1)} %get-tuple-element.15.own_ref), channel_id=1, source_target_pairs={{4,8},{5,9},{6,10},{7,11},{8,4},{9,5},{10,6},{11,7},{12,16},{13,17... | collective-permute-start | bytes 3145736 | tf_op jit(solution)/shard_map/ppermute | solution.py:39
  16.6 0.0 copy-start.1
  16.6 0.6 %copy-done.1 = s32[128]{0:T(128)S(1)} copy-done((s32[128]{0:T(128)S(1)}, s32[128]{0:T(128)}, u32[]{:S(2)}) %copy-start.1) | copy-done | bytes 536
  17.2 0.1 copy.5
  17.3 0.2 reduce-window.9
  17.5 0.8 %convert_reduce_fusion = (s32[]{:T(128)}, s32[]{:T(128)}, s32[]{:T(128)}, s32[]{:T(128)}, s32[]{:T(128)}) fusion(s32[128,1]{1,0:T(8,128)S(1)} %reduce-window.9, s32[]{:T(128)S(6)} %add.35, s32[]{:T(128)S(6)} %add.33, s32[]{:T(128)S(6)} %sub.18, s32[]{:T(128)S(6)} %add.31, s32[]{:T(128)S(6)} %sub.20), kind=kLoop, calls=%fused_computation | loop fusion | flops 2939 | bytes 552 | tf_op jit(solution)/shard_map/reduce_sum | solution.py:44
  21.4 0.1 stack.35
  21.5 2.6 %collective-permute-done.1.raw_ref = bf16[512,1024]{1,0:T(8,128)(2,1)S(1)} collective-permute-done((bf16[512,1024]{1,0:T(8,128)(2,1)}, bf16[512,1024]{1,0:T(8,128)(2,1)S(1)}, u32[]{:S(2)}, u32[]{:S(2)}) %collective-permute-start.1) | collective-permute-done | bytes 1048608 | tf_op jit(solution)/shard_map/ppermute | solution.py:39
  24.1 1.1 %shard_map.29 = (bf16[512,1024]{1,0:T(8,128)(2,1)S(1)}, f32[1,512]{1,0:T(1,128)S(1)}) custom-call(s32[1,8]{1,0:T(1,128)S(1)} %bitcast.10, bf16[512,1024]{1,0:T(8,128)(2,1)S(1)} %collective-permute-done.1.raw_ref, bf16[512,1024]{1,0:T(8,128)(2,1)S(1)} %get-tuple-element.15.own_ref, ...), custom_call_target="tpu_custom_call", output_to_operand_aliasing={{0}: (1, {})} | custom-call | flops 536870912 | bytes 2099232 | tf_op jit(solution)/shard_map/pallas_call | solution.py:171
  25.2 3.8 %collective-permute-done.raw_ref = bf16[512,1024]{1,0:T(8,128)(2,1)S(1)} collective-permute-done((bf16[512,1024]{1,0:T(8,128)(2,1)}, bf16[512,1024]{1,0:T(8,128)(2,1)S(1)}, u32[]{:S(2)}, u32[]{:S(2)}) %collective-permute-start) | collective-permute-done | bytes 1048608 | tf_op jit(solution)/shard_map/ppermute | solution.py:39
  29.0 0.3 shard_map.30
  29.4 0.0 collective-permute-done.2.core_ref
  29.4 1.5 %collective-permute-done.3.column_ref = bf16[512,1024]{1,0:T(8,128)(2,1)} collective-permute-done((bf16[512,1024]{1,0:T(8,128)(2,1)S(1)}, bf16[512,1024]{1,0:T(8,128)(2,1)}, u32[]{:S(2)}, u32[]{:S(2)}) %collective-permute-start.3) | collective-permute-done | bytes 1048608 | tf_op jit(solution)/shard_map/ppermute | solution.py:39
  30.8 2.5 %shard_map.32 = (f32[1,512]{1,0:T(1,128)S(1)}, f32[1,512]{1,0:T(1,128)S(1)}, f32[1,512]{1,0:T(1,128)S(1)}) custom-call(s32[1,8]{1,0:T(1,128)S(1)} %bitcast.12, bf16[512,1024]{1,0:T(8,128)(2,1)} %collective-permute-done.2.core_ref, bf16[512,1024]{1,0:T(8,128)(2,1)} %collective-permute-done.3.column_ref, bf16[512,1024]{1,0:T(8,128)(2,1)S(1)} %get-tuple-element.18.other_ref, ...), custom_call_target="tpu_custom_call" | custom-call | flops 536870912 | bytes 4198432 | tf_op jit(solution)/shard_map/pallas_call | solution.py:171
  33.3 1.3 %collective-permute-start.4 = (f32[1,512]{1,0:T(1,128)S(1)}, f32[1,512]{1,0:T(1,128)S(1)}, u32[]{:S(2)}, u32[]{:S(2)}) collective-permute-start(f32[1,512]{1,0:T(1,128)S(1)} %get-tuple-element.22), channel_id=1, source_target_pairs={{4,0},{251,255}} | collective-permute-start | bytes 6152 | tf_op jit(solution)/shard_map/ppermute | solution.py:39
  34.6 0.7 %collective-permute-start.5 = (f32[1,512]{1,0:T(1,128)S(1)}, f32[1,512]{1,0:T(1,128)S(1)}, u32[]{:S(2)}, u32[]{:S(2)}) collective-permute-start(f32[1,512]{1,0:T(1,128)S(1)} %get-tuple-element.23), channel_id=1, source_target_pairs={{0,255},{1,2},{2,1},{3,4},{4,3},{5,6},{6,5},{7,8},{8,7},{9,10},{10... | collective-permute-start | bytes 6152 | tf_op jit(solution)/shard_map/ppermute | solution.py:39
  35.4 0.1 shard_map.31
  35.5 3.7 %collective-permute-done.5 = f32[1,512]{1,0:T(1,128)S(1)} collective-permute-done((f32[1,512]{1,0:T(1,128)S(1)}, f32[1,512]{1,0:T(1,128)S(1)}, u32[]{:S(2)}, u32[]{:S(2)}) %collective-permute-start.5) | collective-permute-done | bytes 2080 | tf_op jit(solution)/shard_map/ppermute | solution.py:39
  39.2 0.6 %fusion.1 = f32[1,512]{1,0:T(1,128)} fusion(f32[1,512]{1,0:T(1,128)S(1)} %shard_map.31, f32[1,512]{1,0:T(1,128)S(1)} %collective-permute-done.6, f32[1,512]{1,0:T(1,128)S(1)} %collective-permute-done.4, f32[1,512]{1,0:T(1,128)S(1)} %collective-permute-done.5, pred[]{:T(512)S(6)} %or.3), kind=kLoop, calls=%fused_computation.9 | loop fusion | flops 1536 | bytes 10241 | tf_op jit(solution)/shard_map/max | solution.py:241
  (4 shorter events, 0.0 us)
Async XLA Ops:
  0.0 24.1 %collective-permute-start.1 = (bf16[512,1024]{1,0:T(8,128)(2,1)}, bf16[512,1024]{1,0:T(8,128)(2,1)S(1)}, u32[]{:S(2)}, u32[]{:S(2)}) collective-permute-start(bf16[512,1024]{1,0:T(8,128)(2,1)} %raw_ref.1), channel_id=1, source_target_pairs={{0,1},{1,0},{2,3},{3,2},{4,5},{5,4},{6,7},{7,6},{8,9},{9,8},{10,11... | collective-permute-start | bytes 3145736 | tf_op jit(solution)/shard_map/ppermute | solution.py:39
  2.1 26.9 %collective-permute-start = (bf16[512,1024]{1,0:T(8,128)(2,1)}, bf16[512,1024]{1,0:T(8,128)(2,1)S(1)}, u32[]{:S(2)}, u32[]{:S(2)}) collective-permute-start(bf16[512,1024]{1,0:T(8,128)(2,1)} %raw_ref.1), channel_id=1, source_target_pairs={{0,255},{1,2},{2,1},{3,4},{4,3},{5,6},{6,5},{7,8},{8,7},{9,10},{10... | collective-permute-start | bytes 3145736 | tf_op jit(solution)/shard_map/ppermute | solution.py:39
  4.9 1.3 %copy-start = (bf16[512,1024]{1,0:T(8,128)(2,1)S(1)}, bf16[512,1024]{1,0:T(8,128)(2,1)}, u32[]{:S(2)}) copy-start(bf16[512,1024]{1,0:T(8,128)(2,1)} %raw_ref.1) | copy-start | bytes 3145732
  7.5 21.9 %collective-permute-start.2 = (bf16[512,1024]{1,0:T(8,128)(2,1)S(1)}, bf16[512,1024]{1,0:T(8,128)(2,1)}, u32[]{:S(2)}, u32[]{:S(2)}) collective-permute-start(bf16[512,1024]{1,0:T(8,128)(2,1)S(1)} %get-tuple-element.15.own_ref), channel_id=1, source_target_pairs={{0,4},{1,5},{2,6},{3,7},{4,0},{5,1},{6,2},{7,3},{8,12},{9,13},{10,... | collective-permute-start | bytes 3145736 | tf_op jit(solution)/shard_map/ppermute | solution.py:39
  14.6 16.2 %collective-permute-start.3 = (bf16[512,1024]{1,0:T(8,128)(2,1)S(1)}, bf16[512,1024]{1,0:T(8,128)(2,1)}, u32[]{:S(2)}, u32[]{:S(2)}) collective-permute-start(bf16[512,1024]{1,0:T(8,128)(2,1)S(1)} %get-tuple-element.15.own_ref), channel_id=1, source_target_pairs={{4,8},{5,9},{6,10},{7,11},{8,4},{9,5},{10,6},{11,7},{12,16},{13,17... | collective-permute-start | bytes 3145736 | tf_op jit(solution)/shard_map/ppermute | solution.py:39
  16.6 0.7 %copy-start.1 = (s32[128]{0:T(128)S(1)}, s32[128]{0:T(128)}, u32[]{:S(2)}) copy-start(s32[128]{0:T(128)} %param.3) | copy-start | bytes 1540
  33.3 2.2 %collective-permute-start.4 = (f32[1,512]{1,0:T(1,128)S(1)}, f32[1,512]{1,0:T(1,128)S(1)}, u32[]{:S(2)}, u32[]{:S(2)}) collective-permute-start(f32[1,512]{1,0:T(1,128)S(1)} %get-tuple-element.22), channel_id=1, source_target_pairs={{4,0},{251,255}} | collective-permute-start | bytes 6152 | tf_op jit(solution)/shard_map/ppermute | solution.py:39
  34.6 4.6 %collective-permute-start.5 = (f32[1,512]{1,0:T(1,128)S(1)}, f32[1,512]{1,0:T(1,128)S(1)}, u32[]{:S(2)}, u32[]{:S(2)}) collective-permute-start(f32[1,512]{1,0:T(1,128)S(1)} %get-tuple-element.23), channel_id=1, source_target_pairs={{0,255},{1,2},{2,1},{3,4},{4,3},{5,6},{6,5},{7,8},{8,7},{9,10},{10... | collective-permute-start | bytes 6152 | tf_op jit(solution)/shard_map/ppermute | solution.py:39
  35.4 3.9 %collective-permute-start.6 = (f32[1,512]{1,0:T(1,128)S(1)}, f32[1,512]{1,0:T(1,128)S(1)}, u32[]{:S(2)}, u32[]{:S(2)}) collective-permute-start(f32[1,512]{1,0:T(1,128)S(1)} %get-tuple-element.24), channel_id=1, source_target_pairs={{0,1},{1,0},{2,3},{3,2},{4,5},{5,4},{6,7},{7,6},{8,9},{9,8},{10,11... | collective-permute-start | bytes 6152 | tf_op jit(solution)/shard_map/ppermute | solution.py:39

commit v7 on v6

--- a/solution.py
+++ b/solution.py
@@ -29,8 +29,12 @@
     return j if 0 <= j < n else None
 
 
-def to_the_ends(i, n):
-    return {4: 0, n - 5: n - 1}.get(i)
+def return_to_other(i, n):
+    return {4: 0, 0: 3, n - 5: n - 1, n - 1: n - 4}.get(i, other_neighbour(i, n))
+
+
+def beside_the_ends(i, n):
+    return {4: 3, n - 5: n - 4}.get(i)
 
 
 def swapped(block, partner):
@@ -120,7 +124,7 @@
 
 def far_kernel(
     flags_ref, core_ref, column_ref, other_ref, mate_ref, other_in_ref, mate_in_ref,
-    to_other_ref, to_mate_ref, to_core_ref, stage_ref, sems,
+    first_ref, to_mate_ref, to_other_ref, to_core_ref, stage_ref, sems,
 ):
     to_other_ref[...] = other_in_ref[...]
     to_mate_ref[...] = mate_in_ref[...]
@@ -148,6 +152,11 @@
                 line_ref[...] = jnp.maximum(line_ref[...], column_max(products))
                 if far_ref is core_ref and near_ref is other_ref:
                     to_core_ref[...] = row_max(products)
+    first_ref[...] = to_other_ref[...]
+
+    @pl.when(flags_ref[0, 7] == 1)
+    def _():
+        first_ref[...] = to_core_ref[...]
 
 
 def last_kernel(flags_ref, other_ref, own_ref, high_in_ref, high_ref):
@@ -194,6 +203,8 @@
     around = joined(bounds, me - 1, 2)
     before = joined(bounds, me - 4, 3)
     after = joined(bounds, me + 1, 3)
+    blocks = lax.axis_size(AXES)
+    serves_end = (me == 4) | (me == blocks - 5)
     with_core = jnp.where(second == 1, before, after)
     with_column = jnp.where(second == 1, after, before)
     core_to_mate = jnp.where(second == 1, odd, 1 - odd)
@@ -206,7 +217,7 @@
             with_core * core_to_mate,
             with_column * core_to_mate,
             with_column * (1 - core_to_mate),
-            jnp.zeros_like(me),
+            serves_end.astype(jnp.int32),
         ]
     )[None, :]
     units = ((block, width), jnp.bfloat16)
@@ -223,8 +234,12 @@
     other, to_other, to_mate = call(
         between_kernel, (flags, from_other, mate), [units, line, line], flops=tile, aliases={1: 0}
     )
-    both = [pltpu.VMEM((2, block, width), jnp.bfloat16), pltpu.SemaphoreType.DMA((2,))]
-    to_other, to_mate, to_core = call(
+    both = [
+        pltpu.VMEM(*line),
+        pltpu.VMEM((2, block, width), jnp.bfloat16),
+        pltpu.SemaphoreType.DMA((2,)),
+    ]
+    first, to_mate, to_other = call(
         far_kernel,
         (flags, core, column, other, mate, to_other, to_mate),
         [line, line, line],
@@ -232,13 +247,14 @@
         flops=tile,
         in_hbm=(1, 2),
     )
-    from_other = swapped(to_other, other_neighbour)
+    from_first = swapped(first, return_to_other)
     from_mate = swapped(to_mate, pair_mate)
-    from_core = swapped(to_core, to_the_ends)
+    from_beside = swapped(to_other, beside_the_ends)
     high = call(last_kernel, (flags, other, own, high), [line], flops=tile)[0]
-    at_end = (me == 0) | (me == lax.axis_size(AXES) - 1)
-    returned = jnp.maximum(jnp.where(at_end, from_core, from_other), from_mate)
-    return jnp.maximum(high, returned).reshape(block)
+    beside_end = (me == 3) | (me == blocks - 4)
+    returned = jnp.maximum(jnp.where(beside_end, LOWEST, from_first), from_mate)
+    rest = jnp.where(beside_end, from_beside, LOWEST)
+    return jnp.maximum(jnp.maximum(high, returned), rest).reshape(block)
 
 
 def solution(mesh):

time: 40.3 us -> 39.9 us (0.990)
  waiting for transfers between devices: 11.6 us -> 8.49 us
  starting transfers between devices: 15.9 us -> 18.8 us
    ppermute x7, waiting for transfers between devices: 11.6 us -> 8.49 us  [swapped(): return lax.ppermute(block, AXES, [p for p in pairs if p[1] is not None])]
    ppermute x7, starting transfers between devices: 15.9 us -> 18.8 us  [swapped(): return lax.ppermute(block, AXES, [p for p in pairs if p[1] is not None])]
where the time goes in v7:
time: 39.9 us; the launch traced here: 39.7 us
  starting transfers between devices  18.8 us (47%)
  waiting for transfers between devices  8.49 us (21%)
  Pallas kernels  5.47 us (14%)
  between operations  3.29 us (8%)
  local copies, waits for them, and re-layouts  2.11 us (5%)
  other arithmetic  1.49 us (4%)
    ppermute x7, starting transfers between devices, swapped(): return lax.ppermute(block, AXES, [p for p in pairs if p[1] is not None])  18.8 us
    ppermute x7, waiting for transfers between devices, swapped(): return lax.ppermute(block, AXES, [p for p in pairs if p[1] is not None])  8.49 us
    pallas_call x5, Pallas kernels, call(): pl.pallas_call(kernel, in_specs=specs, out_specs=[VMEM] * len(outs), out_...  5.47 us
    unnamed x4, local copies, waits for them, and re-layouts  1.91 us
  transfers between devices with their start and end apart: 7, of which 4 were waited for; matrix products, arithmetic and copies ran while one was open for 3% of the time, Pallas kernels for 7%

profile of v7, /device:TPU:1, one launch (start us, length us, event | category | flops | bytes accessed | tf_op | source)
XLA Modules:
  0.0 39.7 jit_solution(10092672917326148785)
XLA Ops:
  0.0 2.1 %collective-permute-start.1 = (bf16[512,1024]{1,0:T(8,128)(2,1)}, bf16[512,1024]{1,0:T(8,128)(2,1)S(1)}, u32[]{:S(2)}, u32[]{:S(2)}) collective-permute-start(bf16[512,1024]{1,0:T(8,128)(2,1)} %raw_ref.1), channel_id=1, source_target_pairs={{0,1},{1,0},{2,3},{3,2},{4,5},{5,4},{6,7},{7,6},{8,9},{9,8},{10,11... | collective-permute-start | bytes 3145736 | tf_op jit(solution)/shard_map/ppermute | solution.py:43
  2.1 2.7 %collective-permute-start = (bf16[512,1024]{1,0:T(8,128)(2,1)}, bf16[512,1024]{1,0:T(8,128)(2,1)S(1)}, u32[]{:S(2)}, u32[]{:S(2)}) collective-permute-start(bf16[512,1024]{1,0:T(8,128)(2,1)} %raw_ref.1), channel_id=1, source_target_pairs={{0,255},{1,2},{2,1},{3,4},{4,3},{5,6},{6,5},{7,8},{8,7},{9,10},{10... | collective-permute-start | bytes 3145736 | tf_op jit(solution)/shard_map/ppermute | solution.py:43
  4.9 1.3 %copy-done = bf16[512,1024]{1,0:T(8,128)(2,1)S(1)} copy-done((bf16[512,1024]{1,0:T(8,128)(2,1)S(1)}, bf16[512,1024]{1,0:T(8,128)(2,1)}, u32[]{:S(2)}) %copy-start) | copy-done | bytes 1048600
  6.1 1.3 %shard_map.28 = (bf16[512,1024]{1,0:T(8,128)(2,1)S(1)}, f32[1,512]{1,0:T(1,128)S(1)}) custom-call(bf16[512,1024]{1,0:T(8,128)(2,1)S(1)} %copy-done), custom_call_target="tpu_custom_call" | custom-call | flops 536870912 | bytes 1048576 | tf_op jit(solution)/shard_map/pallas_call | solution.py:180
  7.5 7.1 %collective-permute-start.2 = (bf16[512,1024]{1,0:T(8,128)(2,1)S(1)}, bf16[512,1024]{1,0:T(8,128)(2,1)}, u32[]{:S(2)}, u32[]{:S(2)}) collective-permute-start(bf16[512,1024]{1,0:T(8,128)(2,1)S(1)} %get-tuple-element.15.own_ref), channel_id=1, source_target_pairs={{0,4},{1,5},{2,6},{3,7},{4,0},{5,1},{6,2},{7,3},{8,12},{9,13},{10,... | collective-permute-start | bytes 3145736 | tf_op jit(solution)/shard_map/ppermute | solution.py:43
  14.6 1.9 %collective-permute-start.3 = (bf16[512,1024]{1,0:T(8,128)(2,1)S(1)}, bf16[512,1024]{1,0:T(8,128)(2,1)}, u32[]{:S(2)}, u32[]{:S(2)}) collective-permute-start(bf16[512,1024]{1,0:T(8,128)(2,1)S(1)} %get-tuple-element.15.own_ref), channel_id=1, source_target_pairs={{4,8},{5,9},{6,10},{7,11},{8,4},{9,5},{10,6},{11,7},{12,16},{13,17... | collective-permute-start | bytes 3145736 | tf_op jit(solution)/shard_map/ppermute | solution.py:43
  16.6 0.0 copy-start.1
  16.6 0.6 %copy-done.1 = s32[128]{0:T(128)S(1)} copy-done((s32[128]{0:T(128)S(1)}, s32[128]{0:T(128)}, u32[]{:S(2)}) %copy-start.1) | copy-done | bytes 536
  17.2 0.1 copy.5
  17.3 0.2 reduce-window.9
  17.5 0.7 %convert_reduce_fusion = (s32[]{:T(128)}, s32[]{:T(128)}, s32[]{:T(128)}, s32[]{:T(128)}, s32[]{:T(128)}) fusion(s32[128,1]{1,0:T(8,128)S(1)} %reduce-window.9, s32[]{:T(128)S(6)} %add.35, s32[]{:T(128)S(6)} %add.33, s32[]{:T(128)S(6)} %sub.18, s32[]{:T(128)S(6)} %add.31, s32[]{:T(128)S(6)} %sub.20), kind=kLoop, calls=%fused_computation | loop fusion | flops 2939 | bytes 552 | tf_op jit(solution)/shard_map/reduce_sum | solution.py:48
  21.4 0.1 stack.43
  21.5 2.6 %collective-permute-done.1.raw_ref = bf16[512,1024]{1,0:T(8,128)(2,1)S(1)} collective-permute-done((bf16[512,1024]{1,0:T(8,128)(2,1)}, bf16[512,1024]{1,0:T(8,128)(2,1)S(1)}, u32[]{:S(2)}, u32[]{:S(2)}) %collective-permute-start.1) | collective-permute-done | bytes 1048608 | tf_op jit(solution)/shard_map/ppermute | solution.py:43
  24.1 1.1 %shard_map.29 = (bf16[512,1024]{1,0:T(8,128)(2,1)S(1)}, f32[1,512]{1,0:T(1,128)S(1)}) custom-call(s32[1,8]{1,0:T(1,128)S(1)} %bitcast.11, bf16[512,1024]{1,0:T(8,128)(2,1)S(1)} %collective-permute-done.1.raw_ref, bf16[512,1024]{1,0:T(8,128)(2,1)S(1)} %get-tuple-element.15.own_ref, ...), custom_call_target="tpu_custom_call", output_to_operand_aliasing={{0}: (1, {})} | custom-call | flops 536870912 | bytes 2099232 | tf_op jit(solution)/shard_map/pallas_call | solution.py:180
  25.2 3.8 %collective-permute-done.raw_ref = bf16[512,1024]{1,0:T(8,128)(2,1)S(1)} collective-permute-done((bf16[512,1024]{1,0:T(8,128)(2,1)}, bf16[512,1024]{1,0:T(8,128)(2,1)S(1)}, u32[]{:S(2)}, u32[]{:S(2)}) %collective-permute-start) | collective-permute-done | bytes 1048608 | tf_op jit(solution)/shard_map/ppermute | solution.py:43
  29.0 0.3 shard_map.30
  29.4 1.5 %collective-permute-done.3.column_ref = bf16[512,1024]{1,0:T(8,128)(2,1)} collective-permute-done((bf16[512,1024]{1,0:T(8,128)(2,1)S(1)}, bf16[512,1024]{1,0:T(8,128)(2,1)}, u32[]{:S(2)}, u32[]{:S(2)}) %collective-permute-start.3) | collective-permute-done | bytes 1048608 | tf_op jit(solution)/shard_map/ppermute | solution.py:43
  30.8 2.6 %shard_map.32 = (f32[1,512]{1,0:T(1,128)S(1)}, f32[1,512]{1,0:T(1,128)S(1)}, f32[1,512]{1,0:T(1,128)S(1)}) custom-call(s32[1,8]{1,0:T(1,128)S(1)} %bitcast.13, bf16[512,1024]{1,0:T(8,128)(2,1)} %collective-permute-done.2.core_ref, bf16[512,1024]{1,0:T(8,128)(2,1)} %collective-permute-done.3.column_ref, bf16[512,1024]{1,0:T(8,128)(2,1)S(1)} %get-tuple-element.18.other_ref, ...), custom_call_target="tpu_custom_call" | custom-call | flops 536870912 | bytes 4198432 | tf_op jit(solution)/shard_map/pallas_call | solution.py:180
  33.4 0.1 collective-permute-start.4
  33.5 0.1 collective-permute-start.5
  33.6 4.7 %collective-permute-start.6 = (f32[1,512]{1,0:T(1,128)S(1)}, f32[1,512]{1,0:T(1,128)S(1)}, u32[]{:S(2)}, u32[]{:S(2)}) collective-permute-start(f32[1,512]{1,0:T(1,128)S(1)} %get-tuple-element.24), channel_id=1, source_target_pairs={{4,3},{251,252}} | collective-permute-start | bytes 6152 | tf_op jit(solution)/shard_map/ppermute | solution.py:43
  38.4 0.1 shard_map.31
  38.5 0.6 %collective-permute-done.6 = f32[1,512]{1,0:T(1,128)S(1)} collective-permute-done((f32[1,512]{1,0:T(1,128)S(1)}, f32[1,512]{1,0:T(1,128)S(1)}, u32[]{:S(2)}, u32[]{:S(2)}) %collective-permute-start.6) | collective-permute-done | bytes 2080 | tf_op jit(solution)/shard_map/ppermute | solution.py:43
  39.1 0.6 %fusion.2 = f32[1,512]{1,0:T(1,128)} fusion(f32[1,512]{1,0:T(1,128)S(1)} %shard_map.31, f32[1,512]{1,0:T(1,128)S(1)} %collective-permute-done.5, f32[1,512]{1,0:T(1,128)S(1)} %collective-permute-done.4, pred[]{:T(512)S(6)} %or.7, f32[1,512]{1,0:T(1,128)S(1)} %collective-permute-done.6), kind=kLoop, calls=%fused_computation.11 | loop fusion | flops 2560 | bytes 10241 | tf_op jit(solution)/shard_map/max | solution.py:257
  (4 shorter events, 0.0 us)
Async XLA Ops:
  0.0 24.1 %collective-permute-start.1 = (bf16[512,1024]{1,0:T(8,128)(2,1)}, bf16[512,1024]{1,0:T(8,128)(2,1)S(1)}, u32[]{:S(2)}, u32[]{:S(2)}) collective-permute-start(bf16[512,1024]{1,0:T(8,128)(2,1)} %raw_ref.1), channel_id=1, source_target_pairs={{0,1},{1,0},{2,3},{3,2},{4,5},{5,4},{6,7},{7,6},{8,9},{9,8},{10,11... | collective-permute-start | bytes 3145736 | tf_op jit(solution)/shard_map/ppermute | solution.py:43
  2.1 26.9 %collective-permute-start = (bf16[512,1024]{1,0:T(8,128)(2,1)}, bf16[512,1024]{1,0:T(8,128)(2,1)S(1)}, u32[]{:S(2)}, u32[]{:S(2)}) collective-permute-start(bf16[512,1024]{1,0:T(8,128)(2,1)} %raw_ref.1), channel_id=1, source_target_pairs={{0,255},{1,2},{2,1},{3,4},{4,3},{5,6},{6,5},{7,8},{8,7},{9,10},{10... | collective-permute-start | bytes 3145736 | tf_op jit(solution)/shard_map/ppermute | solution.py:43
  4.9 1.3 %copy-start = (bf16[512,1024]{1,0:T(8,128)(2,1)S(1)}, bf16[512,1024]{1,0:T(8,128)(2,1)}, u32[]{:S(2)}) copy-start(bf16[512,1024]{1,0:T(8,128)(2,1)} %raw_ref.1) | copy-start | bytes 3145732
  7.5 21.9 %collective-permute-start.2 = (bf16[512,1024]{1,0:T(8,128)(2,1)S(1)}, bf16[512,1024]{1,0:T(8,128)(2,1)}, u32[]{:S(2)}, u32[]{:S(2)}) collective-permute-start(bf16[512,1024]{1,0:T(8,128)(2,1)S(1)} %get-tuple-element.15.own_ref), channel_id=1, source_target_pairs={{0,4},{1,5},{2,6},{3,7},{4,0},{5,1},{6,2},{7,3},{8,12},{9,13},{10,... | collective-permute-start | bytes 3145736 | tf_op jit(solution)/shard_map/ppermute | solution.py:43
  14.6 16.2 %collective-permute-start.3 = (bf16[512,1024]{1,0:T(8,128)(2,1)S(1)}, bf16[512,1024]{1,0:T(8,128)(2,1)}, u32[]{:S(2)}, u32[]{:S(2)}) collective-permute-start(bf16[512,1024]{1,0:T(8,128)(2,1)S(1)} %get-tuple-element.15.own_ref), channel_id=1, source_target_pairs={{4,8},{5,9},{6,10},{7,11},{8,4},{9,5},{10,6},{11,7},{12,16},{13,17... | collective-permute-start | bytes 3145736 | tf_op jit(solution)/shard_map/ppermute | solution.py:43
  16.6 0.7 %copy-start.1 = (s32[128]{0:T(128)S(1)}, s32[128]{0:T(128)}, u32[]{:S(2)}) copy-start(s32[128]{0:T(128)} %param.3) | copy-start | bytes 1540
  33.4 5.1 %collective-permute-start.4 = (f32[1,512]{1,0:T(1,128)S(1)}, f32[1,512]{1,0:T(1,128)S(1)}, u32[]{:S(2)}, u32[]{:S(2)}) collective-permute-start(f32[1,512]{1,0:T(1,128)S(1)} %get-tuple-element.22), channel_id=1, source_target_pairs={{0,3},{1,2},{2,1},{3,4},{4,0},{5,6},{6,5},{7,8},{8,7},{9,10},{10,9... | collective-permute-start | bytes 6152 | tf_op jit(solution)/shard_map/ppermute | solution.py:43
  33.5 5.0 %collective-permute-start.5 = (f32[1,512]{1,0:T(1,128)S(1)}, f32[1,512]{1,0:T(1,128)S(1)}, u32[]{:S(2)}, u32[]{:S(2)}) collective-permute-start(f32[1,512]{1,0:T(1,128)S(1)} %get-tuple-element.23), channel_id=1, source_target_pairs={{0,1},{1,0},{2,3},{3,2},{4,5},{5,4},{6,7},{7,6},{8,9},{9,8},{10,11... | collective-permute-start | bytes 6152 | tf_op jit(solution)/shard_map/ppermute | solution.py:43
  33.6 5.5 %collective-permute-start.6 = (f32[1,512]{1,0:T(1,128)S(1)}, f32[1,512]{1,0:T(1,128)S(1)}, u32[]{:S(2)}, u32[]{:S(2)}) collective-permute-start(f32[1,512]{1,0:T(1,128)S(1)} %get-tuple-element.24), channel_id=1, source_target_pairs={{4,3},{251,252}} | collective-permute-start | bytes 6152 | tf_op jit(solution)/shard_map/ppermute | solution.py:43

commit v8 on v7

--- a/solution.py
+++ b/solution.py
@@ -123,7 +123,7 @@
 
 
 def far_kernel(
-    flags_ref, core_ref, column_ref, other_ref, mate_ref, other_in_ref, mate_in_ref,
+    flags_ref, column_ref, core_ref, other_ref, mate_ref, other_in_ref, mate_in_ref,
     first_ref, to_mate_ref, to_other_ref, to_core_ref, stage_ref, sems,
 ):
     to_other_ref[...] = other_in_ref[...]
@@ -241,7 +241,7 @@
     ]
     first, to_mate, to_other = call(
         far_kernel,
-        (flags, core, column, other, mate, to_other, to_mate),
+        (flags, column, core, other, mate, to_other, to_mate),
         [line, line, line],
         both,
         flops=tile,

time: 39.9 us -> 39.4 us (0.987)
  the two profiles are of different devices: /device:TPU:1 before, /device:TPU:32 now
where the time goes in v8:
time: 39.4 us; the launch traced here: 38.7 us
  waiting for transfers between devices  15.8 us (40%)
  starting transfers between devices  10.8 us (27%)
  Pallas kernels  5.2 us (13%)
  between operations  3.28 us (8%)
  local copies, waits for them, and re-layouts  2.11 us (5%)
  other arithmetic  1.49 us (4%)
    ppermute x7, waiting for transfers between devices, swapped(): return lax.ppermute(block, AXES, [p for p in pairs if p[1] is not None])  15.8 us
    ppermute x7, starting transfers between devices, swapped(): return lax.ppermute(block, AXES, [p for p in pairs if p[1] is not None])  10.8 us
    pallas_call x5, Pallas kernels, call(): pl.pallas_call(kernel, in_specs=specs, out_specs=[VMEM] * len(outs), out_...  5.2 us
    unnamed x4, local copies, waits for them, and re-layouts  1.91 us
  transfers between devices with their start and end apart: 7, of which 3 were waited for; matrix products, arithmetic and copies ran while one was open for 3% of the time, Pallas kernels for 7%

profile of v8, /device:TPU:32, one launch (start us, length us, event | category | flops | bytes accessed | tf_op | source)
XLA Modules:
  0.0 38.7 jit_solution(16049332082203991565)
XLA Ops:
  0.0 1.6 %collective-permute-start.1 = (bf16[512,1024]{1,0:T(8,128)(2,1)}, bf16[512,1024]{1,0:T(8,128)(2,1)S(1)}, u32[]{:S(2)}, u32[]{:S(2)}) collective-permute-start(bf16[512,1024]{1,0:T(8,128)(2,1)} %raw_ref.1), channel_id=1, source_target_pairs={{0,1},{1,0},{2,3},{3,2},{4,5},{5,4},{6,7},{7,6},{8,9},{9,8},{10,11... | collective-permute-start | bytes 3145736 | tf_op jit(solution)/shard_map/ppermute | solution.py:43
  1.6 3.1 %collective-permute-start = (bf16[512,1024]{1,0:T(8,128)(2,1)}, bf16[512,1024]{1,0:T(8,128)(2,1)S(1)}, u32[]{:S(2)}, u32[]{:S(2)}) collective-permute-start(bf16[512,1024]{1,0:T(8,128)(2,1)} %raw_ref.1), channel_id=1, source_target_pairs={{0,255},{1,2},{2,1},{3,4},{4,3},{5,6},{6,5},{7,8},{8,7},{9,10},{10... | collective-permute-start | bytes 3145736 | tf_op jit(solution)/shard_map/ppermute | solution.py:43
  4.7 1.3 %copy-done = bf16[512,1024]{1,0:T(8,128)(2,1)S(1)} copy-done((bf16[512,1024]{1,0:T(8,128)(2,1)S(1)}, bf16[512,1024]{1,0:T(8,128)(2,1)}, u32[]{:S(2)}) %copy-start) | copy-done | bytes 1048600
  5.9 1.3 %shard_map.28 = (bf16[512,1024]{1,0:T(8,128)(2,1)S(1)}, f32[1,512]{1,0:T(1,128)S(1)}) custom-call(bf16[512,1024]{1,0:T(8,128)(2,1)S(1)} %copy-done), custom_call_target="tpu_custom_call" | custom-call | flops 536870912 | bytes 1048576 | tf_op jit(solution)/shard_map/pallas_call | solution.py:180
  7.3 3.0 %collective-permute-start.2 = (bf16[512,1024]{1,0:T(8,128)(2,1)S(1)}, bf16[512,1024]{1,0:T(8,128)(2,1)}, u32[]{:S(2)}, u32[]{:S(2)}) collective-permute-start(bf16[512,1024]{1,0:T(8,128)(2,1)S(1)} %get-tuple-element.15.own_ref), channel_id=1, source_target_pairs={{4,8},{5,9},{6,10},{7,11},{8,4},{9,5},{10,6},{11,7},{12,16},{13,17... | collective-permute-start | bytes 3145736 | tf_op jit(solution)/shard_map/ppermute | solution.py:43
  10.3 0.1 collective-permute-start.3
  10.5 0.0 copy-start.1
  10.5 0.6 %copy-done.1 = s32[128]{0:T(128)S(1)} copy-done((s32[128]{0:T(128)S(1)}, s32[128]{0:T(128)}, u32[]{:S(2)}) %copy-start.1) | copy-done | bytes 536
  11.1 0.1 copy.5
  11.2 0.2 reduce-window.9
  11.4 0.7 %convert_reduce_fusion = (s32[]{:T(128)}, s32[]{:T(128)}, s32[]{:T(128)}, s32[]{:T(128)}, s32[]{:T(128)}) fusion(s32[128,1]{1,0:T(8,128)S(1)} %reduce-window.9, s32[]{:T(128)S(6)} %add.35, s32[]{:T(128)S(6)} %add.33, s32[]{:T(128)S(6)} %sub.18, s32[]{:T(128)S(6)} %add.31, s32[]{:T(128)S(6)} %sub.20), kind=kLoop, calls=%fused_computation | loop fusion | flops 2939 | bytes 552 | tf_op jit(solution)/shard_map/reduce_sum | solution.py:48
  15.3 0.1 stack.43
  15.4 9.7 %collective-permute-done.1.raw_ref = bf16[512,1024]{1,0:T(8,128)(2,1)S(1)} collective-permute-done((bf16[512,1024]{1,0:T(8,128)(2,1)}, bf16[512,1024]{1,0:T(8,128)(2,1)S(1)}, u32[]{:S(2)}, u32[]{:S(2)}) %collective-permute-start.1) | collective-permute-done | bytes 1048608 | tf_op jit(solution)/shard_map/ppermute | solution.py:43
  25.1 1.1 %shard_map.29 = (bf16[512,1024]{1,0:T(8,128)(2,1)S(1)}, f32[1,512]{1,0:T(1,128)S(1)}) custom-call(s32[1,8]{1,0:T(1,128)S(1)} %bitcast.11, bf16[512,1024]{1,0:T(8,128)(2,1)S(1)} %collective-permute-done.1.raw_ref, bf16[512,1024]{1,0:T(8,128)(2,1)S(1)} %get-tuple-element.15.own_ref, ...), custom_call_target="tpu_custom_call", output_to_operand_aliasing={{0}: (1, {})} | custom-call | flops 536870912 | bytes 2099232 | tf_op jit(solution)/shard_map/pallas_call | solution.py:180
  26.2 0.3 shard_map.30
  26.6 1.9 %collective-permute-done.2.column_ref = bf16[512,1024]{1,0:T(8,128)(2,1)} collective-permute-done((bf16[512,1024]{1,0:T(8,128)(2,1)S(1)}, bf16[512,1024]{1,0:T(8,128)(2,1)}, u32[]{:S(2)}, u32[]{:S(2)}) %collective-permute-start.2) | collective-permute-done | bytes 1048608 | tf_op jit(solution)/shard_map/ppermute | solution.py:43
  28.4 2.3 %shard_map.32 = (f32[1,512]{1,0:T(1,128)S(1)}, f32[1,512]{1,0:T(1,128)S(1)}, f32[1,512]{1,0:T(1,128)S(1)}) custom-call(s32[1,8]{1,0:T(1,128)S(1)} %bitcast.13, bf16[512,1024]{1,0:T(8,128)(2,1)} %collective-permute-done.2.column_ref, bf16[512,1024]{1,0:T(8,128)(2,1)} %collective-permute-done.3.core_ref, bf16[512,1024]{1,0:T(8,128)(2,1)S(1)} %get-tuple-element.18.other_ref, ...), custom_call_target="tpu_custom_call" | custom-call | flops 536870912 | bytes 4198432 | tf_op jit(solution)/shard_map/pallas_call | solution.py:180
  30.8 2.4 %collective-permute-start.4 = (f32[1,512]{1,0:T(1,128)S(1)}, f32[1,512]{1,0:T(1,128)S(1)}, u32[]{:S(2)}, u32[]{:S(2)}) collective-permute-start(f32[1,512]{1,0:T(1,128)S(1)} %get-tuple-element.22), channel_id=1, source_target_pairs={{0,3},{1,2},{2,1},{3,4},{4,0},{5,6},{6,5},{7,8},{8,7},{9,10},{10,9... | collective-permute-start | bytes 6152 | tf_op jit(solution)/shard_map/ppermute | solution.py:43
  33.1 0.0 collective-permute-start.5
  33.1 0.7 %collective-permute-start.6 = (f32[1,512]{1,0:T(1,128)S(1)}, f32[1,512]{1,0:T(1,128)S(1)}, u32[]{:S(2)}, u32[]{:S(2)}) collective-permute-start(f32[1,512]{1,0:T(1,128)S(1)} %get-tuple-element.24), channel_id=1, source_target_pairs={{4,3},{251,252}} | collective-permute-start | bytes 6152 | tf_op jit(solution)/shard_map/ppermute | solution.py:43
  33.8 0.1 shard_map.31
  33.9 4.2 %collective-permute-done.4 = f32[1,512]{1,0:T(1,128)S(1)} collective-permute-done((f32[1,512]{1,0:T(1,128)S(1)}, f32[1,512]{1,0:T(1,128)S(1)}, u32[]{:S(2)}, u32[]{:S(2)}) %collective-permute-start.4) | collective-permute-done | bytes 2080 | tf_op jit(solution)/shard_map/ppermute | solution.py:43
  38.1 0.0 collective-permute-done.6
  38.1 0.6 %fusion.2 = f32[1,512]{1,0:T(1,128)} fusion(f32[1,512]{1,0:T(1,128)S(1)} %shard_map.31, f32[1,512]{1,0:T(1,128)S(1)} %collective-permute-done.5, f32[1,512]{1,0:T(1,128)S(1)} %collective-permute-done.4, pred[]{:T(512)S(6)} %or.7, f32[1,512]{1,0:T(1,128)S(1)} %collective-permute-done.6), kind=kLoop, calls=%fused_computation.11 | loop fusion | flops 2560 | bytes 10241 | tf_op jit(solution)/shard_map/max | solution.py:257
  (4 shorter events, 0.0 us)
Async XLA Ops:
  0.0 25.1 %collective-permute-start.1 = (bf16[512,1024]{1,0:T(8,128)(2,1)}, bf16[512,1024]{1,0:T(8,128)(2,1)S(1)}, u32[]{:S(2)}, u32[]{:S(2)}) collective-permute-start(bf16[512,1024]{1,0:T(8,128)(2,1)} %raw_ref.1), channel_id=1, source_target_pairs={{0,1},{1,0},{2,3},{3,2},{4,5},{5,4},{6,7},{7,6},{8,9},{9,8},{10,11... | collective-permute-start | bytes 3145736 | tf_op jit(solution)/shard_map/ppermute | solution.py:43
  1.6 24.6 %collective-permute-start = (bf16[512,1024]{1,0:T(8,128)(2,1)}, bf16[512,1024]{1,0:T(8,128)(2,1)S(1)}, u32[]{:S(2)}, u32[]{:S(2)}) collective-permute-start(bf16[512,1024]{1,0:T(8,128)(2,1)} %raw_ref.1), channel_id=1, source_target_pairs={{0,255},{1,2},{2,1},{3,4},{4,3},{5,6},{6,5},{7,8},{8,7},{9,10},{10... | collective-permute-start | bytes 3145736 | tf_op jit(solution)/shard_map/ppermute | solution.py:43
  4.7 1.3 %copy-start = (bf16[512,1024]{1,0:T(8,128)(2,1)S(1)}, bf16[512,1024]{1,0:T(8,128)(2,1)}, u32[]{:S(2)}) copy-start(bf16[512,1024]{1,0:T(8,128)(2,1)} %raw_ref.1) | copy-start | bytes 3145732
  7.3 21.1 %collective-permute-start.2 = (bf16[512,1024]{1,0:T(8,128)(2,1)S(1)}, bf16[512,1024]{1,0:T(8,128)(2,1)}, u32[]{:S(2)}, u32[]{:S(2)}) collective-permute-start(bf16[512,1024]{1,0:T(8,128)(2,1)S(1)} %get-tuple-element.15.own_ref), channel_id=1, source_target_pairs={{4,8},{5,9},{6,10},{7,11},{8,4},{9,5},{10,6},{11,7},{12,16},{13,17... | collective-permute-start | bytes 3145736 | tf_op jit(solution)/shard_map/ppermute | solution.py:43
  10.3 18.1 %collective-permute-start.3 = (bf16[512,1024]{1,0:T(8,128)(2,1)S(1)}, bf16[512,1024]{1,0:T(8,128)(2,1)}, u32[]{:S(2)}, u32[]{:S(2)}) collective-permute-start(bf16[512,1024]{1,0:T(8,128)(2,1)S(1)} %get-tuple-element.15.own_ref), channel_id=1, source_target_pairs={{0,4},{1,5},{2,6},{3,7},{4,0},{5,1},{6,2},{7,3},{8,12},{9,13},{10,... | collective-permute-start | bytes 3145736 | tf_op jit(solution)/shard_map/ppermute | solution.py:43
  10.5 0.7 %copy-start.1 = (s32[128]{0:T(128)S(1)}, s32[128]{0:T(128)}, u32[]{:S(2)}) copy-start(s32[128]{0:T(128)} %param.3) | copy-start | bytes 1540
  30.8 7.3 %collective-permute-start.4 = (f32[1,512]{1,0:T(1,128)S(1)}, f32[1,512]{1,0:T(1,128)S(1)}, u32[]{:S(2)}, u32[]{:S(2)}) collective-permute-start(f32[1,512]{1,0:T(1,128)S(1)} %get-tuple-element.22), channel_id=1, source_target_pairs={{0,3},{1,2},{2,1},{3,4},{4,0},{5,6},{6,5},{7,8},{8,7},{9,10},{10,9... | collective-permute-start | bytes 6152 | tf_op jit(solution)/shard_map/ppermute | solution.py:43
  33.1 4.9 %collective-permute-start.5 = (f32[1,512]{1,0:T(1,128)S(1)}, f32[1,512]{1,0:T(1,128)S(1)}, u32[]{:S(2)}, u32[]{:S(2)}) collective-permute-start(f32[1,512]{1,0:T(1,128)S(1)} %get-tuple-element.23), channel_id=1, source_target_pairs={{0,1},{1,0},{2,3},{3,2},{4,5},{5,4},{6,7},{7,6},{8,9},{9,8},{10,11... | collective-permute-start | bytes 6152 | tf_op jit(solution)/shard_map/ppermute | solution.py:43
  33.1 4.9 %collective-permute-start.6 = (f32[1,512]{1,0:T(1,128)S(1)}, f32[1,512]{1,0:T(1,128)S(1)}, u32[]{:S(2)}, u32[]{:S(2)}) collective-permute-start(f32[1,512]{1,0:T(1,128)S(1)} %get-tuple-element.24), channel_id=1, source_target_pairs={{4,3},{251,252}} | collective-permute-start | bytes 6152 | tf_op jit(solution)/shard_map/ppermute | solution.py:43

commit v9 on v8

--- a/solution.py
+++ b/solution.py
@@ -9,7 +9,6 @@
 AXES = ("rows", "bal")
 LOWEST = -2.0
 STRIP = 64
-FETCHES = 4
 
 
 def pair_mate(i, n):
@@ -58,22 +57,6 @@
         unit_ref[rows, :] = (values * scale).astype(jnp.bfloat16)
 
 
-def fetch_units(raw_ref, stage_ref, sems, unit_ref):
-    rows = stage_ref.shape[0] // FETCHES
-    copies = [
-        pltpu.make_async_copy(
-            raw_ref.at[pl.ds(i * rows, rows)], stage_ref.at[pl.ds(i * rows, rows)], sems.at[i]
-        )
-        for i in range(FETCHES)
-    ]
-    for copy in copies:
-        copy.start()
-    for i, copy in enumerate(copies):
-        copy.wait()
-        part = pl.ds(i * rows, rows)
-        write_units(stage_ref.at[part], unit_ref.at[part])
-
-
 def products_of(left, right):
     return lax.dot_general(
         left, right, (((1,), (1,)), ((), ())), preferred_element_type=jnp.float32
@@ -92,8 +75,8 @@
     return jnp.max(folded.T, axis=0, keepdims=True)
 
 
-def own_kernel(raw_ref, unit_ref, high_ref, stage_ref, sems):
-    fetch_units(raw_ref, stage_ref, sems, unit_ref)
+def own_kernel(raw_ref, unit_ref, high_ref):
+    write_units(raw_ref, unit_ref)
     products = products_of(unit_ref[...], unit_ref[...])
     row = lax.broadcasted_iota(jnp.int32, products.shape, 0)
     col = lax.broadcasted_iota(jnp.int32, products.shape, 1)
@@ -129,29 +112,35 @@
     to_other_ref[...] = other_in_ref[...]
     to_mate_ref[...] = mate_in_ref[...]
     to_core_ref[...] = jnp.full_like(to_core_ref, LOWEST)
-    for i, (far_ref, slot) in enumerate(((core_ref, 3), (column_ref, 5))):
+    far = ((core_ref, 3), (column_ref, 5))
+
+    def fetch(i):
+        return pltpu.make_async_copy(far[i][0], stage_ref.at[i], sems.at[i])
+
+    for i, (_, slot) in enumerate(far):
 
         @pl.when(flags_ref[0, slot] + flags_ref[0, slot + 1] > 0)
         def _():
-            pltpu.make_async_copy(far_ref, stage_ref.at[i], sems.at[i]).start()
-
-    for i, (far_ref, slot) in enumerate(((core_ref, 3), (column_ref, 5))):
+            fetch(i).start()
+
+    for i, (_, slot) in enumerate(far):
 
         @pl.when(flags_ref[0, slot] + flags_ref[0, slot + 1] > 0)
         def _():
-            pltpu.make_async_copy(far_ref, stage_ref.at[i], sems.at[i]).wait()
-
-        for near_ref, line_ref, flag in (
-            (other_ref, to_other_ref, flags_ref[0, slot]),
-            (mate_ref, to_mate_ref, flags_ref[0, slot + 1]),
-        ):
-
-            @pl.when(flag == 1)
+            fetch(i).wait()
+
+            @pl.when(flags_ref[0, slot] == 1)
             def _():
-                products = products_of(stage_ref[i], near_ref[...])
-                line_ref[...] = jnp.maximum(line_ref[...], column_max(products))
-                if far_ref is core_ref and near_ref is other_ref:
+                products = products_of(stage_ref[i], other_ref[...])
+                to_other_ref[...] = jnp.maximum(to_other_ref[...], column_max(products))
+                if i == 0:
                     to_core_ref[...] = row_max(products)
+
+            @pl.when(flags_ref[0, slot + 1] == 1)
+            def _():
+                products = products_of(stage_ref[i], mate_ref[...])
+                to_mate_ref[...] = jnp.maximum(to_mate_ref[...], column_max(products))
+
     first_ref[...] = to_other_ref[...]
 
     @pl.when(flags_ref[0, 7] == 1)
@@ -224,8 +213,7 @@
     line = ((1, block), jnp.float32)
     tile = 2 * block * block * width
 
-    stage = [pltpu.VMEM(*units), pltpu.SemaphoreType.DMA((FETCHES,))]
-    own, high = call(own_kernel, (embeddings,), [units, line], stage, flops=tile, in_hbm=(0,))
+    own, high = call(own_kernel, (embeddings,), [units, line], flops=tile)
     column = swapped(own, column_neighbour)
     core = swapped(own, core_mate)
     mate, high = call(

time: 39.4 us -> 39 us (0.990)
  the two profiles are of different devices: /device:TPU:32 before, /device:TPU:1 now
where the time goes in v9:
time: 39 us; the launch traced here: 38.4 us
  starting transfers between devices  18.5 us (47%)
  waiting for transfers between devices  7.96 us (20%)
  Pallas kernels  5.14 us (13%)
  between operations  3.24 us (8%)
  local copies, waits for them, and re-layouts  2.11 us (5%)
  other arithmetic  1.49 us (4%)
    ppermute x7, starting transfers between devices, swapped(): return lax.ppermute(block, AXES, [p for p in pairs if p[1] is not None])  18.5 us
    ppermute x7, waiting for transfers between devices, swapped(): return lax.ppermute(block, AXES, [p for p in pairs if p[1] is not None])  7.96 us
    pallas_call x5, Pallas kernels, call(): pl.pallas_call(kernel, in_specs=specs, out_specs=[VMEM] * len(outs), out_...  5.14 us
    unnamed x4, local copies, waits for them, and re-layouts  1.91 us
  transfers between devices with their start and end apart: 7, of which 4 were waited for; matrix products, arithmetic and copies ran while one was open for 3% of the time, Pallas kernels for 7%

profile of v9, /device:TPU:1, one launch (start us, length us, event | category | flops | bytes accessed | tf_op | source)
XLA Modules:
  0.0 38.4 jit_solution(2697676898347205193)
XLA Ops:
  0.0 2.1 %collective-permute-start.1 = (bf16[512,1024]{1,0:T(8,128)(2,1)}, bf16[512,1024]{1,0:T(8,128)(2,1)S(1)}, u32[]{:S(2)}, u32[]{:S(2)}) collective-permute-start(bf16[512,1024]{1,0:T(8,128)(2,1)} %raw_ref.1), channel_id=1, source_target_pairs={{0,1},{1,0},{2,3},{3,2},{4,5},{5,4},{6,7},{7,6},{8,9},{9,8},{10,11... | collective-permute-start | bytes 3145736 | tf_op jit(solution)/shard_map/ppermute | solution.py:42
  2.1 2.7 %collective-permute-start = (bf16[512,1024]{1,0:T(8,128)(2,1)}, bf16[512,1024]{1,0:T(8,128)(2,1)S(1)}, u32[]{:S(2)}, u32[]{:S(2)}) collective-permute-start(bf16[512,1024]{1,0:T(8,128)(2,1)} %raw_ref.1), channel_id=1, source_target_pairs={{0,255},{1,2},{2,1},{3,4},{4,3},{5,6},{6,5},{7,8},{8,7},{9,10},{10... | collective-permute-start | bytes 3145736 | tf_op jit(solution)/shard_map/ppermute | solution.py:42
  4.9 1.3 %copy-done = bf16[512,1024]{1,0:T(8,128)(2,1)S(1)} copy-done((bf16[512,1024]{1,0:T(8,128)(2,1)S(1)}, bf16[512,1024]{1,0:T(8,128)(2,1)}, u32[]{:S(2)}) %copy-start) | copy-done | bytes 1048600
  6.1 1.0 %shard_map.28 = (bf16[512,1024]{1,0:T(8,128)(2,1)S(1)}, f32[1,512]{1,0:T(1,128)S(1)}) custom-call(bf16[512,1024]{1,0:T(8,128)(2,1)S(1)} %copy-done), custom_call_target="tpu_custom_call" | custom-call | flops 536870912 | bytes 1048576 | tf_op jit(solution)/shard_map/pallas_call | solution.py:169
  7.1 2.5 %collective-permute-start.2 = (bf16[512,1024]{1,0:T(8,128)(2,1)S(1)}, bf16[512,1024]{1,0:T(8,128)(2,1)}, u32[]{:S(2)}, u32[]{:S(2)}) collective-permute-start(bf16[512,1024]{1,0:T(8,128)(2,1)S(1)} %get-tuple-element.15.own_ref), channel_id=1, source_target_pairs={{4,8},{5,9},{6,10},{7,11},{8,4},{9,5},{10,6},{11,7},{12,16},{13,17... | collective-permute-start | bytes 3145736 | tf_op jit(solution)/shard_map/ppermute | solution.py:42
  9.7 6.2 %collective-permute-start.3 = (bf16[512,1024]{1,0:T(8,128)(2,1)S(1)}, bf16[512,1024]{1,0:T(8,128)(2,1)}, u32[]{:S(2)}, u32[]{:S(2)}) collective-permute-start(bf16[512,1024]{1,0:T(8,128)(2,1)S(1)} %get-tuple-element.15.own_ref), channel_id=1, source_target_pairs={{0,4},{1,5},{2,6},{3,7},{4,0},{5,1},{6,2},{7,3},{8,12},{9,13},{10,... | collective-permute-start | bytes 3145736 | tf_op jit(solution)/shard_map/ppermute | solution.py:42
  15.9 0.7 %copy-done.1 = s32[128]{0:T(128)S(1)} copy-done((s32[128]{0:T(128)S(1)}, s32[128]{0:T(128)}, u32[]{:S(2)}) %copy-start.1) | copy-done | bytes 536
  16.5 0.1 copy.5
  16.6 0.2 reduce-window.9
  16.8 0.7 %convert_reduce_fusion = (s32[]{:T(128)}, s32[]{:T(128)}, s32[]{:T(128)}, s32[]{:T(128)}, s32[]{:T(128)}) fusion(s32[128,1]{1,0:T(8,128)S(1)} %reduce-window.9, s32[]{:T(128)S(6)} %add.35, s32[]{:T(128)S(6)} %add.33, s32[]{:T(128)S(6)} %sub.18, s32[]{:T(128)S(6)} %add.31, s32[]{:T(128)S(6)} %sub.20), kind=kLoop, calls=%fused_computation | loop fusion | flops 2939 | bytes 552 | tf_op jit(solution)/shard_map/reduce_sum | solution.py:47
  20.7 0.1 stack.43
  20.8 3.3 %collective-permute-done.1.raw_ref = bf16[512,1024]{1,0:T(8,128)(2,1)S(1)} collective-permute-done((bf16[512,1024]{1,0:T(8,128)(2,1)}, bf16[512,1024]{1,0:T(8,128)(2,1)S(1)}, u32[]{:S(2)}, u32[]{:S(2)}) %collective-permute-start.1) | collective-permute-done | bytes 1048608 | tf_op jit(solution)/shard_map/ppermute | solution.py:42
  24.1 1.1 %shard_map.29 = (bf16[512,1024]{1,0:T(8,128)(2,1)S(1)}, f32[1,512]{1,0:T(1,128)S(1)}) custom-call(s32[1,8]{1,0:T(1,128)S(1)} %bitcast.11, bf16[512,1024]{1,0:T(8,128)(2,1)S(1)} %collective-permute-done.1.raw_ref, bf16[512,1024]{1,0:T(8,128)(2,1)S(1)} %get-tuple-element.15.own_ref, ...), custom_call_target="tpu_custom_call", output_to_operand_aliasing={{0}: (1, {})} | custom-call | flops 536870912 | bytes 2099232 | tf_op jit(solution)/shard_map/pallas_call | solution.py:169
  25.2 3.8 %collective-permute-done.raw_ref = bf16[512,1024]{1,0:T(8,128)(2,1)S(1)} collective-permute-done((bf16[512,1024]{1,0:T(8,128)(2,1)}, bf16[512,1024]{1,0:T(8,128)(2,1)S(1)}, u32[]{:S(2)}, u32[]{:S(2)}) %collective-permute-start) | collective-permute-done | bytes 1048608 | tf_op jit(solution)/shard_map/ppermute | solution.py:42
  29.0 0.3 shard_map.30
  29.4 0.2 collective-permute-done.2.column_ref
  29.6 2.6 %shard_map.32 = (f32[1,512]{1,0:T(1,128)S(1)}, f32[1,512]{1,0:T(1,128)S(1)}, f32[1,512]{1,0:T(1,128)S(1)}) custom-call(s32[1,8]{1,0:T(1,128)S(1)} %bitcast.13, bf16[512,1024]{1,0:T(8,128)(2,1)} %collective-permute-done.2.column_ref, bf16[512,1024]{1,0:T(8,128)(2,1)} %collective-permute-done.3.core_ref, bf16[512,1024]{1,0:T(8,128)(2,1)S(1)} %get-tuple-element.18.other_ref, ...), custom_call_target="tpu_custom_call" | custom-call | flops 536870912 | bytes 4198432 | tf_op jit(solution)/shard_map/pallas_call | solution.py:169
  32.2 0.1 collective-permute-start.4
  32.3 0.1 collective-permute-start.5
  32.4 4.7 %collective-permute-start.6 = (f32[1,512]{1,0:T(1,128)S(1)}, f32[1,512]{1,0:T(1,128)S(1)}, u32[]{:S(2)}, u32[]{:S(2)}) collective-permute-start(f32[1,512]{1,0:T(1,128)S(1)} %get-tuple-element.24), channel_id=1, source_target_pairs={{4,3},{251,252}} | collective-permute-start | bytes 6152 | tf_op jit(solution)/shard_map/ppermute | solution.py:42
  37.1 0.1 shard_map.31
  37.2 0.0 collective-permute-done.5
  37.3 0.6 %collective-permute-done.6 = f32[1,512]{1,0:T(1,128)S(1)} collective-permute-done((f32[1,512]{1,0:T(1,128)S(1)}, f32[1,512]{1,0:T(1,128)S(1)}, u32[]{:S(2)}, u32[]{:S(2)}) %collective-permute-start.6) | collective-permute-done | bytes 2080 | tf_op jit(solution)/shard_map/ppermute | solution.py:42
  37.8 0.6 %fusion.2 = f32[1,512]{1,0:T(1,128)} fusion(f32[1,512]{1,0:T(1,128)S(1)} %shard_map.31, f32[1,512]{1,0:T(1,128)S(1)} %collective-permute-done.5, f32[1,512]{1,0:T(1,128)S(1)} %collective-permute-done.4, pred[]{:T(512)S(6)} %or.7, f32[1,512]{1,0:T(1,128)S(1)} %collective-permute-done.6), kind=kLoop, calls=%fused_computation.11 | loop fusion | flops 2560 | bytes 10241 | tf_op jit(solution)/shard_map/max | solution.py:245
  (4 shorter events, 0.0 us)
Async XLA Ops:
  0.0 24.1 %collective-permute-start.1 = (bf16[512,1024]{1,0:T(8,128)(2,1)}, bf16[512,1024]{1,0:T(8,128)(2,1)S(1)}, u32[]{:S(2)}, u32[]{:S(2)}) collective-permute-start(bf16[512,1024]{1,0:T(8,128)(2,1)} %raw_ref.1), channel_id=1, source_target_pairs={{0,1},{1,0},{2,3},{3,2},{4,5},{5,4},{6,7},{7,6},{8,9},{9,8},{10,11... | collective-permute-start | bytes 3145736 | tf_op jit(solution)/shard_map/ppermute | solution.py:42
  2.1 26.9 %collective-permute-start = (bf16[512,1024]{1,0:T(8,128)(2,1)}, bf16[512,1024]{1,0:T(8,128)(2,1)S(1)}, u32[]{:S(2)}, u32[]{:S(2)}) collective-permute-start(bf16[512,1024]{1,0:T(8,128)(2,1)} %raw_ref.1), channel_id=1, source_target_pairs={{0,255},{1,2},{2,1},{3,4},{4,3},{5,6},{6,5},{7,8},{8,7},{9,10},{10... | collective-permute-start | bytes 3145736 | tf_op jit(solution)/shard_map/ppermute | solution.py:42
  4.9 1.3 %copy-start = (bf16[512,1024]{1,0:T(8,128)(2,1)S(1)}, bf16[512,1024]{1,0:T(8,128)(2,1)}, u32[]{:S(2)}) copy-start(bf16[512,1024]{1,0:T(8,128)(2,1)} %raw_ref.1) | copy-start | bytes 3145732
  7.1 22.4 %collective-permute-start.2 = (bf16[512,1024]{1,0:T(8,128)(2,1)S(1)}, bf16[512,1024]{1,0:T(8,128)(2,1)}, u32[]{:S(2)}, u32[]{:S(2)}) collective-permute-start(bf16[512,1024]{1,0:T(8,128)(2,1)S(1)} %get-tuple-element.15.own_ref), channel_id=1, source_target_pairs={{4,8},{5,9},{6,10},{7,11},{8,4},{9,5},{10,6},{11,7},{12,16},{13,17... | collective-permute-start | bytes 3145736 | tf_op jit(solution)/shard_map/ppermute | solution.py:42
  9.7 19.9 %collective-permute-start.3 = (bf16[512,1024]{1,0:T(8,128)(2,1)S(1)}, bf16[512,1024]{1,0:T(8,128)(2,1)}, u32[]{:S(2)}, u32[]{:S(2)}) collective-permute-start(bf16[512,1024]{1,0:T(8,128)(2,1)S(1)} %get-tuple-element.15.own_ref), channel_id=1, source_target_pairs={{0,4},{1,5},{2,6},{3,7},{4,0},{5,1},{6,2},{7,3},{8,12},{9,13},{10,... | collective-permute-start | bytes 3145736 | tf_op jit(solution)/shard_map/ppermute | solution.py:42
  15.9 0.7 %copy-start.1 = (s32[128]{0:T(128)S(1)}, s32[128]{0:T(128)}, u32[]{:S(2)}) copy-start(s32[128]{0:T(128)} %param.3) | copy-start | bytes 1540
  32.2 5.1 %collective-permute-start.4 = (f32[1,512]{1,0:T(1,128)S(1)}, f32[1,512]{1,0:T(1,128)S(1)}, u32[]{:S(2)}, u32[]{:S(2)}) collective-permute-start(f32[1,512]{1,0:T(1,128)S(1)} %get-tuple-element.22), channel_id=1, source_target_pairs={{0,3},{1,2},{2,1},{3,4},{4,0},{5,6},{6,5},{7,8},{8,7},{9,10},{10,9... | collective-permute-start | bytes 6152 | tf_op jit(solution)/shard_map/ppermute | solution.py:42
  32.3 5.0 %collective-permute-start.5 = (f32[1,512]{1,0:T(1,128)S(1)}, f32[1,512]{1,0:T(1,128)S(1)}, u32[]{:S(2)}, u32[]{:S(2)}) collective-permute-start(f32[1,512]{1,0:T(1,128)S(1)} %get-tuple-element.23), channel_id=1, source_target_pairs={{0,1},{1,0},{2,3},{3,2},{4,5},{5,4},{6,7},{7,6},{8,9},{9,8},{10,11... | collective-permute-start | bytes 6152 | tf_op jit(solution)/shard_map/ppermute | solution.py:42
  32.4 5.5 %collective-permute-start.6 = (f32[1,512]{1,0:T(1,128)S(1)}, f32[1,512]{1,0:T(1,128)S(1)}, u32[]{:S(2)}, u32[]{:S(2)}) collective-permute-start(f32[1,512]{1,0:T(1,128)S(1)} %get-tuple-element.24), channel_id=1, source_target_pairs={{4,3},{251,252}} | collective-permute-start | bytes 6152 | tf_op jit(solution)/shard_map/ppermute | solution.py:42

commit v10 on v9

--- a/solution.py
+++ b/solution.py
@@ -8,7 +8,7 @@
 EPSILON = 1e-06
 AXES = ("rows", "bal")
 LOWEST = -2.0
-STRIP = 64
+STRIP = 32
 
 
 def pair_mate(i, n):

time: 39 us -> 39 us (level)
  no operation moved by 1% of the time
where the time goes in v10:
time: 39 us; the launch traced here: 38.4 us
  starting transfers between devices  18.5 us (47%)
  waiting for transfers between devices  7.96 us (20%)
  Pallas kernels  5.14 us (13%)
  between operations  3.24 us (8%)
  local copies, waits for them, and re-layouts  2.11 us (5%)
  other arithmetic  1.49 us (4%)
    ppermute x7, starting transfers between devices, swapped(): return lax.ppermute(block, AXES, [p for p in pairs if p[1] is not None])  18.5 us
    ppermute x7, waiting for transfers between devices, swapped(): return lax.ppermute(block, AXES, [p for p in pairs if p[1] is not None])  7.96 us
    pallas_call x5, Pallas kernels, call(): pl.pallas_call(kernel, in_specs=specs, out_specs=[VMEM] * len(outs), out_...  5.14 us
    unnamed x4, local copies, waits for them, and re-layouts  1.91 us
  transfers between devices with their start and end apart: 7, of which 4 were waited for; matrix products, arithmetic and copies ran while one was open for 3% of the time, Pallas kernels for 7%

profile of v10, /device:TPU:1, one launch (start us, length us, event | category | flops | bytes accessed | tf_op | source)
XLA Modules:
  0.0 38.4 jit_solution(2697676898347205193)
XLA Ops:
  0.0 2.1 %collective-permute-start.1 = (bf16[512,1024]{1,0:T(8,128)(2,1)}, bf16[512,1024]{1,0:T(8,128)(2,1)S(1)}, u32[]{:S(2)}, u32[]{:S(2)}) collective-permute-start(bf16[512,1024]{1,0:T(8,128)(2,1)} %raw_ref.1), channel_id=1, source_target_pairs={{0,1},{1,0},{2,3},{3,2},{4,5},{5,4},{6,7},{7,6},{8,9},{9,8},{10,11... | collective-permute-start | bytes 3145736 | tf_op jit(solution)/shard_map/ppermute | solution.py:42
  2.1 2.7 %collective-permute-start = (bf16[512,1024]{1,0:T(8,128)(2,1)}, bf16[512,1024]{1,0:T(8,128)(2,1)S(1)}, u32[]{:S(2)}, u32[]{:S(2)}) collective-permute-start(bf16[512,1024]{1,0:T(8,128)(2,1)} %raw_ref.1), channel_id=1, source_target_pairs={{0,255},{1,2},{2,1},{3,4},{4,3},{5,6},{6,5},{7,8},{8,7},{9,10},{10... | collective-permute-start | bytes 3145736 | tf_op jit(solution)/shard_map/ppermute | solution.py:42
  4.9 1.3 %copy-done = bf16[512,1024]{1,0:T(8,128)(2,1)S(1)} copy-done((bf16[512,1024]{1,0:T(8,128)(2,1)S(1)}, bf16[512,1024]{1,0:T(8,128)(2,1)}, u32[]{:S(2)}) %copy-start) | copy-done | bytes 1048600
  6.1 1.0 %shard_map.28 = (bf16[512,1024]{1,0:T(8,128)(2,1)S(1)}, f32[1,512]{1,0:T(1,128)S(1)}) custom-call(bf16[512,1024]{1,0:T(8,128)(2,1)S(1)} %copy-done), custom_call_target="tpu_custom_call" | custom-call | flops 536870912 | bytes 1048576 | tf_op jit(solution)/shard_map/pallas_call | solution.py:169
  7.1 2.5 %collective-permute-start.2 = (bf16[512,1024]{1,0:T(8,128)(2,1)S(1)}, bf16[512,1024]{1,0:T(8,128)(2,1)}, u32[]{:S(2)}, u32[]{:S(2)}) collective-permute-start(bf16[512,1024]{1,0:T(8,128)(2,1)S(1)} %get-tuple-element.15.own_ref), channel_id=1, source_target_pairs={{4,8},{5,9},{6,10},{7,11},{8,4},{9,5},{10,6},{11,7},{12,16},{13,17... | collective-permute-start | bytes 3145736 | tf_op jit(solution)/shard_map/ppermute | solution.py:42
  9.7 6.2 %collective-permute-start.3 = (bf16[512,1024]{1,0:T(8,128)(2,1)S(1)}, bf16[512,1024]{1,0:T(8,128)(2,1)}, u32[]{:S(2)}, u32[]{:S(2)}) collective-permute-start(bf16[512,1024]{1,0:T(8,128)(2,1)S(1)} %get-tuple-element.15.own_ref), channel_id=1, source_target_pairs={{0,4},{1,5},{2,6},{3,7},{4,0},{5,1},{6,2},{7,3},{8,12},{9,13},{10,... | collective-permute-start | bytes 3145736 | tf_op jit(solution)/shard_map/ppermute | solution.py:42
  15.9 0.7 %copy-done.1 = s32[128]{0:T(128)S(1)} copy-done((s32[128]{0:T(128)S(1)}, s32[128]{0:T(128)}, u32[]{:S(2)}) %copy-start.1) | copy-done | bytes 536
  16.5 0.1 copy.5
  16.6 0.2 reduce-window.9
  16.8 0.7 %convert_reduce_fusion = (s32[]{:T(128)}, s32[]{:T(128)}, s32[]{:T(128)}, s32[]{:T(128)}, s32[]{:T(128)}) fusion(s32[128,1]{1,0:T(8,128)S(1)} %reduce-window.9, s32[]{:T(128)S(6)} %add.35, s32[]{:T(128)S(6)} %add.33, s32[]{:T(128)S(6)} %sub.18, s32[]{:T(128)S(6)} %add.31, s32[]{:T(128)S(6)} %sub.20), kind=kLoop, calls=%fused_computation | loop fusion | flops 2939 | bytes 552 | tf_op jit(solution)/shard_map/reduce_sum | solution.py:47
  20.7 0.1 stack.43
  20.8 3.3 %collective-permute-done.1.raw_ref = bf16[512,1024]{1,0:T(8,128)(2,1)S(1)} collective-permute-done((bf16[512,1024]{1,0:T(8,128)(2,1)}, bf16[512,1024]{1,0:T(8,128)(2,1)S(1)}, u32[]{:S(2)}, u32[]{:S(2)}) %collective-permute-start.1) | collective-permute-done | bytes 1048608 | tf_op jit(solution)/shard_map/ppermute | solution.py:42
  24.1 1.1 %shard_map.29 = (bf16[512,1024]{1,0:T(8,128)(2,1)S(1)}, f32[1,512]{1,0:T(1,128)S(1)}) custom-call(s32[1,8]{1,0:T(1,128)S(1)} %bitcast.11, bf16[512,1024]{1,0:T(8,128)(2,1)S(1)} %collective-permute-done.1.raw_ref, bf16[512,1024]{1,0:T(8,128)(2,1)S(1)} %get-tuple-element.15.own_ref, ...), custom_call_target="tpu_custom_call", output_to_operand_aliasing={{0}: (1, {})} | custom-call | flops 536870912 | bytes 2099232 | tf_op jit(solution)/shard_map/pallas_call | solution.py:169
  25.2 3.8 %collective-permute-done.raw_ref = bf16[512,1024]{1,0:T(8,128)(2,1)S(1)} collective-permute-done((bf16[512,1024]{1,0:T(8,128)(2,1)}, bf16[512,1024]{1,0:T(8,128)(2,1)S(1)}, u32[]{:S(2)}, u32[]{:S(2)}) %collective-permute-start) | collective-permute-done | bytes 1048608 | tf_op jit(solution)/shard_map/ppermute | solution.py:42
  29.0 0.3 shard_map.30
  29.4 0.2 collective-permute-done.2.column_ref
  29.6 2.6 %shard_map.32 = (f32[1,512]{1,0:T(1,128)S(1)}, f32[1,512]{1,0:T(1,128)S(1)}, f32[1,512]{1,0:T(1,128)S(1)}) custom-call(s32[1,8]{1,0:T(1,128)S(1)} %bitcast.13, bf16[512,1024]{1,0:T(8,128)(2,1)} %collective-permute-done.2.column_ref, bf16[512,1024]{1,0:T(8,128)(2,1)} %collective-permute-done.3.core_ref, bf16[512,1024]{1,0:T(8,128)(2,1)S(1)} %get-tuple-element.18.other_ref, ...), custom_call_target="tpu_custom_call" | custom-call | flops 536870912 | bytes 4198432 | tf_op jit(solution)/shard_map/pallas_call | solution.py:169
  32.2 0.1 collective-permute-start.4
  32.3 0.1 collective-permute-start.5
  32.4 4.7 %collective-permute-start.6 = (f32[1,512]{1,0:T(1,128)S(1)}, f32[1,512]{1,0:T(1,128)S(1)}, u32[]{:S(2)}, u32[]{:S(2)}) collective-permute-start(f32[1,512]{1,0:T(1,128)S(1)} %get-tuple-element.24), channel_id=1, source_target_pairs={{4,3},{251,252}} | collective-permute-start | bytes 6152 | tf_op jit(solution)/shard_map/ppermute | solution.py:42
  37.1 0.1 shard_map.31
  37.2 0.0 collective-permute-done.5
  37.3 0.6 %collective-permute-done.6 = f32[1,512]{1,0:T(1,128)S(1)} collective-permute-done((f32[1,512]{1,0:T(1,128)S(1)}, f32[1,512]{1,0:T(1,128)S(1)}, u32[]{:S(2)}, u32[]{:S(2)}) %collective-permute-start.6) | collective-permute-done | bytes 2080 | tf_op jit(solution)/shard_map/ppermute | solution.py:42
  37.8 0.6 %fusion.2 = f32[1,512]{1,0:T(1,128)} fusion(f32[1,512]{1,0:T(1,128)S(1)} %shard_map.31, f32[1,512]{1,0:T(1,128)S(1)} %collective-permute-done.5, f32[1,512]{1,0:T(1,128)S(1)} %collective-permute-done.4, pred[]{:T(512)S(6)} %or.7, f32[1,512]{1,0:T(1,128)S(1)} %collective-permute-done.6), kind=kLoop, calls=%fused_computation.11 | loop fusion | flops 2560 | bytes 10241 | tf_op jit(solution)/shard_map/max | solution.py:245
  (4 shorter events, 0.0 us)
Async XLA Ops:
  0.0 24.1 %collective-permute-start.1 = (bf16[512,1024]{1,0:T(8,128)(2,1)}, bf16[512,1024]{1,0:T(8,128)(2,1)S(1)}, u32[]{:S(2)}, u32[]{:S(2)}) collective-permute-start(bf16[512,1024]{1,0:T(8,128)(2,1)} %raw_ref.1), channel_id=1, source_target_pairs={{0,1},{1,0},{2,3},{3,2},{4,5},{5,4},{6,7},{7,6},{8,9},{9,8},{10,11... | collective-permute-start | bytes 3145736 | tf_op jit(solution)/shard_map/ppermute | solution.py:42
  2.1 26.9 %collective-permute-start = (bf16[512,1024]{1,0:T(8,128)(2,1)}, bf16[512,1024]{1,0:T(8,128)(2,1)S(1)}, u32[]{:S(2)}, u32[]{:S(2)}) collective-permute-start(bf16[512,1024]{1,0:T(8,128)(2,1)} %raw_ref.1), channel_id=1, source_target_pairs={{0,255},{1,2},{2,1},{3,4},{4,3},{5,6},{6,5},{7,8},{8,7},{9,10},{10... | collective-permute-start | bytes 3145736 | tf_op jit(solution)/shard_map/ppermute | solution.py:42
  4.9 1.3 %copy-start = (bf16[512,1024]{1,0:T(8,128)(2,1)S(1)}, bf16[512,1024]{1,0:T(8,128)(2,1)}, u32[]{:S(2)}) copy-start(bf16[512,1024]{1,0:T(8,128)(2,1)} %raw_ref.1) | copy-start | bytes 3145732
  7.1 22.4 %collective-permute-start.2 = (bf16[512,1024]{1,0:T(8,128)(2,1)S(1)}, bf16[512,1024]{1,0:T(8,128)(2,1)}, u32[]{:S(2)}, u32[]{:S(2)}) collective-permute-start(bf16[512,1024]{1,0:T(8,128)(2,1)S(1)} %get-tuple-element.15.own_ref), channel_id=1, source_target_pairs={{4,8},{5,9},{6,10},{7,11},{8,4},{9,5},{10,6},{11,7},{12,16},{13,17... | collective-permute-start | bytes 3145736 | tf_op jit(solution)/shard_map/ppermute | solution.py:42
  9.7 19.9 %collective-permute-start.3 = (bf16[512,1024]{1,0:T(8,128)(2,1)S(1)}, bf16[512,1024]{1,0:T(8,128)(2,1)}, u32[]{:S(2)}, u32[]{:S(2)}) collective-permute-start(bf16[512,1024]{1,0:T(8,128)(2,1)S(1)} %get-tuple-element.15.own_ref), channel_id=1, source_target_pairs={{0,4},{1,5},{2,6},{3,7},{4,0},{5,1},{6,2},{7,3},{8,12},{9,13},{10,... | collective-permute-start | bytes 3145736 | tf_op jit(solution)/shard_map/ppermute | solution.py:42
  15.9 0.7 %copy-start.1 = (s32[128]{0:T(128)S(1)}, s32[128]{0:T(128)}, u32[]{:S(2)}) copy-start(s32[128]{0:T(128)} %param.3) | copy-start | bytes 1540
  32.2 5.1 %collective-permute-start.4 = (f32[1,512]{1,0:T(1,128)S(1)}, f32[1,512]{1,0:T(1,128)S(1)}, u32[]{:S(2)}, u32[]{:S(2)}) collective-permute-start(f32[1,512]{1,0:T(1,128)S(1)} %get-tuple-element.22), channel_id=1, source_target_pairs={{0,3},{1,2},{2,1},{3,4},{4,0},{5,6},{6,5},{7,8},{8,7},{9,10},{10,9... | collective-permute-start | bytes 6152 | tf_op jit(solution)/shard_map/ppermute | solution.py:42
  32.3 5.0 %collective-permute-start.5 = (f32[1,512]{1,0:T(1,128)S(1)}, f32[1,512]{1,0:T(1,128)S(1)}, u32[]{:S(2)}, u32[]{:S(2)}) collective-permute-start(f32[1,512]{1,0:T(1,128)S(1)} %get-tuple-element.23), channel_id=1, source_target_pairs={{0,1},{1,0},{2,3},{3,2},{4,5},{5,4},{6,7},{7,6},{8,9},{9,8},{10,11... | collective-permute-start | bytes 6152 | tf_op jit(solution)/shard_map/ppermute | solution.py:42
  32.4 5.5 %collective-permute-start.6 = (f32[1,512]{1,0:T(1,128)S(1)}, f32[1,512]{1,0:T(1,128)S(1)}, u32[]{:S(2)}, u32[]{:S(2)}) collective-permute-start(f32[1,512]{1,0:T(1,128)S(1)} %get-tuple-element.24), channel_id=1, source_target_pairs={{4,3},{251,252}} | collective-permute-start | bytes 6152 | tf_op jit(solution)/shard_map/ppermute | solution.py:42
